TPU v7x, 32 devices: a whole 2x2x4 slice. The times are simulated.
32 devices in a mesh: ctx: 16 (over z, y, x), fsdp: 2 (over core).
Axes of the slice: x: 2, y: 2, z: 4, core: 2. Of those that a mesh axis runs over, the one named last changes fastest.
Arguments:
- tokens: bfloat16 [2, 2048, 2304], P('fsdp', 'ctx'), may hold values from -6 to 6
- cotangent: bfloat16 [2, 2048, 2304], P('fsdp', 'ctx'), may hold values from -6 to 6
- pair_table: int32 [16], replicated, may hold values from 0 to 15, each once
- query_weight: bfloat16 [2304, 2048], P(None, ('ctx', 'fsdp')), may hold values from -0.20833333 to 0.20833333
- key_weight: bfloat16 [2304, 1024], P(None, ('ctx', 'fsdp')), may hold values from -0.20833333 to 0.20833333
- value_weight: bfloat16 [2304, 1024], P(None, ('ctx', 'fsdp')), may hold values from -0.125 to 0.125
- output_weight: bfloat16 [2048, 2304], P(('ctx', 'fsdp')), may hold values from -0.125 to 0.125
- gate_weight: bfloat16 [2304, 9216], P(None, ('ctx', 'fsdp')), may hold values from -0.125 to 0.125
- up_weight: bfloat16 [2304, 9216], P(None, ('ctx', 'fsdp')), may hold values from -0.125 to 0.125
- down_weight: bfloat16 [9216, 2304], P(('ctx', 'fsdp')), may hold values from -0.0625 to 0.0625
- norm_scales: bfloat16 [4, 2304], replicated, may hold values from 0.099609375 to 1.8984375
Outputs:
- output: bfloat16 [2, 2048, 2304], P('fsdp', 'ctx')
- input_grad: bfloat16 [2, 2048, 2304], P('fsdp', 'ctx')
- query_weight_grad: float32 [2304, 2048], P(None, ('ctx', 'fsdp'))
- key_weight_grad: float32 [2304, 1024], P(None, ('ctx', 'fsdp'))
- value_weight_grad: float32 [2304, 1024], P(None, ('ctx', 'fsdp'))
- output_weight_grad: float32 [2048, 2304], P(('ctx', 'fsdp'))
- gate_weight_grad: float32 [2304, 9216], P(None, ('ctx', 'fsdp'))
- up_weight_grad: float32 [2304, 9216], P(None, ('ctx', 'fsdp'))
- down_weight_grad: float32 [9216, 2304], P(('ctx', 'fsdp'))
- scale_grad: float32 [4, 2304], P(None, ('ctx', 'fsdp'))
Inputs may be any that keep to these rules, and one draw needn't show every extreme that they name: Each index of ctx holds position blocks pair_table[index] and 31 - pair_table[index]; every value appears once.
All inputs are finite; a program needn't handle non-finite values.
Results may differ from a plain program's by a relative error of at most 0.019.
The roundings to bfloat16 on the way count: a program that leaves them out, or rounds other values in their place, can miss the bound.
Values may be sent and summed in bfloat16 or wider, within the bound.
No kernel may reach another device: no remote copies, remote signals or barrier semaphores. Data moves between devices by JAX's collectives and lax.ppermute only.
A program may use at most 640 MiB of HBM per device.

v0:
```python
import jax
import jax.numpy as jnp
from jax import lax
from jax.sharding import PartitionSpec as P

HEADS = 8
KV_HEADS = 4
HEAD = 256


EPSILON = 1e-06
SOFT_CAP = 50.0
QUERY_SCALE = 0.0625
HUGE_VALUE = 1e30


def contract(left, right, left_dim, right_dim):
    return lax.dot_general(
        left, right, (((left_dim,), (right_dim,)), ((), ())), preferred_element_type=jnp.float32
    )


def inverse_root(matrix_in):
    return lax.rsqrt(jnp.mean(matrix_in * matrix_in, axis=-1, keepdims=True) + EPSILON)


def norm_back(matrix_in, inverse, scale_row, upstream):
    weighted = upstream * scale_row
    inner = jnp.mean(matrix_in * weighted, axis=-1, keepdims=True)
    back = inverse * weighted - matrix_in * (inverse * inverse * inverse) * inner
    return (back, jnp.sum(upstream * matrix_in * inverse, axis=0))


def paired_term(left_rows, gate_cols, up_cols, shard_width, amount):
    gate_part = contract(gate_cols, left_rows, 0, 0)
    up_part = contract(up_cols, left_rows, 0, 0)
    groups = amount // (2 * shard_width)
    stacked = jnp.stack(
        [gate_part.reshape(groups, shard_width, -1), up_part.reshape(groups, shard_width, -1)],
        axis=1,
    )
    return stacked.reshape(amount, -1)


def rope_tables(positions):
    half_size = HEAD // 2
    frequency = 10000.0 ** (-jnp.arange(half_size, dtype=jnp.float32) * 2.0 / HEAD)
    angles = positions.astype(jnp.float32)[:, None] * frequency[None, :]
    return (jnp.cos(angles)[:, None, :], jnp.sin(angles)[:, None, :])


def rotate(matrix_in, cosine, sine_table, head_count, direction):
    row_count = matrix_in.shape[0]
    half_size = HEAD // 2
    shaped = matrix_in.reshape(row_count, head_count, HEAD)
    first_half = shaped[..., :half_size]
    second_half = shaped[..., half_size:]
    turned = jnp.concatenate(
        [
            first_half * cosine - direction * second_half * sine_table,
            second_half * cosine + direction * first_half * sine_table,
        ],
        axis=-1,
    )
    return turned.reshape(row_count, head_count * HEAD)


def score_block(queries, key_rows, offset, key_block, places):
    keys_part = lax.dynamic_slice_in_dim(key_rows, offset, key_block, 0).reshape(
        key_block, KV_HEADS, HEAD
    )
    raw_scores = jnp.einsum(
        "bgjd,kgd->gjbk", queries, keys_part, preferred_element_type=jnp.float32
    )
    capped = SOFT_CAP * jnp.tanh(raw_scores / SOFT_CAP)
    key_places = offset + jnp.arange(key_block, dtype=jnp.int32)
    allowed = key_places[None, :] <= places[:, None]
    return (capped, allowed, keys_part)


def log_norm(queries, key_rows, places, key_block):
    shape_rows = (KV_HEADS, HEADS // KV_HEADS, queries.shape[0])

    def advance(block_index, state_now):
        running_max, running_sum = state_now
        capped, allowed, keys_part = score_block(
            queries, key_rows, block_index * key_block, key_block, places
        )
        capped = jnp.where(allowed[None, None], capped, -HUGE_VALUE)
        new_max = jnp.maximum(running_max, jnp.max(capped, axis=-1))
        running_sum = running_sum * jnp.exp(running_max - new_max) + jnp.sum(
            jnp.exp(capped - new_max[..., None]), axis=-1
        )
        return (new_max, running_sum)

    block_total = places[-1] // key_block + 1
    start_state = (
        jnp.full(shape_rows, -HUGE_VALUE, jnp.float32),
        jnp.zeros(shape_rows, jnp.float32),
    )
    running_max, running_sum = lax.fori_loop(0, block_total, advance, start_state)
    return running_max + jnp.log(running_sum)


def attend_forward(queries, key_rows, value_rows, places, key_block, log_total):

    def advance(block_index, output_sum):
        offset = block_index * key_block
        capped, allowed, keys_part = score_block(queries, key_rows, offset, key_block, places)
        weights_soft = jnp.where(
            allowed[None, None], jnp.exp(capped - log_total[..., None]), 0.0
        ).astype(jnp.bfloat16)
        values_part = lax.dynamic_slice_in_dim(value_rows, offset, key_block, 0).reshape(
            key_block, KV_HEADS, HEAD
        )
        return output_sum + jnp.einsum(
            "gjbk,kgd->bgjd", weights_soft, values_part, preferred_element_type=jnp.float32
        )

    block_total = places[-1] // key_block + 1
    return lax.fori_loop(0, block_total, advance, jnp.zeros(queries.shape, jnp.float32))


def attend_backward(
    queries,
    key_rows,
    value_rows,
    places,
    key_block,
    log_total,
    grad_low,
    row_inner,
    key_grads,
    value_grads,
):

    def advance(block_index, state_now):
        query_grad, key_sums, value_sums = state_now
        offset = block_index * key_block
        capped, allowed, keys_part = score_block(queries, key_rows, offset, key_block, places)
        weights_soft = jnp.where(allowed[None, None], jnp.exp(capped - log_total[..., None]), 0.0)
        values_part = lax.dynamic_slice_in_dim(value_rows, offset, key_block, 0).reshape(
            key_block, KV_HEADS, HEAD
        )
        weight_grad = jnp.einsum(
            "bgjd,kgd->gjbk", grad_low, values_part, preferred_element_type=jnp.float32
        )
        score_grad = (
            weights_soft * (weight_grad - row_inner[..., None]) * (1.0 - (capped / SOFT_CAP) ** 2)
        ).astype(jnp.bfloat16)
        query_grad = query_grad + jnp.einsum(
            "gjbk,kgd->bgjd", score_grad, keys_part, preferred_element_type=jnp.float32
        )
        key_part_grad = jnp.einsum(
            "gjbk,bgjd->kgd", score_grad, queries, preferred_element_type=jnp.float32
        ).reshape(key_block, -1)
        value_part_grad = jnp.einsum(
            "gjbk,bgjd->kgd",
            weights_soft.astype(jnp.bfloat16),
            grad_low,
            preferred_element_type=jnp.float32,
        ).reshape(key_block, -1)
        key_sums = lax.dynamic_update_slice_in_dim(
            key_sums,
            lax.dynamic_slice_in_dim(key_sums, offset, key_block, 0) + key_part_grad,
            offset,
            0,
        )
        value_sums = lax.dynamic_update_slice_in_dim(
            value_sums,
            lax.dynamic_slice_in_dim(value_sums, offset, key_block, 0) + value_part_grad,
            offset,
            0,
        )
        return (query_grad, key_sums, value_sums)

    block_total = places[-1] // key_block + 1
    start_state = (jnp.zeros(queries.shape, jnp.float32), key_grads, value_grads)
    return lax.fori_loop(0, block_total, advance, start_state)


def shards(
    tokens,
    cotangent,
    pair_table,
    query_weight,
    key_weight,
    value_weight,
    output_weight,
    gate_weight,
    up_weight,
    down_weight,
    norm_scales,
):
    inputs = tokens[0].astype(jnp.float32)
    row_count = inputs.shape[0]
    half_rows = row_count // 2
    group_size = HEADS // KV_HEADS
    query_local = query_weight.shape[1]
    key_local = key_weight.shape[1]
    ff_local = gate_weight.shape[1]
    devices = lax.axis_size("ctx")
    fsdp_count = lax.axis_size("fsdp")
    all_count = devices * fsdp_count
    query_width = query_local * all_count
    key_width = key_local * all_count
    own_pair = pair_table[lax.axis_index("ctx")]
    offsets = jnp.arange(row_count, dtype=jnp.int32)
    positions = jnp.where(
        offsets < half_rows,
        own_pair * half_rows + offsets,
        (2 * devices - 1 - own_pair) * half_rows + offsets - half_rows,
    )
    cosine, sine_table = rope_tables(positions)
    scales = norm_scales.astype(jnp.float32)
    inverse_one = inverse_root(inputs)
    normed_first = (inputs * inverse_one * scales[0]).astype(jnp.bfloat16)
    pieces = (
        lax.all_gather(query_weight, ("ctx", "fsdp"), axis=1, tiled=True),
        lax.all_gather(key_weight, ("ctx", "fsdp"), axis=1, tiled=True),
        lax.all_gather(value_weight, ("ctx", "fsdp"), axis=1, tiled=True),
    )
    query_raw = jnp.dot(normed_first, pieces[0], preferred_element_type=jnp.float32)
    key_raw = jnp.dot(normed_first, pieces[1], preferred_element_type=jnp.float32)
    value_raw = jnp.dot(normed_first, pieces[2], preferred_element_type=jnp.float32)
    queries = (rotate(query_raw, cosine, sine_table, HEADS, 1.0) * QUERY_SCALE).astype(jnp.bfloat16)
    key_rows = rotate(key_raw, cosine, sine_table, KV_HEADS, 1.0).astype(jnp.bfloat16)
    value_rows = value_raw.astype(jnp.bfloat16)
    gathered_keys, gathered_values = (
        lax.all_gather(key_rows, "ctx", axis=0, tiled=True),
        lax.all_gather(value_rows, "ctx", axis=0, tiled=True),
    )
    pair_ids = jnp.arange(devices, dtype=jnp.int32)
    owner = jnp.sum(
        jnp.where(pair_table[None, :] == pair_ids[:, None], pair_ids[None, :], 0), axis=1
    )
    block_ids = jnp.arange(2 * devices, dtype=jnp.int32)
    source_device = owner[jnp.minimum(block_ids, 2 * devices - 1 - block_ids)]
    source_side = (block_ids >= devices).astype(jnp.int32)
    ordered_keys = gathered_keys.reshape(devices, 2, half_rows, key_width)[
        source_device, source_side
    ].reshape(-1, key_width)
    ordered_values = gathered_values.reshape(devices, 2, half_rows, key_width)[
        source_device, source_side
    ].reshape(-1, key_width)
    seq_length = ordered_keys.shape[0]
    key_block = min(512, seq_length)
    head_shape = (half_rows, KV_HEADS, group_size, HEAD)
    attn_parts = []
    norm_parts = []
    for side_index in range(2):
        query_part = queries[side_index * half_rows : (side_index + 1) * half_rows].reshape(
            head_shape
        )
        place_part = positions[side_index * half_rows : (side_index + 1) * half_rows]
        log_total = log_norm(query_part, ordered_keys, place_part, key_block)
        attn_parts.append(
            attend_forward(
                query_part, ordered_keys, ordered_values, place_part, key_block, log_total
            ).reshape(half_rows, query_width)
        )
        norm_parts.append(log_total)
    attn_full = jnp.concatenate(attn_parts, axis=0)
    attn_low = attn_full.astype(jnp.bfloat16)
    branch_out = jnp.dot(
        attn_low,
        lax.all_gather(output_weight, ("ctx", "fsdp"), axis=0, tiled=True),
        preferred_element_type=jnp.float32,
    )
    inverse_two = inverse_root(branch_out)
    hidden = inputs + branch_out * inverse_two * scales[1]
    inverse_three = inverse_root(hidden)
    normed_second = (hidden * inverse_three * scales[2]).astype(jnp.bfloat16)
    pieces = (
        lax.all_gather(gate_weight, ("ctx", "fsdp"), axis=1, tiled=True),
        lax.all_gather(up_weight, ("ctx", "fsdp"), axis=1, tiled=True),
    )
    gate_out = jnp.dot(normed_second, pieces[0], preferred_element_type=jnp.float32)
    up_out = jnp.dot(normed_second, pieces[1], preferred_element_type=jnp.float32)
    mixed = (jax.nn.gelu(gate_out, approximate=True) * up_out).astype(jnp.bfloat16)
    ffn_out = jnp.dot(
        mixed,
        lax.all_gather(down_weight, ("ctx", "fsdp"), axis=0, tiled=True),
        preferred_element_type=jnp.float32,
    )
    inverse_four = inverse_root(ffn_out)
    result = hidden + ffn_out * inverse_four * scales[3]
    upstream = cotangent[0].astype(jnp.float32)
    ffn_grad, scale_four = norm_back(ffn_out, inverse_four, scales[3], upstream)
    ffn_grad_low = ffn_grad.astype(jnp.bfloat16)
    mixed_grad = contract(
        ffn_grad_low, lax.all_gather(down_weight, ("ctx", "fsdp"), axis=0, tiled=True), 1, 1
    )
    _, gelu_pull = jax.vjp(
        lambda gate_in, up_in: jax.nn.gelu(gate_in, approximate=True) * up_in, gate_out, up_out
    )
    gate_grad, up_grad = gelu_pull(mixed_grad)
    gate_grad_low = gate_grad.astype(jnp.bfloat16)
    up_grad_low = up_grad.astype(jnp.bfloat16)
    pieces = (
        lax.all_gather(gate_weight, ("ctx", "fsdp"), axis=1, tiled=True),
        lax.all_gather(up_weight, ("ctx", "fsdp"), axis=1, tiled=True),
    )
    second_grad = contract(gate_grad_low, pieces[0], 1, 1) + contract(up_grad_low, pieces[1], 1, 1)
    down_grad_share = lax.psum_scatter(
        contract(mixed, ffn_grad_low, 0, 0), ("ctx", "fsdp"), scatter_dimension=0, tiled=True
    )
    ffn_share = lax.psum_scatter(
        paired_term(
            normed_second,
            gate_grad_low,
            up_grad_low,
            ff_local,
            2 * ff_local * lax.axis_size(("ctx", "fsdp")),
        ),
        ("ctx", "fsdp"),
        scatter_dimension=0,
        tiled=True,
    )
    hidden_part, scale_three = norm_back(hidden, inverse_three, scales[2], second_grad)
    hidden_grad = upstream + hidden_part
    branch_grad, scale_two = norm_back(branch_out, inverse_two, scales[1], hidden_grad)
    branch_grad_low = branch_grad.astype(jnp.bfloat16)
    attn_grad = contract(
        branch_grad_low, lax.all_gather(output_weight, ("ctx", "fsdp"), axis=0, tiled=True), 1, 1
    )
    output_weight_grad = contract(attn_low, branch_grad_low, 0, 0)
    attn_grad_low = attn_grad.astype(jnp.bfloat16)
    key_grads = jnp.zeros((seq_length, key_width), jnp.float32)
    value_grads = jnp.zeros((seq_length, key_width), jnp.float32)
    query_parts = []
    for side_index in range(2):
        lower_row = side_index * half_rows
        query_part = queries[lower_row : lower_row + half_rows].reshape(head_shape)
        place_part = positions[lower_row : lower_row + half_rows]
        grad_part = attn_grad_low[lower_row : lower_row + half_rows].reshape(head_shape)
        row_inner = jnp.einsum(
            "bgjd,bgjd->gjb",
            grad_part.astype(jnp.float32),
            attn_full[lower_row : lower_row + half_rows].reshape(head_shape),
        )
        part_grad, key_grads, value_grads = attend_backward(
            query_part,
            ordered_keys,
            ordered_values,
            place_part,
            key_block,
            norm_parts[side_index],
            grad_part,
            row_inner,
            key_grads,
            value_grads,
        )
        query_parts.append(part_grad.reshape(half_rows, query_width))
    query_grad = jnp.concatenate(query_parts, axis=0)
    target_blocks = jnp.stack([pair_table, 2 * devices - 1 - pair_table], axis=1)
    device_keys = key_grads.reshape(2 * devices, half_rows, key_width)[target_blocks].reshape(
        -1, key_width
    )
    device_values = value_grads.reshape(2 * devices, half_rows, key_width)[target_blocks].reshape(
        -1, key_width
    )
    own_key_grad, own_value_grad = (
        lax.psum_scatter(device_keys, "ctx", scatter_dimension=0, tiled=True),
        lax.psum_scatter(device_values, "ctx", scatter_dimension=0, tiled=True),
    )
    query_raw_low = (rotate(query_grad, cosine, sine_table, HEADS, -1.0) * QUERY_SCALE).astype(
        jnp.bfloat16
    )
    key_raw_low = rotate(own_key_grad, cosine, sine_table, KV_HEADS, -1.0).astype(jnp.bfloat16)
    value_raw_low = own_value_grad.astype(jnp.bfloat16)
    pieces = (
        lax.all_gather(query_weight, ("ctx", "fsdp"), axis=1, tiled=True),
        lax.all_gather(key_weight, ("ctx", "fsdp"), axis=1, tiled=True),
        lax.all_gather(value_weight, ("ctx", "fsdp"), axis=1, tiled=True),
    )
    first_grad = (
        contract(query_raw_low, pieces[0], 1, 1)
        + contract(key_raw_low, pieces[1], 1, 1)
        + contract(value_raw_low, pieces[2], 1, 1)
    )
    query_weight_grad = contract(normed_first, query_raw_low, 0, 0)
    key_weight_grad = contract(normed_first, key_raw_low, 0, 0)
    value_weight_grad = contract(normed_first, value_raw_low, 0, 0)
    input_part, scale_one = norm_back(inputs, inverse_one, scales[0], first_grad)
    input_grad = hidden_grad + input_part
    scale_grads = jnp.stack([scale_one, scale_two, scale_three, scale_four], axis=0)
    query_share, key_share, value_share, output_share, scale_share = (
        lax.psum_scatter(query_weight_grad, ("ctx", "fsdp"), scatter_dimension=1, tiled=True),
        lax.psum_scatter(key_weight_grad, ("ctx", "fsdp"), scatter_dimension=1, tiled=True),
        lax.psum_scatter(value_weight_grad, ("ctx", "fsdp"), scatter_dimension=1, tiled=True),
        lax.psum_scatter(output_weight_grad, ("ctx", "fsdp"), scatter_dimension=0, tiled=True),
        lax.psum_scatter(scale_grads, ("ctx", "fsdp"), scatter_dimension=1, tiled=True),
    )
    gate_share = ffn_share[:ff_local].T
    up_share = ffn_share[ff_local:].T
    return (
        result.astype(jnp.bfloat16)[None],
        input_grad.astype(jnp.bfloat16)[None],
        query_share,
        key_share,
        value_share,
        output_share,
        gate_share,
        up_share,
        down_grad_share,
        scale_share,
    )


def solution(mesh):
    return jax.shard_map(
        shards,
        mesh=mesh,
        in_specs=(
            P("fsdp", "ctx", None),
            P("fsdp", "ctx", None),
            P(),
            P(None, ("ctx", "fsdp")),
            P(None, ("ctx", "fsdp")),
            P(None, ("ctx", "fsdp")),
            P(("ctx", "fsdp"), None),
            P(None, ("ctx", "fsdp")),
            P(None, ("ctx", "fsdp")),
            P(("ctx", "fsdp"), None),
            P(),
        ),
        out_specs=(
            P("fsdp", "ctx", None),
            P("fsdp", "ctx", None),
            P(None, ("ctx", "fsdp")),
            P(None, ("ctx", "fsdp")),
            P(None, ("ctx", "fsdp")),
            P(("ctx", "fsdp"), None),
            P(None, ("ctx", "fsdp")),
            P(None, ("ctx", "fsdp")),
            P(("ctx", "fsdp"), None),
            P(None, ("ctx", "fsdp")),
        ),
        check_vma=False,
    )
```

profile of v0, /device:TPU:0, one launch (start us, length us, event | category | flops | bytes accessed | tf_op | source)
XLA Modules:
  0.0 4565.4 jit_solution(3715221287507149533)
XLA Ops:
  11.3 65.9 %all-gather.10.cloned.1.call-done = bf16[2304,1024]{0,1:T(8,128)(2,1)} async-done(((bf16[2304,32]{0,1:T(8,128)(2,1)}), bf16[2304,1024]{0,1:T(8,128)(2,1)}) %all-gather.10.cloned.1.call-update) | async-done | bytes 4718608 | tf_op jit(solution)/shard_map/all_gather | solution.py:221
  85.2 57.5 %all-gather.14.cloned.1.call-done = bf16[2304,1024]{0,1:T(8,128)(2,1)} async-done(((bf16[2304,32]{0,1:T(8,128)(2,1)}), bf16[2304,1024]{0,1:T(8,128)(2,1)}) %all-gather.14.cloned.1.call-update) | async-done | bytes 4718608 | tf_op jit(solution)/shard_map/all_gather | solution.py:220
  158.6 62.3 %all-gather.12.cloned.1.call-done = bf16[2048,1024]{1,0:T(8,128)(2,1)} async-done(((bf16[128,1024]{1,0:T(8,128)(2,1)}), bf16[2048,1024]{1,0:T(8,128)(2,1)}) %all-gather.12.cloned.1.call-update) | async-done | bytes 4194320 | tf_op jit(solution)/shard_map/all_gather | solution.py:231
  232.4 79.5 %all-gather.16.cloned.1.call-done = bf16[2048,1024]{0,1:T(8,128)(2,1)} async-done(((bf16[128,1024]{0,1:T(8,128)(2,1)}), bf16[2048,1024]{0,1:T(8,128)(2,1)}) %all-gather.16.cloned.1.call-update) | async-done | bytes 4194320 | tf_op jit(solution)/shard_map/all_gather | solution.py:230
  329.8 65.1 %all-gather.18.cloned.1.call-done = bf16[2304,2048]{0,1:T(8,128)(2,1)} async-done(((bf16[2304,64]{0,1:T(8,128)(2,1)}), bf16[2304,2048]{0,1:T(8,128)(2,1)}) %all-gather.18.cloned.1.call-update) | async-done | bytes 9437200 | tf_op jit(solution)/shard_map/all_gather | solution.py:219
  440.6 37.7 all-gather.20.cloned.1.call-done
  484.0 233.5 %all-gather.22.cloned.1.call-done = bf16[2304,9216]{0,1:T(8,128)(2,1)} async-done(((bf16[2304,288]{0,1:T(8,128)(2,1)}), bf16[2304,9216]{0,1:T(8,128)(2,1)}) %all-gather.22.cloned.1.call-update) | async-done | bytes 42467344 | tf_op jit(solution)/shard_map/all_gather | solution.py:275
  739.6 216.7 %all-gather.24.cloned.1.call-done = bf16[2304,9216]{0,1:T(8,128)(2,1)} async-done(((bf16[2304,288]{0,1:T(8,128)(2,1)}), bf16[2304,9216]{0,1:T(8,128)(2,1)}) %all-gather.24.cloned.1.call-update) | async-done | bytes 42467344 | tf_op jit(solution)/shard_map/all_gather | solution.py:276
  956.3 25.0 multiply_convert_fusion.1
  981.3 213.9 %all-gather.26.cloned.1.call-done = bf16[9216,2304]{1,0:T(8,128)(2,1)} async-done(((bf16[288,2304]{1,0:T(8,128)(2,1)}), bf16[9216,2304]{1,0:T(8,128)(2,1)}) %all-gather.26.cloned.1.call-update) | async-done | bytes 42467344 | tf_op jit(solution)/shard_map/all_gather | solution.py:283
  1314.8 30.3 while.81
  1381.5 30.8 fusion.151
  1412.4 32.4 fusion.150
  1444.8 111.4 %pad_maximum_fusion = f32[32,2,288,2304]{3,2,0,1:T(8,128)} fusion(f32[32,1,288,2304]{3,2,0,1:T(8,128)} %bitcast.93, f32[32,1,288,2304]{3,2,0,1:T(8,128)} %bitcast.92), kind=kLoop, calls=%fused_computation.125 | loop fusion | flops 42467328 | bytes 339738624 | tf_op jit(solution)/shard_map/stack | solution.py:38
  1556.2 112.0 %copy.199 = f32[32,2,288,2304]{3,2,1,0:T(8,128)} copy(f32[32,2,288,2304]{3,2,0,1:T(8,128)} %pad_maximum_fusion) | data formatting | bytes 339738624 | tf_op jit(solution)/shard_map/stack | solution.py:38
  1693.9 27.3 reduce-scatter.10.cloned.1.call-done
  1729.8 48.3 %fusion.152 = f32[9216,2304]{1,0:T(8,128)} fusion(bf16[128,9216]{1,0:T(8,128)(2,1)S(1)} %copy-done.8, bf16[128,2304]{1,0:T(8,128)(2,1)} %get-tuple-element.931), kind=kOutput, calls=%fused_computation.281 | convolution fusion | flops 5435817984 | bytes 87883776 | tf_op jit(solution)/shard_map/dot_general | solution.py:18
  1794.2 42.4 all-reduce
  1838.6 1284.4 %reduce-scatter.22.cloned.1.call-done = f32[576,2304]{1,0:T(8,128)} async-done(((f32[18432,2304]{1,0:T(8,128)}), f32[576,2304]{1,0:T(8,128)}) %reduce-scatter.22.cloned.1.call-update) | async-done | bytes 5308432 | tf_op jit(solution)/shard_map/reduce_scatter | solution.py:308
  3128.3 208.6 %reduce-scatter.20.cloned.1.call-done = f32[64,2304]{1,0:T(8,128)} async-done(((f32[2048,2304]{1,0:T(8,128)}), f32[64,2304]{1,0:T(8,128)}) %reduce-scatter.20.cloned.1.call-update) | async-done | bytes 589840 | tf_op jit(solution)/shard_map/reduce_scatter | solution.py:392
  3336.9 213.6 %reduce-scatter.14.cloned.1.call-done = f32[2304,64]{0,1:T(8,128)} async-done(((f32[2304,2048]{0,1:T(8,128)}), f32[2304,64]{0,1:T(8,128)}) %reduce-scatter.14.cloned.1.call-update) | async-done | bytes 589840 | tf_op jit(solution)/shard_map/reduce_scatter | solution.py:389
  3550.5 141.7 %reduce-scatter.18.cloned.1.call-done = f32[2304,32]{0,1:T(8,128)} async-done(((f32[2304,1024]{0,1:T(8,128)}), f32[2304,32]{0,1:T(8,128)}) %reduce-scatter.18.cloned.1.call-update) | async-done | bytes 294928 | tf_op jit(solution)/shard_map/reduce_scatter | solution.py:391
  3692.2 141.1 %reduce-scatter.16.cloned.1.call-done = f32[2304,32]{0,1:T(8,128)} async-done(((f32[2304,1024]{0,1:T(8,128)}), f32[2304,32]{0,1:T(8,128)}) %reduce-scatter.16.cloned.1.call-update) | async-done | bytes 294928 | tf_op jit(solution)/shard_map/reduce_scatter | solution.py:390
  3833.3 725.3 %reduce-scatter.24.cloned.1.call-done = f32[288,2304]{1,0:T(8,128)} async-done(((f32[9216,2304]{1,0:T(8,128)}), f32[288,2304]{1,0:T(8,128)}) %reduce-scatter.24.cloned.1.call-update) | async-done | bytes 2654224 | tf_op jit(solution)/shard_map/reduce_scatter | solution.py:305
  (347 shorter events, 420.3 us)
Async XLA Ops:
  7.2 70.1 %all-gather.10.cloned.1.call-start = ((), (), s32[]{:S(2)}) async-start(), calls=%async_computation.8 | async-start | bytes 4866048 | tf_op jit(solution)/shard_map/all_gather | solution.py:221
  7.9 134.8 %all-gather.14.cloned.1.call-start = ((), (), s32[]{:S(2)}) async-start(), calls=%async_computation.10 | async-start | bytes 4866048 | tf_op jit(solution)/shard_map/all_gather | solution.py:220
  8.7 212.3 %all-gather.12.cloned.1.call-start = ((), (), s32[]{:S(2)}) async-start(), calls=%async_computation.9 | async-start | bytes 4456448 | tf_op jit(solution)/shard_map/all_gather | solution.py:231
  9.5 385.4 %copy-start.28 = (f32[2304]{0:T(1024)}, f32[2304]{0:T(1024)S(1)}, u32[]{:S(2)}) copy-start(f32[2304]{0:T(1024)S(1)} %get-tuple-element.801) | copy-start | bytes 27652
  11.3 383.6 %copy-start.39 = (f32[128]{0:T(128)}, f32[128]{0:T(128)S(1)}, u32[]{:S(2)}) copy-start(f32[128]{0:T(128)S(1)} %get-tuple-element.951) | copy-start | bytes 1540
  77.3 65.4 %copy-start = (bf16[1,128,2304]{2,1,0:T(8,128)(2,1)S(1)}, bf16[1,128,2304]{2,1,0:T(8,128)(2,1)}, u32[]{:S(2)}) copy-start(bf16[1,128,2304]{2,1,0:T(8,128)(2,1)} %param.23) | copy-start | bytes 1769476
  82.3 229.7 %all-gather.16.cloned.1.call-start = ((), (), s32[]{:S(2)}) async-start(), calls=%async_computation.11 | async-start | bytes 4456448 | tf_op jit(solution)/shard_map/all_gather | solution.py:230
  85.2 316.6 %copy-start.26 = (f32[128,128]{1,0:T(8,128)}, f32[128,128]{1,0:T(8,128)S(1)}, u32[]{:S(2)}) copy-start(f32[128,128]{1,0:T(8,128)S(1)} %get-tuple-element.949) | copy-start | bytes 196612
  147.7 247.3 %all-gather.18.cloned.1.call-start = ((), (), s32[]{:S(2)}) async-start(), calls=%async_computation.12 | async-start | bytes 9732096 | tf_op jit(solution)/shard_map/all_gather | solution.py:219
  148.3 330.0 %all-gather.20.cloned.1.call-start = ((), (), s32[]{:S(2)}) async-start(), calls=%async_computation.13 | async-start | bytes 9732096 | tf_op jit(solution)/shard_map/all_gather | solution.py:267
  148.8 568.6 %all-gather.22.cloned.1.call-start = ((), (), s32[]{:S(2)}) async-start(), calls=%async_computation.14 | async-start | bytes 43794432 | tf_op jit(solution)/shard_map/all_gather | solution.py:275
  149.6 806.7 %all-gather.24.cloned.1.call-start = ((), (), s32[]{:S(2)}) async-start(), calls=%async_computation.15 | async-start | bytes 43794432 | tf_op jit(solution)/shard_map/all_gather | solution.py:276
  150.3 1044.8 %all-gather.26.cloned.1.call-start = ((), (), s32[]{:S(2)}) async-start(), calls=%async_computation.16 | async-start | bytes 43794432 | tf_op jit(solution)/shard_map/all_gather | solution.py:283
  151.1 1536.7 %reduce-scatter.12.cloned.1.call-start = ((), (), s32[]{:S(2)}) async-start(), calls=%async_computation.18 | async-start | bytes 8912896 | tf_op jit(solution)/shard_map/reduce_scatter | solution.py:365
  484.0 472.3 %copy-start.9 = (bf16[128,2304]{1,0:T(8,128)(2,1)}, bf16[128,2304]{1,0:T(8,128)(2,1)S(1)}, u32[]{:S(2)}) copy-start(bf16[128,2304]{1,0:T(8,128)(2,1)S(1)} %multiply_convert_fusion.2) | copy-start | bytes 1769476
  1362.4 358.8 %reduce-scatter.10.cloned.1.call-start = ((), (), s32[]{:S(2)}) async-start(), calls=%async_computation.17 | async-start | bytes 8912896 | tf_op jit(solution)/shard_map/reduce_scatter | solution.py:364
  1379.7 1743.3 %reduce-scatter.22.cloned.1.call-start = ((), (), s32[]{:S(2)}) async-start(), calls=%async_computation.23 | async-start | bytes 175177728 | tf_op jit(solution)/shard_map/reduce_scatter | solution.py:308
  1668.1 1668.7 %reduce-scatter.20.cloned.1.call-start = ((), (), s32[]{:S(2)}) async-start(), calls=%async_computation.22 | async-start | bytes 19464192 | tf_op jit(solution)/shard_map/reduce_scatter | solution.py:392
  1677.3 1873.2 %reduce-scatter.14.cloned.1.call-start = ((), (), s32[]{:S(2)}) async-start(), calls=%async_computation.19 | async-start | bytes 19464192 | tf_op jit(solution)/shard_map/reduce_scatter | solution.py:389
  1687.5 2004.8 %reduce-scatter.18.cloned.1.call-start = ((), (), s32[]{:S(2)}) async-start(), calls=%async_computation.21 | async-start | bytes 9732096 | tf_op jit(solution)/shard_map/reduce_scatter | solution.py:391
  1693.9 2139.5 %reduce-scatter.16.cloned.1.call-start = ((), (), s32[]{:S(2)}) async-start(), calls=%async_computation.20 | async-start | bytes 9732096 | tf_op jit(solution)/shard_map/reduce_scatter | solution.py:390
  1728.2 2830.5 %reduce-scatter.24.cloned.1.call-start = ((), (), s32[]{:S(2)}) async-start(), calls=%async_computation.24 | async-start | bytes 87588864 | tf_op jit(solution)/shard_map/reduce_scatter | solution.py:305
  1789.7 47.6 %copy-start.13 = (f32[128,2304]{1,0:T(8,128)S(1)}, f32[128,2304]{1,0:T(8,128)}, u32[]{:S(2)}) copy-start(f32[128,2304]{1,0:T(8,128)} %copy-done.12) | copy-start | bytes 3538948
  1789.7 47.6 %copy-start.41 = (f32[128]{0:T(128)S(1)}, f32[128]{0:T(128)}, u32[]{:S(2)}) copy-start(f32[128]{0:T(128)} %get-tuple-element.950) | copy-start | bytes 1540
  (36 other events, 230.6 us)
Sparse Core Ops, SparseCore 0:
  10.9 66.3 all-gather.9
  80.2 62.4 all-gather.13
  146.0 74.8 all-gather.11
  224.1 87.7 all-gather.15
  314.7 80.2 all-gather.17
  397.7 80.4 all-gather.19
  481.1 236.3 all-gather.21
  720.4 235.8 all-gather.23
  959.2 235.8 all-gather.25
  1362.6 175.9 reduce-scatter.11
  1540.9 180.2 reduce-scatter.9
  1727.5 1395.5 reduce-scatter.21
  3131.2 205.6 reduce-scatter.19
  3344.8 205.6 reduce-scatter.13
  3557.8 134.3 reduce-scatter.17
  3698.6 134.6 reduce-scatter.15
  3841.3 717.3 reduce-scatter.23
where the time goes:
time: 4580 us; the launch traced here: 4570 us
  waiting for transfers between devices  3780 us (83%)
  matrix products  331 us (7%)
  local copies, waits for them, and re-layouts  236 us (5%)
  other arithmetic  154 us (3%)
    reduce_scatter x1, waiting for transfers between devices, shards(): lax.psum_scatter(paired_term(normed_second, gate_grad_low, up_grad_low, f...  1280 us
    reduce_scatter x1, waiting for transfers between devices, shards(): lax.psum_scatter(contract(mixed, ffn_grad_low, 0, 0), ('ctx', 'fsdp'), sc...  725 us
    all_gather x1, waiting for transfers between devices, shards(): lax.all_gather(gate_weight, ('ctx', 'fsdp'), axis=1, tiled=True)  233 us
    dot_general x14, matrix products, contract(): lax.dot_general(left, right, (((left_dim,), (right_dim,)), ((), ())), pre...  219 us
    all_gather x1, waiting for transfers between devices, shards(): lax.all_gather(up_weight, ('ctx', 'fsdp'), axis=1, tiled=True)  217 us
    all_gather x1, waiting for transfers between devices, shards(): lax.all_gather(down_weight, ('ctx', 'fsdp'), axis=0, tiled=True)  214 us
    reduce_scatter x1, waiting for transfers between devices, shards(): lax.psum_scatter(query_weight_grad, ('ctx', 'fsdp'), scatter_dimension=1,...  214 us
    reduce_scatter x1, waiting for transfers between devices, shards(): lax.psum_scatter(output_weight_grad, ('ctx', 'fsdp'), scatter_dimension=0...  209 us
  transfers between devices with their start and end apart: 17, of which 16 were waited for; matrix products, arithmetic and copies ran while one was open for 12% of the time, Pallas kernels for 0%

commit v1 on v0

v1 whole, which is shorter than its diff:
```python
import jax
import jax.numpy as jnp
from jax import lax
from jax.sharding import Mesh, PartitionSpec as P

HEADS = 8
KV_HEADS = 4
HEAD = 256

EPSILON = 1e-06
SOFT_CAP = 50.0
QUERY_SCALE = 0.0625

LOW = jnp.bfloat16
WIDE = jnp.float32

EVERY = ("line", "plane", "fsdp")


def contract(left, right, left_dim, right_dim):
    return lax.dot_general(
        left, right, (((left_dim,), (right_dim,)), ((), ())), preferred_element_type=WIDE
    )


def inverse_root(matrix_in):
    return lax.rsqrt(jnp.mean(matrix_in * matrix_in, axis=-1, keepdims=True) + EPSILON)


def norm_back(matrix_in, inverse, scale_row, upstream):
    weighted = upstream * scale_row
    inner = jnp.mean(matrix_in * weighted, axis=-1, keepdims=True)
    back = inverse * weighted - matrix_in * (inverse * inverse * inverse) * inner
    return (back, jnp.sum(upstream * matrix_in * inverse, axis=0))


def rope_tables(positions):
    half_size = HEAD // 2
    frequency = 10000.0 ** (-jnp.arange(half_size, dtype=WIDE) * 2.0 / HEAD)
    angles = positions.astype(WIDE)[:, None] * frequency[None, :]
    return (jnp.cos(angles)[:, None, :], jnp.sin(angles)[:, None, :])


def rotate(matrix_in, cosine, sine_table, head_count, direction):
    row_count = matrix_in.shape[0]
    half_size = HEAD // 2
    shaped = matrix_in.reshape(row_count, head_count, HEAD)
    first_half = shaped[..., :half_size]
    second_half = shaped[..., half_size:]
    return jnp.concatenate(
        [
            first_half * cosine - direction * second_half * sine_table,
            second_half * cosine + direction * first_half * sine_table,
        ],
        axis=-1,
    )


def line_gather(block):
    count = lax.axis_size("line")
    place = lax.axis_index("line")
    up, down = block, block
    ups, downs = {}, {}
    for step in range(1, count):
        up = lax.ppermute(up, "line", [(z, z + 1) for z in range(step - 1, count - 1)])
        down = lax.ppermute(down, "line", [(z, z - 1) for z in range(1, count - step + 1)])
        ups[step], downs[step] = up, down
    slots = [block]
    for turn in range(1, count):
        slots.append(jnp.where(place + turn < count, downs[turn], ups[count - turn]))
    return jnp.concatenate(slots, axis=0)


def line_scatter(parts):
    count = lax.axis_size("line")
    up = parts[count - 1].astype(LOW)
    down = parts[1].astype(LOW)
    for step in range(1, count):
        up = lax.ppermute(up, "line", [(z, z + 1) for z in range(0, step)])
        down = lax.ppermute(down, "line", [(z, z - 1) for z in range(count - step, count)])
        if step < count - 1:
            up = (parts[count - 1 - step] + up.astype(WIDE)).astype(LOW)
            down = (parts[1 + step] + down.astype(WIDE)).astype(LOW)
            up, down = lax.optimization_barrier((up, down))
    return parts[0] + up.astype(WIDE) + down.astype(WIDE)


def swap(value, bits):
    count = lax.axis_size("plane")
    return lax.ppermute(value, "plane", [(b, b ^ bits) for b in range(count)])


def plane_order():
    count = lax.axis_size("plane")
    if count == 4:
        own = lax.axis_index("plane")
        return [own, own ^ 1, own ^ 2, own ^ 3]
    return list(range(count))


def plane_gather(block):
    if lax.axis_size("plane") != 4:
        return lax.all_gather(block, "plane", axis=0, tiled=True)
    half = block.shape[0] // 2
    one, two = swap(block, 1), swap(block, 2)
    first, second = swap(two[:half], 1), swap(one[half:], 2)
    return jnp.concatenate([block, one, two, first, second], axis=0)


def plane_scatter(total):
    count = lax.axis_size("plane")
    if count != 4:
        return lax.psum_scatter(total, "plane", scatter_dimension=0, tiled=True)
    rows = total.shape[0] // count
    half = rows // 2
    own, one, two, far = [total[i * rows : (i + 1) * rows] for i in range(count)]
    low_far = far.astype(LOW)
    for_two = swap(low_far[:half], 1).astype(WIDE)
    for_one = swap(low_far[half:], 2).astype(WIDE)
    send_one = jnp.concatenate([one[:half], one[half:] + for_one], axis=0).astype(LOW)
    send_two = jnp.concatenate([two[:half] + for_two, two[half:]], axis=0).astype(LOW)
    return own + swap(send_one, 1).astype(WIDE) + swap(send_two, 2).astype(WIDE)


def sibling(value):
    return lax.ppermute(value, "fsdp", [(0, 1), (1, 0)])


def shards(
    tokens,
    cotangent,
    pair_table,
    query_weight,
    key_weight,
    value_weight,
    output_weight,
    gate_weight,
    up_weight,
    down_weight,
    norm_scales,
):
    line_count = lax.axis_size("line")
    plane_count = lax.axis_size("plane")
    fsdp_count = lax.axis_size("fsdp")
    sharers = plane_count * fsdp_count
    line_place = lax.axis_index("line")
    plane_place = lax.axis_index("plane")
    core = lax.axis_index("fsdp")
    devices = line_count * plane_count
    model = tokens.shape[2]
    row_count = tokens.shape[1]
    half_rows = row_count // 2
    span = line_count * row_count
    group_size = HEADS // KV_HEADS
    query_local = query_weight.shape[1]
    key_local = key_weight.shape[1]
    output_local = output_weight.shape[0]
    ff_local = gate_weight.shape[1]
    query_width = query_local * sharers
    key_width = key_local * sharers

    tokens_own = tokens[0]
    tokens_line = line_gather(tokens_own)

    attn_local = jnp.concatenate(
        [jnp.concatenate([query_weight, key_weight, value_weight], axis=1).T, output_weight], axis=0
    )
    attn_all = lax.all_gather(attn_local, ("plane", "fsdp"), axis=0, tiled=False)
    paired_local = jnp.concatenate([gate_weight.T, up_weight.T], axis=0)
    paired_all = lax.all_gather(paired_local, ("fsdp", "plane"), axis=0, tiled=True)
    down_all = lax.all_gather(down_weight, ("fsdp", "plane"), axis=0, tiled=True)

    edge_one = query_local
    edge_two = edge_one + key_local
    edge_three = edge_two + key_local
    projection = jnp.concatenate(
        [
            attn_all[:, :edge_one].reshape(-1, model),
            attn_all[:, edge_one:edge_two].reshape(-1, model),
            attn_all[:, edge_two:edge_three].reshape(-1, model),
        ],
        axis=0,
    )
    output_all = attn_all[:, edge_three:].reshape(-1, model)

    offsets = jnp.arange(row_count, dtype=jnp.int32)

    def place_rows(line_index, plane_index):
        pair = pair_table[line_index * plane_count + plane_index]
        return jnp.where(
            offsets < half_rows,
            pair * half_rows + offsets,
            (2 * devices - 1 - pair) * half_rows + offsets - half_rows,
        )

    line_order = [(line_place + turn) % line_count for turn in range(line_count)]
    positions = jnp.concatenate([place_rows(line, plane_place) for line in line_order])
    key_positions = jnp.concatenate(
        [place_rows(line, plane) for plane in plane_order() for line in line_order]
    )
    cosine, sine_table = rope_tables(positions)
    scales = norm_scales.astype(WIDE)

    wide_line = tokens_line.astype(WIDE)
    inverse_line = inverse_root(wide_line)
    unit_line = wide_line * inverse_line
    normed_first = (unit_line * scales[0]).astype(LOW)

    raw = contract(normed_first, projection, 1, 1)
    queries = (
        rotate(raw[:, :query_width], cosine, sine_table, group_size, 1.0) * QUERY_SCALE
    ).astype(LOW)
    key_rows = rotate(raw[:, query_width : query_width + key_width], cosine, sine_table, 1, 1.0)
    value_rows = raw[:, query_width + key_width :]
    both = jnp.concatenate([key_rows[:, 0].astype(LOW), value_rows.astype(LOW)], axis=1)
    both_all = plane_gather(both)
    keys_all = both_all[:, :key_width]
    values_all = both_all[:, key_width:]

    allowed = key_positions[None, :] <= positions[:, None]
    stacked = queries.transpose(1, 0, 2).reshape(group_size * span, HEAD)
    bounded = jnp.tanh(contract(stacked, keys_all, 1, 1) * (1.0 / SOFT_CAP))
    allowed_all = jnp.concatenate([allowed] * group_size, axis=0)
    grown = jnp.where(allowed_all, jnp.exp(SOFT_CAP * bounded), 0.0)
    weights_soft = grown * (1.0 / jnp.sum(grown, axis=-1, keepdims=True))
    weights_low = weights_soft.astype(LOW)
    slope = weights_soft * (1.0 - bounded * bounded)
    attn_full = contract(weights_low, values_all, 1, 0)
    attn_low = (
        attn_full.astype(LOW).reshape(group_size, span, HEAD).transpose(1, 0, 2).reshape(span, -1)
    )

    branch_out = line_scatter(
        contract(attn_low, output_all, 1, 0).reshape(line_count, row_count, model)
    )

    inputs = tokens_own.astype(WIDE)
    inverse_two = inverse_root(branch_out)
    hidden = inputs + branch_out * inverse_two * scales[1]
    inverse_three = inverse_root(hidden)
    normed_second = line_gather((hidden * inverse_three * scales[2]).astype(LOW))

    pair_out = contract(paired_all, normed_second, 1, 1).reshape(sharers, 2 * ff_local, span)

    def mix(gate_in, up_in):
        return jax.nn.gelu(gate_in, approximate=True) * up_in

    gate_out = pair_out[:, :ff_local]
    up_out = pair_out[:, ff_local:]
    mixed = mix(gate_out, up_out).astype(LOW).reshape(sharers * ff_local, span)
    ffn_out = line_scatter(contract(mixed, down_all, 0, 0).reshape(line_count, row_count, model))

    inverse_four = inverse_root(ffn_out)
    result = hidden + ffn_out * inverse_four * scales[3]
    upstream = cotangent[0].astype(WIDE)
    ffn_grad, scale_four = norm_back(ffn_out, inverse_four, scales[3], upstream)
    ffn_grad_low = line_gather(ffn_grad.astype(LOW))

    mixed_grad = contract(down_all, ffn_grad_low, 1, 1).reshape(sharers, ff_local, span)
    _, gelu_pull = jax.vjp(mix, gate_out, up_out)
    gate_grad, up_grad = gelu_pull(mixed_grad)
    pair_grad = jnp.concatenate([gate_grad.astype(LOW), up_grad.astype(LOW)], axis=1).reshape(
        sharers * 2 * ff_local, span
    )
    second_grad = line_scatter(
        contract(pair_grad, paired_all, 0, 0).reshape(line_count, row_count, model)
    )

    def both_cores(value):
        amount = value.shape[0] // fsdp_count
        own = lax.dynamic_slice_in_dim(value, core * amount, amount, 0)
        away = lax.dynamic_slice_in_dim(value, (1 - core) * amount, amount, 0)
        return jnp.concatenate([own, sibling(away)], axis=1)

    down_grad = contract(
        both_cores(mixed), jnp.concatenate([ffn_grad_low, sibling(ffn_grad_low)], axis=0), 1, 0
    )
    down_share = lax.psum_scatter(
        down_grad.astype(LOW), "plane", scatter_dimension=0, tiled=True
    ).astype(WIDE)
    paired_weight_grad = contract(
        both_cores(pair_grad),
        jnp.concatenate([normed_second, sibling(normed_second)], axis=0),
        1,
        0,
    )
    paired_share = lax.psum_scatter(
        paired_weight_grad.astype(LOW), "plane", scatter_dimension=0, tiled=True
    ).astype(WIDE)

    hidden_part, scale_three = norm_back(hidden, inverse_three, scales[2], second_grad)
    hidden_grad = upstream + hidden_part
    branch_grad, scale_two = norm_back(branch_out, inverse_two, scales[1], hidden_grad)
    branch_grad_low = line_gather(branch_grad.astype(LOW))

    attn_grad = contract(branch_grad_low, output_all, 1, 1).astype(LOW)
    output_weight_grad = contract(attn_low, branch_grad_low, 0, 0)
    attn_grad = (
        attn_grad.reshape(span, group_size, HEAD)
        .transpose(1, 0, 2)
        .reshape(group_size * span, HEAD)
    )
    row_inner = jnp.sum(attn_grad.astype(WIDE) * attn_full, axis=-1, keepdims=True)
    weight_grad = contract(attn_grad, values_all, 1, 1)
    score_grad = (slope * (weight_grad - row_inner)).astype(LOW)
    key_grad = contract(score_grad, stacked, 0, 0)
    value_grad = contract(weights_low, attn_grad, 0, 0)
    query_grad = contract(score_grad, keys_all, 1, 0)
    own_grad = plane_scatter(jnp.concatenate([key_grad, value_grad], axis=1))

    query_grad = query_grad.reshape(group_size, span, HEAD).transpose(1, 0, 2)
    query_raw_low = (
        (rotate(query_grad, cosine, sine_table, group_size, -1.0) * QUERY_SCALE)
        .astype(LOW)
        .reshape(span, query_width)
    )
    key_raw_low = rotate(own_grad[:, :key_width], cosine, sine_table, 1, -1.0)[:, 0].astype(LOW)
    raw_low = jnp.concatenate([query_raw_low, key_raw_low, own_grad[:, key_width:].astype(LOW)], 1)
    first_part = contract(raw_low, projection, 1, 0)
    scale_one = jnp.sum(first_part * unit_line, axis=0)
    first_grad = line_scatter(first_part.reshape(line_count, row_count, model))

    projection_grad = contract(raw_low, normed_first, 0, 0).astype(LOW)
    attn_weight_grad = jnp.concatenate(
        [
            projection_grad[:query_width].reshape(sharers, query_local, model),
            projection_grad[query_width : query_width + key_width].reshape(
                sharers, key_local, model
            ),
            projection_grad[query_width + key_width :].reshape(sharers, key_local, model),
            output_weight_grad.astype(LOW).reshape(sharers, output_local, model),
        ],
        axis=1,
    )
    attn_share = lax.psum_scatter(
        attn_weight_grad.reshape(-1, model), ("plane", "fsdp"), scatter_dimension=0, tiled=True
    ).astype(WIDE)

    input_part, _ = norm_back(inputs, inverse_root(inputs), scales[0], first_grad)
    input_grad = hidden_grad + input_part

    scale_grads = jnp.stack([scale_one, scale_two, scale_three, scale_four], axis=0)
    all_count = devices * fsdp_count
    scale_cut = scale_grads.reshape(4, all_count, -1).transpose(1, 0, 2).reshape(all_count, -1)
    scale_share = jnp.sum(lax.all_to_all(scale_cut, EVERY, 0, 0, tiled=True), axis=0).reshape(4, -1)

    return (
        result.astype(LOW)[None],
        input_grad.astype(LOW)[None],
        attn_share[:edge_one].T,
        attn_share[edge_one:edge_two].T,
        attn_share[edge_two:edge_three].T,
        attn_share[edge_three:],
        paired_share[:ff_local].T,
        paired_share[ff_local:].T,
        down_share,
        scale_share,
    )


def solution(mesh):
    devices, fsdp_count = mesh.devices.shape
    inner = Mesh(
        mesh.devices.reshape(KV_HEADS, devices // KV_HEADS, fsdp_count), EVERY
    )
    rows = P("fsdp", ("line", "plane"), None)
    return jax.shard_map(
        shards,
        mesh=inner,
        in_specs=(
            rows,
            rows,
            P(),
            P(None, EVERY),
            P(None, EVERY),
            P(None, EVERY),
            P(EVERY, None),
            P(None, EVERY),
            P(None, EVERY),
            P(EVERY, None),
            P(),
        ),
        out_specs=(
            rows,
            rows,
            P(None, EVERY),
            P(None, EVERY),
            P(None, EVERY),
            P(EVERY, None),
            P(None, EVERY),
            P(None, EVERY),
            P(EVERY, None),
            P(None, EVERY),
        ),
        check_vma=False,
    )
```

time: 4580 us -> 778 us (0.17)
  waiting for transfers between devices: 3780 us -> 350 us
  matrix products: 331 us -> 119 us
  local copies, waits for them, and re-layouts: 236 us -> 67.2 us
  starting transfers between devices: 1.07 us -> 110 us
  other arithmetic: 154 us -> 76.8 us
    reduce_scatter x8 -> x3, waiting for transfers between devices: 2740 us -> 60.7 us  [the longest x1 60.7 us: shards(): lax.psum_scatter(paired_weight_grad.astype(LOW), 'plane', scatter_dimensi...]
    all_gather x9 -> x3, waiting for transfers between devices: 1030 us -> 0.01 us  [the longest x1 0.01 us: shards(): lax.all_gather(attn_local, ('plane', 'fsdp'), axis=0, tiled=False)]
    ppermute x0 -> x60, waiting for transfers between devices: none -> 289 us  [the longest x12 106 us: line_scatter(): up = lax.ppermute(up, 'line', [(z, z + 1) for z in range(0, step)])]
    another operation x13 -> x0, local copies, waits for them, and re-layouts: 123 us -> none  [the longest x1 112 us: paired_term(): jnp.stack([gate_part.reshape(groups, shard_width, -1), up_part.reshape(gr...]
    dot_general x42 -> x0, matrix products: 112 us -> none  [the longest x1 25 us: shards(): jnp.dot(normed_second, pieces[1], preferred_element_type=jnp.float32)]
    another operation x6 -> x4, other arithmetic: 114 us -> 3.36 us  [the longest x1 111 us: paired_term(): jnp.stack([gate_part.reshape(groups, shard_width, -1), up_part.reshape(gr...]
    ppermute x0 -> x60, starting transfers between devices: none -> 110 us  [the longest x12 55.7 us: line_scatter(): up = lax.ppermute(up, 'line', [(z, z + 1) for z in range(0, step)])]
    dot_general x14 -> x18, matrix products: 219 us -> 119 us  [contract(): lax.dot_general(left, right, (((left_dim,), (right_dim,)), ((), ())), pre...]
  transfers between devices with their start and end apart: 17 -> 66, of which waited for: 16 -> 38; matrix products, arithmetic and copies ran while one was open for 12% -> 24% of each run, Pallas kernels for 0% -> 0%
where the time goes in v1:
time: 778 us; the launch traced here: 772 us
  waiting for transfers between devices  350 us (45%)
  matrix products  119 us (15%)
  starting transfers between devices  110 us (14%)
  other arithmetic  76.8 us (10%)
  local copies, waits for them, and re-layouts  67.2 us (9%)
  between operations  37.2 us (5%)
  blocking collectives  12 us (2%)
    dot_general x18, matrix products, contract(): lax.dot_general(left, right, (((left_dim,), (right_dim,)), ((), ())), pre...  119 us
    ppermute x12, waiting for transfers between devices, line_scatter(): up = lax.ppermute(up, 'line', [(z, z + 1) for z in range(0, step)])  106 us
    ppermute x12, waiting for transfers between devices, line_gather(): lax.ppermute(down, 'line', [(z, z - 1) for z in range(1, count - step + 1)])  101 us
    reduce_scatter x1, waiting for transfers between devices, shards(): lax.psum_scatter(paired_weight_grad.astype(LOW), 'plane', scatter_dimensi...  60.7 us
    ppermute x12, starting transfers between devices, line_scatter(): up = lax.ppermute(up, 'line', [(z, z + 1) for z in range(0, step)])  55.7 us
    ppermute x8, waiting for transfers between devices, swap(): return lax.ppermute(value, 'plane', [(b, b ^ bits) for b in range(count)])  45 us
    ppermute x12, starting transfers between devices, line_gather(): lax.ppermute(up, 'line', [(z, z + 1) for z in range(step - 1, count - 1)])  17.5 us
    ppermute x12, waiting for transfers between devices, line_gather(): lax.ppermute(up, 'line', [(z, z + 1) for z in range(step - 1, count - 1)])  17.4 us
  transfers between devices with their start and end apart: 66, of which 38 were waited for; matrix products, arithmetic and copies ran while one was open for 24% of the time, Pallas kernels for 0%

profile of v1, /device:TPU:0, one launch (start us, length us, event | category | flops | bytes accessed | tf_op | source)
XLA Modules:
  0.0 772.1 jit_solution(14609098836705468392)
XLA Ops:
  51.7 11.6 %collective-permute-done.4 = bf16[128,2304]{1,0:T(8,128)(2,1)S(1)} collective-permute-done((bf16[128,2304]{1,0:T(8,128)(2,1)S(1)}, bf16[128,2304]{1,0:T(8,128)(2,1)S(1)}, u32[]{:S(2)}, u32[]{:S(2)}) %collective-permute-start.4) | collective-permute-done | bytes 589856 | tf_op jit(solution)/shard_map/ppermute | solution.py:66
  64.9 13.9 %collective-permute-done.5 = bf16[128,2304]{1,0:T(8,128)(2,1)S(1)} collective-permute-done((bf16[128,2304]{1,0:T(8,128)(2,1)S(1)}, bf16[128,2304]{1,0:T(8,128)(2,1)S(1)}, u32[]{:S(2)}, u32[]{:S(2)}) %collective-permute-start.5) | collective-permute-done | bytes 589856 | tf_op jit(solution)/shard_map/ppermute | solution.py:66
  99.7 17.7 %collective-permute-done.7 = bf16[512,512]{1,0:T(8,128)(2,1)} collective-permute-done((bf16[512,512]{1,0:T(8,128)(2,1)}, bf16[512,512]{1,0:T(8,128)(2,1)}, u32[]{:S(2)}, u32[]{:S(2)}) %collective-permute-start.7) | collective-permute-done | bytes 524320 | tf_op jit(solution)/shard_map/ppermute | solution.py:90
  149.3 11.4 %collective-permute-done.10 = bf16[128,2304]{1,0:T(8,128)(2,1)S(1)} collective-permute-done((bf16[128,2304]{1,0:T(8,128)(2,1)S(1)}, bf16[128,2304]{1,0:T(8,128)(2,1)S(1)}, u32[]{:S(2)}, u32[]{:S(2)}) %collective-permute-start.10) | collective-permute-done | bytes 589856 | tf_op jit(solution)/shard_map/ppermute | solution.py:79
  166.3 11.6 %collective-permute-done.12 = bf16[128,2304]{1,0:T(8,128)(2,1)S(1)} collective-permute-done((bf16[128,2304]{1,0:T(8,128)(2,1)S(1)}, bf16[128,2304]{1,0:T(8,128)(2,1)S(1)}, u32[]{:S(2)}, u32[]{:S(2)}) %collective-permute-start.12) | collective-permute-done | bytes 589856 | tf_op jit(solution)/shard_map/ppermute | solution.py:79
  185.8 9.1 %collective-permute-done.14 = bf16[128,2304]{1,0:T(8,128)(2,1)S(1)} collective-permute-done((bf16[128,2304]{1,0:T(8,128)(2,1)S(1)}, bf16[128,2304]{1,0:T(8,128)(2,1)S(1)}, u32[]{:S(2)}, u32[]{:S(2)}) %collective-permute-start.14) | collective-permute-done | bytes 589856 | tf_op jit(solution)/shard_map/ppermute | solution.py:79
  222.0 12.9 %collective-permute-done.20 = bf16[128,2304]{1,0:T(8,128)(2,1)S(1)} collective-permute-done((bf16[128,2304]{1,0:T(8,128)(2,1)S(1)}, bf16[128,2304]{1,0:T(8,128)(2,1)S(1)}, u32[]{:S(2)}, u32[]{:S(2)}) %collective-permute-start.20) | collective-permute-done | bytes 589856 | tf_op jit(solution)/shard_map/ppermute | solution.py:66
  238.1 8.5 %collective-permute-done.21 = bf16[128,2304]{1,0:T(8,128)(2,1)S(1)} collective-permute-done((bf16[128,2304]{1,0:T(8,128)(2,1)S(1)}, bf16[128,2304]{1,0:T(8,128)(2,1)S(1)}, u32[]{:S(2)}, u32[]{:S(2)}) %collective-permute-start.21) | collective-permute-done | bytes 589856 | tf_op jit(solution)/shard_map/ppermute | solution.py:66
  247.8 15.0 %fusion.86 = f32[4608,512]{1,0:T(8,128)S(1)} fusion(bf16[4608,2304]{1,0:T(8,128)(2,1)} %all-gather.5.cloned.1.call-done, bf16[128,2304]{1,0:T(8,128)(2,1)} %get-tuple-element.63, bf16[128,2304]{1,0:T(8,128)(2,1)S(1)} %get-tuple-element.65, bf16[128,2304]{1,0:T(8,128)(2,1)S(1)} %get-tuple-element.67, bf16[128,2304]{1,0:T(8,128)(2,1)} %copy-done.26), kind=kOutput, calls=%fused_computation.264 | convolution fusion | flops 10881073152 | bytes 33030144 | tf_op jit(solution)/shard_map/dot_general | solution.py:21
  269.1 9.0 %fusion.102 = f32[512,2304]{1,0:T(8,128)S(1)} fusion(bf16[2304,512]{1,0:T(8,128)(2,1)} %bitcast.135, bf16[2304,2304]{1,0:T(8,128)(2,1)} %all-gather.7.cloned.1.call-done), kind=kOutput, calls=%fused_computation.277 | convolution fusion | flops 5435817984 | bytes 17694720 | tf_op jit(solution)/shard_map/dot_general | solution.py:21
  280.4 8.8 %collective-permute-done.22 = bf16[128,2304]{1,0:T(8,128)(2,1)S(1)} collective-permute-done((bf16[128,2304]{1,0:T(8,128)(2,1)S(1)}, bf16[128,2304]{1,0:T(8,128)(2,1)S(1)}, u32[]{:S(2)}, u32[]{:S(2)}) %collective-permute-start.22) | collective-permute-done | bytes 589856 | tf_op jit(solution)/shard_map/ppermute | solution.py:79
  303.3 11.8 %collective-permute-start.26 = (bf16[128,2304]{1,0:T(8,128)(2,1)S(1)}, bf16[128,2304]{1,0:T(8,128)(2,1)S(1)}, u32[]{:S(2)}, u32[]{:S(2)}) collective-permute-start(bf16[128,2304]{1,0:T(8,128)(2,1)S(1)} %get-tuple-element.32), channel_id=1, source_target_pairs={{0,8},{8,16},{16,24},{1,9},{9,17},{17,25},{2,10},{10,18},{18,26},{... | collective-permute-start | bytes 1769480 | tf_op jit(solution)/shard_map/ppermute | solution.py:79
  316.3 12.4 %collective-permute-done.26 = bf16[128,2304]{1,0:T(8,128)(2,1)S(1)} collective-permute-done((bf16[128,2304]{1,0:T(8,128)(2,1)S(1)}, bf16[128,2304]{1,0:T(8,128)(2,1)S(1)}, u32[]{:S(2)}, u32[]{:S(2)}) %collective-permute-start.26) | collective-permute-done | bytes 589856 | tf_op jit(solution)/shard_map/ppermute | solution.py:79
  352.8 9.8 %collective-permute-done.32 = bf16[128,2304]{1,0:T(8,128)(2,1)S(1)} collective-permute-done((bf16[128,2304]{1,0:T(8,128)(2,1)S(1)}, bf16[128,2304]{1,0:T(8,128)(2,1)S(1)}, u32[]{:S(2)}, u32[]{:S(2)}) %collective-permute-start.32) | collective-permute-done | bytes 589856 | tf_op jit(solution)/shard_map/ppermute | solution.py:66
  364.5 9.8 %collective-permute-done.33 = bf16[128,2304]{1,0:T(8,128)(2,1)S(1)} collective-permute-done((bf16[128,2304]{1,0:T(8,128)(2,1)S(1)}, bf16[128,2304]{1,0:T(8,128)(2,1)S(1)}, u32[]{:S(2)}, u32[]{:S(2)}) %collective-permute-start.33) | collective-permute-done | bytes 589856 | tf_op jit(solution)/shard_map/ppermute | solution.py:66
  377.5 12.5 %convolution_bitcast_fusion = f32[2304,512]{0,1:T(8,128)} fusion(bf16[2304,2304]{1,0:T(8,128)(2,1)} %all-gather.7.cloned.1.call-done, bf16[128,2304]{1,0:T(8,128)(2,1)S(1)} %get-tuple-element.55, bf16[128,2304]{1,0:T(8,128)(2,1)S(1)} %get-tuple-element.57, bf16[128,2304]{1,0:T(8,128)(2,1)S(1)} %get-tuple-element.59, bf16[128,2304]{1,0:T(8,128)(2,1)S(1)} %get-tuple-element.61), kind=kOutput, calls=%fused_computation.21 | convolution fusion | flops 5445255168 | bytes 17694720 | tf_op jit(solution)/shard_map/dot_general | solution.py:21
  403.3 16.6 %fusion.103 = f32[512,2304]{1,0:T(8,128)S(1)} fusion(bf16[4608,512]{1,0:T(8,128)(2,1)S(1)} %bitcast.129, bf16[4608,2304]{1,0:T(8,128)(2,1)} %all-gather.5.cloned.1.call-done), kind=kOutput, calls=%fused_computation.278 | convolution fusion | flops 10871635968 | bytes 30670848 | tf_op jit(solution)/shard_map/dot_general | solution.py:21
  523.1 8.6 %multiply_convert_fusion = bf16[1024,2048]{1,0:T(8,128)(2,1)S(1)} fusion(f32[1024,2048]{1,0:T(8,128)} %copy-done.11, bf16[1024,256]{1,0:T(8,128)(2,1)S(1)} %bitcast.153, f32[1024]{0:T(1024)S(1)} %multiply_reduce_fusion.7, f32[1024]{0:T(1024)S(1)} %broadcast_divide_fusion, pred[512,2048]{1,0:T(32,128)(4,1)S(1)} %copy-done.15, bf16[2048,512]{1,0:T(8,128)(2,1)S(1)} %copy-done.63), kind=kOutput, calls=%fused_computation.2 | convolution fusion | flops 1096810496 | bytes 15212544 | tf_op jit(solution)/shard_map/dot_general | solution.py:21
  554.2 10.5 %collective-permute-done.49 = bf16[512,512]{1,0:T(8,128)(2,1)} collective-permute-done((bf16[512,512]{1,0:T(8,128)(2,1)}, bf16[512,512]{1,0:T(8,128)(2,1)}, u32[]{:S(2)}, u32[]{:S(2)}) %collective-permute-start.49) | collective-permute-done | bytes 524320 | tf_op jit(solution)/shard_map/ppermute | solution.py:90
  599.7 16.0 %convolution_convert_fusion = bf16[2304,2304]{1,0:T(8,128)(2,1)} fusion(bf16[1024,2304]{1,0:T(8,128)(2,1)} %constant_dynamic-update-slice_fusion.6, bf16[2304,512]{1,0:T(8,128)(2,1)S(1)} %collective-permute-done.56, bf16[2304,512]{1,0:T(8,128)(2,1)S(1)} %get-tuple-element.93), kind=kOutput, calls=%fused_computation | convolution fusion | flops 10886381568 | bytes 20054016 | tf_op jit(solution)/shard_map/dot_general | solution.py:21
  625.6 13.4 %collective-permute-done.50 = bf16[128,2304]{1,0:T(8,128)(2,1)S(1)} collective-permute-done((bf16[128,2304]{1,0:T(8,128)(2,1)S(1)}, bf16[128,2304]{1,0:T(8,128)(2,1)S(1)}, u32[]{:S(2)}, u32[]{:S(2)}) %collective-permute-start.50) | collective-permute-done | bytes 589856 | tf_op jit(solution)/shard_map/ppermute | solution.py:79
  644.4 11.9 %collective-permute-done.52 = bf16[128,2304]{1,0:T(8,128)(2,1)S(1)} collective-permute-done((bf16[128,2304]{1,0:T(8,128)(2,1)S(1)}, bf16[128,2304]{1,0:T(8,128)(2,1)S(1)}, u32[]{:S(2)}, u32[]{:S(2)}) %collective-permute-start.52) | collective-permute-done | bytes 589856 | tf_op jit(solution)/shard_map/ppermute | solution.py:79
  673.8 12.0 %all_to_all.10 = f32[32,1,288]{2,1,0:T(1,128)} all-to-all(f32[32,1,288]{2,1,0:T(1,128)} %all_to_all.8), channel_id=1, replica_groups=mesh['line'=4,'plane'=4,'fsdp'=2] {'line','plane','fsdp'}, dimensions={0} | all-to-all | bytes 73728 | tf_op jit(solution)/shard_map/all_to_all | solution.py:345
  699.4 60.7 %reduce-scatter.6.cloned.1.call-done = bf16[576,2304]{1,0:T(8,128)(2,1)} async-done(((bf16[2304,2304]{1,0:T(8,128)(2,1)}), bf16[576,2304]{1,0:T(8,128)(2,1)}) %reduce-scatter.6.cloned.1.call-update) | async-done | bytes 2654224 | tf_op jit(solution)/shard_map/reduce_scatter | solution.py:287
  (447 shorter events, 399.8 us)
Async XLA Ops:
  7.2 72.5 %all-gather.9.cloned.1.call-start = ((), (), s32[]{:S(2)}) async-start(), calls=%async_computation.9 | async-start | bytes 7962624 | tf_op jit(solution)/shard_map/all_gather | solution.py:168
  10.5 237.3 %all-gather.5.cloned.1.call-start = ((), (), s32[]{:S(2)}) async-start(), calls=%async_computation.4 | async-start | bytes 23887872 | tf_op jit(solution)/shard_map/all_gather | solution.py:170
  12.3 256.8 %all-gather.7.cloned.1.call-start = ((), (), s32[]{:S(2)}) async-start(), calls=%async_computation.5 | async-start | bytes 11943936 | tf_op jit(solution)/shard_map/all_gather | solution.py:171
  13.3 29.4 %collective-permute-start.1 = (bf16[128,2304]{1,0:T(8,128)(2,1)S(1)}, bf16[128,2304]{1,0:T(8,128)(2,1)S(1)}, u32[]{:S(2)}, u32[]{:S(2)}) collective-permute-start(bf16[128,2304]{1,0:T(8,128)(2,1)S(1)} %bitcast.137), channel_id=1, source_target_pairs={{0,8},{8,16},{16,24},{1,9},{9,17},{17,25},{2,10},{10,18},{18,26},{... | collective-permute-start | bytes 1769480 | tf_op jit(solution)/shard_map/ppermute | solution.py:65
  18.3 25.2 %collective-permute-start = (bf16[128,2304]{1,0:T(8,128)(2,1)S(1)}, bf16[128,2304]{1,0:T(8,128)(2,1)S(1)}, u32[]{:S(2)}, u32[]{:S(2)}) collective-permute-start(bf16[128,2304]{1,0:T(8,128)(2,1)S(1)} %bitcast.138), channel_id=1, source_target_pairs={{8,0},{16,8},{24,16},{9,1},{17,9},{25,17},{10,2},{18,10},{26,18},{... | collective-permute-start | bytes 1769480 | tf_op jit(solution)/shard_map/ppermute | solution.py:66
  19.6 672.0 %reduce-scatter.8.cloned.1.call-start = ((), (), s32[]{:S(2)}) async-start(), calls=%async_computation.8 | async-start | bytes 6635520 | tf_op jit(solution)/shard_map/reduce_scatter | solution.py:278
  43.4 19.8 %collective-permute-start.4 = (bf16[128,2304]{1,0:T(8,128)(2,1)S(1)}, bf16[128,2304]{1,0:T(8,128)(2,1)S(1)}, u32[]{:S(2)}, u32[]{:S(2)}) collective-permute-start(bf16[128,2304]{1,0:T(8,128)(2,1)S(1)} %collective-permute-done), channel_id=1, source_target_pairs={{8,0},{16,8},{9,1},{17,9},{10,2},{18,10},{11,3},{19,11},{12,4},{20... | collective-permute-start | bytes 1769480 | tf_op jit(solution)/shard_map/ppermute | solution.py:66
  92.4 27.5 %collective-permute-start.6 = (bf16[512,512]{1,0:T(8,128)(2,1)}, bf16[512,512]{1,0:T(8,128)(2,1)}, u32[]{:S(2)}, u32[]{:S(2)}) collective-permute-start(bf16[512,512]{1,0:T(8,128)(2,1)} %get-tuple-element.142), channel_id=1, source_target_pairs={{0,2},{2,0},{4,6},{6,4},{1,3},{3,1},{5,7},{7,5},{8,10},{10,8},{12,... | collective-permute-start | bytes 1572872 | tf_op jit(solution)/shard_map/ppermute | solution.py:90
  93.9 23.5 %collective-permute-start.7 = (bf16[512,512]{1,0:T(8,128)(2,1)}, bf16[512,512]{1,0:T(8,128)(2,1)}, u32[]{:S(2)}, u32[]{:S(2)}) collective-permute-start(bf16[512,512]{1,0:T(8,128)(2,1)} %get-tuple-element.142), channel_id=1, source_target_pairs={{0,4},{2,6},{4,0},{6,2},{1,5},{3,7},{5,1},{7,3},{8,12},{10,14},{12... | collective-permute-start | bytes 1572872 | tf_op jit(solution)/shard_map/ppermute | solution.py:90
  161.0 17.0 %collective-permute-start.12 = (bf16[128,2304]{1,0:T(8,128)(2,1)S(1)}, bf16[128,2304]{1,0:T(8,128)(2,1)S(1)}, u32[]{:S(2)}, u32[]{:S(2)}) collective-permute-start(bf16[128,2304]{1,0:T(8,128)(2,1)S(1)} %get-tuple-element.26), channel_id=1, source_target_pairs={{0,8},{8,16},{1,9},{9,17},{2,10},{10,18},{3,11},{11,19},{4,12},{12... | collective-permute-start | bytes 1769480 | tf_op jit(solution)/shard_map/ppermute | solution.py:79
  178.2 16.7 %collective-permute-start.14 = (bf16[128,2304]{1,0:T(8,128)(2,1)S(1)}, bf16[128,2304]{1,0:T(8,128)(2,1)S(1)}, u32[]{:S(2)}, u32[]{:S(2)}) collective-permute-start(bf16[128,2304]{1,0:T(8,128)(2,1)S(1)} %get-tuple-element.28), channel_id=1, source_target_pairs={{0,8},{8,16},{16,24},{1,9},{9,17},{17,25},{2,10},{10,18},{18,26},{... | collective-permute-start | bytes 1769480 | tf_op jit(solution)/shard_map/ppermute | solution.py:79
  303.3 25.4 %collective-permute-start.26 = (bf16[128,2304]{1,0:T(8,128)(2,1)S(1)}, bf16[128,2304]{1,0:T(8,128)(2,1)S(1)}, u32[]{:S(2)}, u32[]{:S(2)}) collective-permute-start(bf16[128,2304]{1,0:T(8,128)(2,1)S(1)} %get-tuple-element.32), channel_id=1, source_target_pairs={{0,8},{8,16},{16,24},{1,9},{9,17},{17,25},{2,10},{10,18},{18,26},{... | collective-permute-start | bytes 1769480 | tf_op jit(solution)/shard_map/ppermute | solution.py:79
  315.0 17.8 %collective-permute-start.27 = (bf16[128,2304]{1,0:T(8,128)(2,1)S(1)}, bf16[128,2304]{1,0:T(8,128)(2,1)S(1)}, u32[]{:S(2)}, u32[]{:S(2)}) collective-permute-start(bf16[128,2304]{1,0:T(8,128)(2,1)S(1)} %get-tuple-element.33), channel_id=1, source_target_pairs={{8,0},{16,8},{24,16},{9,1},{17,9},{25,17},{10,2},{18,10},{26,18},{... | collective-permute-start | bytes 1769480 | tf_op jit(solution)/shard_map/ppermute | solution.py:80
  454.9 32.2 %collective-permute-start.58 = (bf16[1152,512]{1,0:T(8,128)(2,1)S(1)}, bf16[1152,512]{1,0:T(8,128)(2,1)S(1)}, u32[]{:S(2)}, u32[]{:S(2)}) collective-permute-start(bf16[1152,512]{1,0:T(8,128)(2,1)S(1)} %get-tuple-element.124), channel_id=1, source_target_pairs={{0,1},{1,0},{2,3},{3,2},{4,5},{5,4},{6,7},{7,6},{8,9},{9,8},{10,11... | collective-permute-start | bytes 3538952 | tf_op jit(solution)/shard_map/ppermute | solution.py:126
  455.2 31.7 %collective-permute-start.59 = (bf16[512,2304]{1,0:T(8,128)(2,1)S(1)}, bf16[512,2304]{1,0:T(8,128)(2,1)S(1)}, u32[]{:S(2)}, u32[]{:S(2)}) collective-permute-start(bf16[512,2304]{1,0:T(8,128)(2,1)S(1)} %pad_maximum_fusion.7), channel_id=1, source_target_pairs={{0,1},{1,0},{2,3},{3,2},{4,5},{5,4},{6,7},{7,6},{8,9},{9,8},{10,11... | collective-permute-start | bytes 7077896 | tf_op jit(solution)/shard_map/ppermute | solution.py:126
  477.2 17.4 %collective-permute-start.42 = (bf16[128,2304]{1,0:T(8,128)(2,1)}, bf16[128,2304]{1,0:T(8,128)(2,1)}, u32[]{:S(2)}, u32[]{:S(2)}) collective-permute-start(bf16[128,2304]{1,0:T(8,128)(2,1)} %collective-permute-done.41), channel_id=1, source_target_pairs={{8,16},{16,24},{9,17},{17,25},{10,18},{18,26},{11,19},{19,27},{12,... | collective-permute-start | bytes 1769480 | tf_op jit(solution)/shard_map/ppermute | solution.py:65
  485.6 16.3 %collective-permute-start.44 = (bf16[128,2304]{1,0:T(8,128)(2,1)}, bf16[128,2304]{1,0:T(8,128)(2,1)}, u32[]{:S(2)}, u32[]{:S(2)}) collective-permute-start(bf16[128,2304]{1,0:T(8,128)(2,1)} %collective-permute-done.40), channel_id=1, source_target_pairs={{8,0},{16,8},{9,1},{17,9},{10,2},{18,10},{11,3},{19,11},{12,4},{20... | collective-permute-start | bytes 1769480 | tf_op jit(solution)/shard_map/ppermute | solution.py:66
  494.6 200.0 %reduce-scatter.4.cloned.1.call-start = ((), (), s32[]{:S(2)}) async-start(), calls=%async_computation.6 | async-start | bytes 7962624 | tf_op jit(solution)/shard_map/reduce_scatter | solution.py:335
  543.9 20.7 %collective-permute-start.49 = (bf16[512,512]{1,0:T(8,128)(2,1)}, bf16[512,512]{1,0:T(8,128)(2,1)}, u32[]{:S(2)}, u32[]{:S(2)}) collective-permute-start(bf16[512,512]{1,0:T(8,128)(2,1)} %pad_maximum_fusion.15), channel_id=1, source_target_pairs={{0,4},{2,6},{4,0},{6,2},{1,5},{3,7},{5,1},{7,3},{8,12},{10,14},{12... | collective-permute-start | bytes 1572872 | tf_op jit(solution)/shard_map/ppermute | solution.py:90
  544.9 20.5 %collective-permute-start.47 = (bf16[512,512]{1,0:T(8,128)(2,1)}, bf16[512,512]{1,0:T(8,128)(2,1)}, u32[]{:S(2)}, u32[]{:S(2)}) collective-permute-start(bf16[512,512]{1,0:T(8,128)(2,1)} %pad_maximum_fusion.14), channel_id=1, source_target_pairs={{0,2},{2,0},{4,6},{6,4},{1,3},{3,1},{5,7},{7,5},{8,10},{10,8},{12,... | collective-permute-start | bytes 1572872 | tf_op jit(solution)/shard_map/ppermute | solution.py:90
  585.5 174.6 %reduce-scatter.6.cloned.1.call-start = ((), (), s32[]{:S(2)}) async-start(), calls=%async_computation.7 | async-start | bytes 13271040 | tf_op jit(solution)/shard_map/reduce_scatter | solution.py:287
  639.3 17.0 %collective-permute-start.52 = (bf16[128,2304]{1,0:T(8,128)(2,1)S(1)}, bf16[128,2304]{1,0:T(8,128)(2,1)S(1)}, u32[]{:S(2)}, u32[]{:S(2)}) collective-permute-start(bf16[128,2304]{1,0:T(8,128)(2,1)S(1)} %get-tuple-element.38), channel_id=1, source_target_pairs={{0,8},{8,16},{1,9},{9,17},{2,10},{10,18},{3,11},{11,19},{4,12},{12... | collective-permute-start | bytes 1769480 | tf_op jit(solution)/shard_map/ppermute | solution.py:79
  657.4 29.9 %collective-permute-start.54 = (bf16[128,2304]{1,0:T(8,128)(2,1)}, bf16[128,2304]{1,0:T(8,128)(2,1)S(1)}, u32[]{:S(2)}, u32[]{:S(2)}) collective-permute-start(bf16[128,2304]{1,0:T(8,128)(2,1)} %get-tuple-element.40), channel_id=1, source_target_pairs={{0,8},{8,16},{16,24},{1,9},{9,17},{17,25},{2,10},{10,18},{18,26},{... | collective-permute-start | bytes 1769480 | tf_op jit(solution)/shard_map/ppermute | solution.py:79
  663.7 23.5 %collective-permute-start.55 = (bf16[128,2304]{1,0:T(8,128)(2,1)S(1)}, bf16[128,2304]{1,0:T(8,128)(2,1)S(1)}, u32[]{:S(2)}, u32[]{:S(2)}) collective-permute-start(bf16[128,2304]{1,0:T(8,128)(2,1)S(1)} %get-tuple-element.41), channel_id=1, source_target_pairs={{8,0},{16,8},{24,16},{9,1},{17,9},{25,17},{10,2},{18,10},{26,18},{... | collective-permute-start | bytes 1769480 | tf_op jit(solution)/shard_map/ppermute | solution.py:80
  (129 other events, 1643.5 us)
Sparse Core Ops, SparseCore 0:
  10.6 51.5 all-gather.8
  64.7 122.6 all-gather.4
  189.2 62.8 all-gather.6
  494.7 72.1 reduce-scatter.7
  585.6 66.0 reduce-scatter.3
  655.0 105.1 reduce-scatter.5

commit v2 on v1

v2 whole, which is shorter than its diff:
```python
import functools

import jax
import jax.numpy as jnp
from jax import lax
from jax.experimental import pallas as pl
from jax.experimental.pallas import tpu as pltpu
from jax.sharding import Mesh, PartitionSpec as P

HEADS = 8
KV_HEADS = 4
HEAD = 256

EPSILON = 1e-06
SOFT_CAP = 50.0
QUERY_SCALE = 0.0625

LOW = jnp.bfloat16
WIDE = jnp.float32

EVERY = ("line", "plane", "fsdp")


def contract(left, right, left_dim, right_dim):
    return lax.dot_general(
        left, right, (((left_dim,), (right_dim,)), ((), ())), preferred_element_type=WIDE
    )


def inverse_root(matrix_in):
    return lax.rsqrt(jnp.mean(matrix_in * matrix_in, axis=-1, keepdims=True) + EPSILON)


def norm_back(matrix_in, inverse, scale_row, upstream):
    weighted = upstream * scale_row
    inner = jnp.mean(matrix_in * weighted, axis=-1, keepdims=True)
    return inverse * weighted - matrix_in * (inverse * inverse * inverse) * inner


def rope_tables(positions):
    half_size = HEAD // 2
    frequency = 10000.0 ** (-jnp.arange(half_size, dtype=WIDE) * 2.0 / HEAD)
    angles = positions.astype(WIDE)[:, None] * frequency[None, :]
    return (jnp.cos(angles), jnp.sin(angles))


VMEM_LIMIT = 56 * 1024 * 1024
COST = pl.CostEstimate(flops=0, bytes_accessed=64 * 1024 * 1024, transcendentals=0)


def params():
    return pltpu.CompilerParams(vmem_limit_bytes=VMEM_LIMIT)


def project_kernel(
    rows_ref, weight_ref, scale_ref, cos_ref, sin_ref, normed_ref, query_ref, pair_ref, *scratch
):
    key_width = pair_ref.shape[1] // 2
    query_width = query_ref.shape[0] // rows_ref.shape[0] * HEAD
    span = rows_ref.shape[0]
    packed = weight_ref
    if scratch:
        packed = scratch[0]
        sharers = weight_ref.shape[0]
        query_local, key_local = query_width // sharers, key_width // sharers
        for j in range(sharers):
            packed[j * query_local : (j + 1) * query_local] = weight_ref[j, :query_local]
            at = query_width + j * key_local
            from_row = query_local
            for _ in range(2):
                packed[at : at + key_local] = weight_ref[j, from_row : from_row + key_local]
                at += key_width
                from_row += key_local
    rows = rows_ref[...].astype(WIDE)
    inverse = lax.rsqrt(jnp.mean(rows * rows, axis=-1, keepdims=True) + EPSILON)
    normed = (rows * inverse * scale_ref[...]).astype(LOW)
    normed_ref[...] = normed
    cosine, sine_table = cos_ref[...], sin_ref[...]
    half = HEAD // 2

    def turn(raw):
        first, second = raw[:, :half], raw[:, half:]
        return first * cosine - second * sine_table, second * cosine + first * sine_table

    for head in range(query_width // HEAD):
        raw = contract(normed, packed[head * HEAD : (head + 1) * HEAD], 1, 1)
        first, second = turn(raw)
        query_ref[head * span : (head + 1) * span, :half] = (first * QUERY_SCALE).astype(LOW)
        query_ref[head * span : (head + 1) * span, half:] = (second * QUERY_SCALE).astype(LOW)
    raw = contract(normed, packed[query_width:], 1, 1)
    first, second = turn(raw[:, :key_width])
    pair_ref[:, :half] = first.astype(LOW)
    pair_ref[:, half:key_width] = second.astype(LOW)
    pair_ref[:, key_width:] = raw[:, key_width:].astype(LOW)


def project_call(rows, weights, scale_row, cosine, sine_table, query_width, key_width):
    span, model = rows.shape
    heads = query_width // HEAD
    return pl.pallas_call(
        project_kernel,
        out_shape=(
            jax.ShapeDtypeStruct((span, model), LOW),
            jax.ShapeDtypeStruct((heads * span, HEAD), LOW),
            jax.ShapeDtypeStruct((span, 2 * key_width), LOW),
        ),
        scratch_shapes=[pltpu.VMEM((query_width + 2 * key_width, model), LOW)]
        if weights.ndim == 3
        else [],
        compiler_params=params(),
        cost_estimate=COST,
    )(rows, weights, scale_row, cosine, sine_table)


KEY_BLOCK = 2048


def as_row(column):
    return jnp.broadcast_to(column, (column.shape[0], 128)).T[:1]


def attend_kernel(query_ref, pair_ref, place_ref, key_place_ref, out_ref, low_ref, inverse_ref):
    keys = pair_ref[:, :HEAD]
    values = pair_ref[:, HEAD:]
    bounded = jnp.tanh(contract(query_ref[...], keys, 1, 1) * (1.0 / SOFT_CAP))
    allowed = key_place_ref[...] <= place_ref[...]
    grown = jnp.where(allowed, jnp.exp(SOFT_CAP * bounded), 0.0)
    inverse = 1.0 / jnp.sum(grown, axis=-1, keepdims=True)
    weights = (grown * inverse).astype(LOW)
    out = contract(weights, values, 1, 0)
    out_ref[...] = out
    low_ref[...] = out.astype(LOW)
    inverse_ref[...] = as_row(inverse)


def attend_call(queries, pair, places_column, key_places_row, group_size):
    count = queries.shape[0]
    span = count // group_size
    keys = pair.shape[0]
    by_head = pl.BlockSpec((span, HEAD), lambda h: (0, h))
    return pl.pallas_call(
        attend_kernel,
        grid=(group_size,),
        in_specs=[
            pl.BlockSpec((span, HEAD), lambda h: (h, 0)),
            pl.BlockSpec((keys, 2 * HEAD), lambda h: (0, 0)),
            pl.BlockSpec((span, 1), lambda h: (0, 0)),
            pl.BlockSpec((1, keys), lambda h: (0, 0)),
        ],
        out_specs=[by_head, by_head, pl.BlockSpec((1, span), lambda h: (0, h))],
        out_shape=(
            jax.ShapeDtypeStruct((span, group_size * HEAD), WIDE),
            jax.ShapeDtypeStruct((span, group_size * HEAD), LOW),
            jax.ShapeDtypeStruct((1, count), WIDE),
        ),
        compiler_params=params(),
        cost_estimate=COST,
    )(queries, pair, places_column, key_places_row)


def attend_back_kernel(*refs):
    query_ref, grad_ref, out_ref, pair_ref, inverse_ref, place_ref, key_place_ref = refs[:7]
    cos_ref, sin_ref, *prior_refs, query_grad_ref, pair_grad_ref, total_ref, held_ref = refs[7:]
    part, head = pl.program_id(0), pl.program_id(1)
    keys = pair_ref[:, :HEAD]
    values = pair_ref[:, HEAD:]
    queries = query_ref[...]
    grads = grad_ref[...]
    inner = as_row(jnp.sum(grads.astype(WIDE) * out_ref[...], axis=-1, keepdims=True))
    bounded = jnp.tanh(contract(keys, queries, 1, 1) * (1.0 / SOFT_CAP))
    allowed = key_place_ref[...] <= place_ref[...]
    weights = jnp.where(allowed, jnp.exp(SOFT_CAP * bounded) * inverse_ref[...], 0.0)
    weight_grad = contract(values, grads, 1, 1)
    score_grad = (weights * (weight_grad - inner) * (1.0 - bounded * bounded)).astype(LOW)
    query_part = contract(score_grad, keys, 0, 0)

    @pl.when(part == 0)
    def _():
        held_ref[head] = query_part

    @pl.when(part > 0)
    def _():
        held_ref[head] += query_part

    query_grad = held_ref[head]
    half = HEAD // 2
    first, second = query_grad[:, :half], query_grad[:, half:]
    cosine, sine_table = cos_ref[...], sin_ref[...]
    query_grad_ref[:, :half] = ((first * cosine + second * sine_table) * QUERY_SCALE).astype(LOW)
    query_grad_ref[:, half:] = ((second * cosine - first * sine_table) * QUERY_SCALE).astype(LOW)
    key_grad = contract(score_grad, queries, 1, 0)
    value_grad = contract(weights.astype(LOW), grads, 1, 0)

    @pl.when(head == 0)
    def _():
        if prior_refs:
            total_ref[:, :HEAD] = prior_refs[0][:, :HEAD] + key_grad
            total_ref[:, HEAD:] = prior_refs[0][:, HEAD:] + value_grad
        else:
            total_ref[:, :HEAD] = key_grad
            total_ref[:, HEAD:] = value_grad

    @pl.when(head > 0)
    def _():
        total_ref[:, :HEAD] += key_grad
        total_ref[:, HEAD:] += value_grad

    @pl.when(head == pl.num_programs(1) - 1)
    def _():
        pair_grad_ref[...] = total_ref[...].astype(pair_grad_ref.dtype)


def attend_back_call(
    queries, grads, out, pair, inverse, places_row, key_places_column, cosine, sine_table, prior, group_size
):
    count = queries.shape[0]
    span = count // group_size
    keys = pair.shape[0]
    block = min(keys, KEY_BLOCK)
    by_head = pl.BlockSpec((span, HEAD), lambda k, h: (0, h))
    by_keys = pl.BlockSpec((block, 2 * HEAD), lambda k, h: (k, 0))
    table = pl.BlockSpec((span, HEAD // 2), lambda k, h: (0, 0))
    extra = [] if prior is None else [prior]
    return pl.pallas_call(
        attend_back_kernel,
        grid=(keys // block, group_size),
        in_specs=[
            pl.BlockSpec((span, HEAD), lambda k, h: (h, 0)),
            by_head,
            by_head,
            by_keys,
            pl.BlockSpec((1, span), lambda k, h: (0, h)),
            pl.BlockSpec((1, span), lambda k, h: (0, 0)),
            pl.BlockSpec((block, 1), lambda k, h: (k, 0)),
            table,
            table,
        ]
        + [by_keys] * len(extra),
        out_specs=[by_head, by_keys],
        out_shape=(
            jax.ShapeDtypeStruct((span, group_size * HEAD), LOW),
            jax.ShapeDtypeStruct((keys, 2 * HEAD), WIDE if prior is None else LOW),
        ),
        scratch_shapes=[
            pltpu.VMEM((block, 2 * HEAD), WIDE),
            pltpu.VMEM((group_size, span, HEAD), WIDE),
        ],
        compiler_params=params(),
        cost_estimate=COST,
    )(queries, grads, out, pair, inverse, places_row, key_places_column, cosine, sine_table, *extra)


def project_back_kernel(
    query_ref, own_ref, one_ref, two_ref, weight_ref, cos_ref, sin_ref, raw_ref, part_ref
):
    query_width = query_ref.shape[1]
    total = own_ref[...].astype(WIDE) + one_ref[...].astype(WIDE) + two_ref[...].astype(WIDE)
    half = HEAD // 2
    first, second = total[:, :half], total[:, half:HEAD]
    cosine, sine_table = cos_ref[...], sin_ref[...]
    raw_ref[:, :query_width] = query_ref[...]
    raw_ref[:, query_width : query_width + half] = (first * cosine + second * sine_table).astype(LOW)
    raw_ref[:, query_width + half : query_width + HEAD] = (
        second * cosine - first * sine_table
    ).astype(LOW)
    raw_ref[:, query_width + HEAD :] = total[:, HEAD:].astype(LOW)
    part_ref[...] = contract(raw_ref[...], weight_ref[...], 1, 0)


def project_back_call(query_grad, own, one, two, weights, cosine, sine_table):
    span = query_grad.shape[0]
    width, model = weights.shape
    return pl.pallas_call(
        project_back_kernel,
        out_shape=(
            jax.ShapeDtypeStruct((span, width), LOW),
            jax.ShapeDtypeStruct((span, model), WIDE),
        ),
        compiler_params=params(),
        cost_estimate=COST,
    )(query_grad, own, one, two, weights, cosine, sine_table)


GELU_ROOT = 0.7978845608028654
GELU_CUBE = 0.044715


STEPS = 4


def blocks_of(value, count, first):
    rows = value.shape[0] // (2 * count)
    return jnp.concatenate(
        [value[(2 * p + first) * rows : (2 * p + first + 1) * rows] for p in range(count)], axis=0
    )


def widen_kernel(
    parts, core_ref, rows_ref, weight_ref, mixed_ref, away_ref, bent_ref, slope_ref
):
    step = pl.program_id(0)
    both = contract(weight_ref[...], rows_ref[...], 1, 1)
    gate, up = blocks_of(both, parts, 0), blocks_of(both, parts, 1)
    square = gate * gate
    curve = jnp.tanh(GELU_ROOT * gate * (1.0 + GELU_CUBE * square))
    rise = 0.5 * (1.0 + curve)
    bent = gate * rise
    mixed = (bent * up).astype(LOW)
    mixed_ref[...] = mixed
    bent_ref[...] = bent
    steep = GELU_ROOT * (1.0 + 3.0 * GELU_CUBE * square)
    slope_ref[...] = up * (rise + 0.5 * gate * (1.0 - curve * curve) * steep)

    @pl.when(step // (STEPS // 2) != core_ref[0])
    def _():
        away_ref[...] = mixed


def away_block(step, core_ref):
    first = (1 - core_ref[0]) * (STEPS // 2)
    return (jnp.clip(step - first, 0, STEPS // 2 - 1), 0)


def widen_call(rows, weights, core, sharers):
    span, model = rows.shape
    amount = weights.shape[0] // 2
    block = amount // STEPS
    by_step = pl.BlockSpec((block, span), lambda j, core_ref: (j, 0))
    return pl.pallas_call(
        functools.partial(widen_kernel, sharers // STEPS),
        grid_spec=pltpu.PrefetchScalarGridSpec(
            num_scalar_prefetch=1,
            grid=(STEPS,),
            in_specs=[
                pl.BlockSpec((span, model), lambda j, core_ref: (0, 0)),
                pl.BlockSpec((2 * block, model), lambda j, core_ref: (j, 0)),
            ],
            out_specs=[by_step, pl.BlockSpec((block, span), away_block), by_step, by_step],
        ),
        out_shape=(
            jax.ShapeDtypeStruct((amount, span), LOW),
            jax.ShapeDtypeStruct((amount // 2, span), LOW),
            jax.ShapeDtypeStruct((amount, span), WIDE),
            jax.ShapeDtypeStruct((amount, span), WIDE),
        ),
        compiler_params=params(),
        cost_estimate=COST,
    )(core, rows, weights)


def narrow_back_kernel(
    parts, core_ref, rows_ref, weight_ref, bent_ref, slope_ref, grad_ref, away_ref
):
    step = pl.program_id(0)
    mixed_grad = contract(weight_ref[...], rows_ref[...], 1, 1)
    gate, up = mixed_grad * slope_ref[...], mixed_grad * bent_ref[...]
    rows = gate.shape[0] // parts
    grad = jnp.concatenate(
        [part[p * rows : (p + 1) * rows] for p in range(parts) for part in (gate, up)], axis=0
    ).astype(LOW)
    grad_ref[...] = grad

    @pl.when(step // (STEPS // 2) != core_ref[0])
    def _():
        away_ref[...] = grad


def narrow_back_call(rows, weights, bent, slope, core, sharers):
    span, model = rows.shape
    amount = weights.shape[0]
    block = amount // STEPS
    by_step = pl.BlockSpec((block, span), lambda j, core_ref: (j, 0))
    return pl.pallas_call(
        functools.partial(narrow_back_kernel, sharers // STEPS),
        grid_spec=pltpu.PrefetchScalarGridSpec(
            num_scalar_prefetch=1,
            grid=(STEPS,),
            in_specs=[
                pl.BlockSpec((span, model), lambda j, core_ref: (0, 0)),
                pl.BlockSpec((block, model), lambda j, core_ref: (j, 0)),
                by_step,
                by_step,
            ],
            out_specs=[
                pl.BlockSpec((2 * block, span), lambda j, core_ref: (j, 0)),
                pl.BlockSpec((2 * block, span), away_block),
            ],
        ),
        out_shape=(
            jax.ShapeDtypeStruct((2 * amount, span), LOW),
            jax.ShapeDtypeStruct((amount, span), LOW),
        ),
        compiler_params=params(),
        cost_estimate=COST,
    )(core, rows, weights, bent, slope)


def weight_grad_kernel(core_ref, *refs):
    *pairs, out_ref = refs
    half = len(pairs) // 2
    total = contract(pairs[0][...], pairs[half][...], 1, 0)
    for left, right in zip(pairs[1:half], pairs[half + 1 :]):
        total += contract(left[...], right[...], 1, 0)
    out_ref[...] = total.astype(LOW)


def weight_grad_call(own, away, rows, core):
    span, model = rows[0].shape
    amount = own[0].shape[0] // 2
    block = amount // STEPS
    mine = pl.BlockSpec((block, span), lambda j, core_ref: (core_ref[0] * STEPS + j, 0))
    theirs = pl.BlockSpec((block, span), lambda j, core_ref: (j, 0))
    whole = pl.BlockSpec((span, model), lambda j, core_ref: (0, 0))
    return pl.pallas_call(
        weight_grad_kernel,
        grid_spec=pltpu.PrefetchScalarGridSpec(
            num_scalar_prefetch=1,
            grid=(STEPS,),
            in_specs=[mine] * len(own) + [theirs] * len(away) + [whole] * len(rows),
            out_specs=pl.BlockSpec((block, model), lambda j, core_ref: (j, 0)),
        ),
        out_shape=jax.ShapeDtypeStruct((amount, model), LOW),
        compiler_params=params(),
        cost_estimate=COST,
    )(core, *own, *away, *rows)


def shard_grad_kernel(parts, place_ref, *refs):
    *pairs, near_ref, away_ref, total_ref = refs
    half = len(pairs) // 2
    total = contract(pairs[0][...], pairs[half][...], 0, 0)
    for left, right in zip(pairs[1:half], pairs[half + 1 :]):
        total += contract(left[...], right[...], 0, 0)
    total_ref[...] = total.astype(LOW)
    own, core = place_ref[0], place_ref[1]
    planes = near_ref.shape[0]
    for plane in range(planes):
        for side in range(2):
            to_row = 0
            for first, rows in parts:
                block = total_ref[pl.ds(first + (2 * plane + side) * rows, rows)]

                @pl.when(core == side)
                def _():
                    near_ref[plane ^ own, pl.ds(to_row, rows)] = block

                @pl.when(core != side)
                def _():
                    away_ref[plane ^ own, pl.ds(to_row, rows)] = block

                to_row += rows


def shard_grad_call(left, right, parts, place, planes):
    width, model = left[0].shape[1], right[0].shape[1]
    rows = sum(part[1] for part in parts)
    shape = jax.ShapeDtypeStruct((planes, rows, model), LOW)
    return pl.pallas_call(
        functools.partial(shard_grad_kernel, parts),
        in_specs=[pl.BlockSpec(memory_space=pltpu.SMEM)]
        + [pl.BlockSpec(memory_space=pltpu.VMEM)] * (len(left) + len(right)),
        out_specs=[pl.BlockSpec(memory_space=pltpu.VMEM)] * 2,
        out_shape=(shape, shape),
        scratch_shapes=[pltpu.VMEM((width, model), LOW)],
        compiler_params=params(),
        cost_estimate=COST,
    )(place, *left, *right)


def tie(value, *others):
    return lax.optimization_barrier((value, others))[0]


def choose(flag, one, two):
    return jnp.where(flag, one, two)


def nothing(*others):
    return ()


def line_gather(block, work, while_first=nothing, while_last=nothing):
    place = lax.axis_index("line")
    up = lax.ppermute(block, "line", [(0, 1), (1, 2), (2, 3)])
    down = lax.ppermute(block, "line", [(1, 0), (2, 1), (3, 2)])
    done = while_first(lambda value: tie(value, block))
    up, down, done_first = lax.optimization_barrier((up, down, done))
    up_two = lax.ppermute(up, "line", [(1, 2), (2, 3)])
    down_two = lax.ppermute(down, "line", [(1, 0), (2, 1)])
    first = work(0, jnp.concatenate([block, choose(place >= 1, up, down)], axis=0))
    up_two, down_two = tie((up_two, down_two), first)
    up_three = lax.ppermute(up_two, "line", [(2, 3)])
    down_three = lax.ppermute(down_two, "line", [(1, 0)])
    done = while_last(lambda value: tie(value, up_two, down_two))
    up_three, down_three, done_last = lax.optimization_barrier((up_three, down_three, done))
    third = choose(place >= 2, up_two, down_two)
    fourth = choose(place == 0, down_three, choose(place == 3, up_three, down))
    second = work(1, jnp.concatenate([third, fourth], axis=0))
    return first, second, done_first, done_last


def line_order():
    place = lax.axis_index("line")
    return jnp.stack(
        [
            place,
            choose(place >= 1, place - 1, 1),
            lax.rem(place + 2, 4),
            choose(place >= 1, lax.rem(place + 1, 4), 3),
        ]
    ).astype(jnp.int32)


def line_scatter(late, work, while_second=nothing, while_last=nothing):
    place = lax.axis_index("line")
    rows = late.shape[0] // 2
    third, fourth = late[:rows], late[rows:]
    low_fourth = fourth.astype(LOW)
    up = lax.ppermute(low_fourth, "line", [(0, 1)])
    down = lax.ppermute(low_fourth, "line", [(3, 2)])
    up, down, (early, done_first) = lax.optimization_barrier((up, down, work()))
    own, second = early[:rows], early[rows:]
    up = (third + up.astype(WIDE)).astype(LOW)
    down = (third + down.astype(WIDE)).astype(LOW)
    sent_up, sent_down = lax.optimization_barrier((up, down))
    up = lax.ppermute(sent_up, "line", [(0, 1), (1, 2)])
    down = lax.ppermute(sent_down, "line", [(3, 2), (2, 1)])
    done = while_second(lambda value: tie(value, sent_up, sent_down), done_first)
    up, down, done_second = lax.optimization_barrier((up, down, done))
    up = (choose(place == 0, second, fourth) + up.astype(WIDE)).astype(LOW)
    down = (second + down.astype(WIDE)).astype(LOW)
    sent_up, sent_down = lax.optimization_barrier((up, down))
    up = lax.ppermute(sent_up, "line", [(0, 1), (1, 2), (2, 3)])
    down = lax.ppermute(sent_down, "line", [(3, 2), (2, 1), (1, 0)])
    done = while_last(lambda value: tie(value, sent_up, sent_down), done_second)
    up, down, done_last = lax.optimization_barrier((up, down, done))
    return own + up.astype(WIDE) + down.astype(WIDE), done_first, done_second, done_last


def swap(value, bits):
    count = lax.axis_size("plane")
    return lax.ppermute(value, "plane", [(b, b ^ bits) for b in range(count)])


def plane_order():
    count = lax.axis_size("plane")
    if count == 4:
        own = lax.axis_index("plane")
        return [own, own ^ 1, own ^ 2, own ^ 3]
    return list(range(count))


def plane_gather(block):
    if lax.axis_size("plane") != 4:
        return lax.all_gather(block, "plane", axis=0, tiled=True)
    half = block.shape[0] // 2
    one, two = swap(block, 1), swap(block, 2)
    first, second = swap(two[:half], 1), swap(one[half:], 2)
    return jnp.concatenate([block, one, two, first, second], axis=0)


def plane_scatter_far(total):
    count = lax.axis_size("plane")
    rows = total.shape[0] // count
    half = rows // 2
    own, one, two, far = [total[i * rows : (i + 1) * rows] for i in range(count)]
    one, two = one.astype(WIDE), two.astype(WIDE)
    low_far = far.astype(LOW)
    for_two = swap(low_far[:half], 1).astype(WIDE)
    for_one = swap(low_far[half:], 2).astype(WIDE)
    send_one = jnp.concatenate([one[:half], one[half:] + for_one], axis=0).astype(LOW)
    send_two = jnp.concatenate([two[:half] + for_two, two[half:]], axis=0).astype(LOW)
    return own, send_one, send_two


def plane_scatter(total):
    if lax.axis_size("plane") != 4:
        summed = lax.psum_scatter(total, "plane", scatter_dimension=0, tiled=True)
        empty = jnp.zeros(summed.shape, LOW)
        return summed, empty, empty
    own, send_one, send_two = plane_scatter_far(total)
    return own, swap(send_one, 1), swap(send_two, 2)


def sibling(value):
    return lax.ppermute(value, "fsdp", [(0, 1), (1, 0)])


def shards(
    tokens,
    cotangent,
    pair_table,
    query_weight,
    key_weight,
    value_weight,
    output_weight,
    gate_weight,
    up_weight,
    down_weight,
    norm_scales,
):
    line_count = lax.axis_size("line")
    plane_count = lax.axis_size("plane")
    fsdp_count = lax.axis_size("fsdp")
    sharers = plane_count * fsdp_count
    line_place = lax.axis_index("line")
    plane_place = lax.axis_index("plane")
    core = lax.axis_index("fsdp")
    devices = line_count * plane_count
    model = tokens.shape[2]
    row_count = tokens.shape[1]
    half_rows = row_count // 2
    span = 2 * row_count
    group_size = HEADS // KV_HEADS
    query_local = query_weight.shape[1]
    key_local = key_weight.shape[1]
    ff_local = gate_weight.shape[1]
    query_width = query_local * sharers
    key_width = key_local * sharers
    chunks = range(2)

    attn_local = jnp.concatenate(
        [jnp.concatenate([query_weight, key_weight, value_weight], axis=1).T, output_weight], axis=0
    )
    attn_flat = lax.all_gather(attn_local, ("plane", "fsdp"), axis=0, tiled=False)
    core_ref = core.astype(jnp.int32)[None]
    place_ref = jnp.stack([plane_place, core]).astype(jnp.int32)
    paired_local = jnp.concatenate([gate_weight.T, up_weight.T], axis=0)
    paired_all = lax.all_gather(paired_local, ("fsdp", "plane"), axis=0, tiled=True)
    down_all = lax.all_gather(down_weight, ("fsdp", "plane"), axis=0, tiled=True)

    edge_one = query_local
    edge_two = edge_one + key_local
    edge_three = edge_two + key_local
    edge_four = edge_three + output_weight.shape[0]
    pair_ids = jnp.arange(devices, dtype=jnp.int32)
    order = line_order()

    def places(members, chunk):
        lines = order[2 * chunk : 2 * chunk + 2]
        index = (lines[None, :] * plane_count + members[:, None]).reshape(-1)
        pair = jnp.sum(
            jnp.where(index[:, None] == pair_ids[None, :], pair_table[None, :], 0), axis=1
        )
        offsets = jnp.arange(row_count, dtype=jnp.int32)
        return jnp.where(
            offsets[None, :] < half_rows,
            pair[:, None] * half_rows + offsets[None, :],
            (2 * devices - 1 - pair[:, None]) * half_rows + offsets[None, :] - half_rows,
        ).reshape(-1)

    members = jnp.stack([jnp.asarray(member, jnp.int32) for member in plane_order()])
    positions = [places(plane_place[None], c) for c in chunks]
    key_positions = jnp.concatenate([places(members, c) for c in chunks])
    tables = [rope_tables(positions[c]) for c in chunks]
    scales = norm_scales.astype(WIDE)

    tokens_own = tokens[0]
    tokens_line, normed_first, queries = [None] * 2, [None] * 2, [None] * 2

    def packed(held):
        return jnp.concatenate(
            [
                held[:, :edge_one].reshape(-1, model),
                held[:, edge_one:edge_two].reshape(-1, model),
                held[:, edge_two:edge_three].reshape(-1, model),
            ],
            axis=0,
        )

    def project(c, rows):
        tokens_line[c] = rows
        weights = attn_flat if plane_count == 4 else packed(attn_flat)
        normed_first[c], queries[c], both = project_call(
            rows, weights, scales[0:1], *tables[c], query_width, key_width
        )
        return plane_gather(both)

    pair_all = jnp.concatenate(line_gather(tokens_own, project)[:2], axis=0)
    attn_held = tie(attn_flat, queries[1])
    output_all = attn_held[:, edge_three:].reshape(-1, model)

    attn_full, attn_low, inverse_sums = [None] * 2, [None] * 2, [None] * 2

    def attend(c):
        attn_full[c], attn_low[c], inverse_sums[c] = attend_call(
            queries[c], pair_all, positions[c][:, None], key_positions[None, :], group_size
        )
        return contract(attn_low[c], output_all, 1, 0)

    def reorder(gate, _):
        return packed(gate(attn_flat))

    branch_out, _, projection, _ = line_scatter(
        attend(1), lambda: (attend(0), ()), while_second=reorder
    )

    inputs = tokens_own.astype(WIDE)
    inverse_two = inverse_root(branch_out)
    hidden = inputs + branch_out * inverse_two * scales[1]
    inverse_three = inverse_root(hidden)

    normed_second, mixed, mixed_away = [None] * 2, [None] * 2, [None] * 2
    bent, slope = [None] * 2, [None] * 2

    def widen(c, rows):
        normed_second[c] = rows
        mixed[c], mixed_away[c], bent[c], slope[c] = widen_call(rows, paired_all, core_ref, sharers)
        return mixed[c]

    line_gather((hidden * inverse_three * scales[2]).astype(LOW), widen)

    def keep_mixed(gate, _):
        return [sibling(gate(part)) for part in mixed_away]

    def keep_second(gate, _):
        return [sibling(gate(part)) for part in normed_second]

    ffn_out, _, mixed_theirs, second_theirs = line_scatter(
        contract(mixed[1], down_all, 0, 0),
        lambda: (contract(mixed[0], down_all, 0, 0), ()),
        while_second=keep_mixed,
        while_last=keep_second,
    )

    inverse_four = inverse_root(ffn_out)
    result = hidden + ffn_out * inverse_four * scales[3]
    upstream = cotangent[0].astype(WIDE)
    ffn_grad = norm_back(ffn_out, inverse_four, scales[3], upstream)

    ffn_grad_low, pair_grad, pair_away = [None] * 2, [None] * 2, [None] * 2

    def narrow_back(c, rows):
        ffn_grad_low[c] = rows
        pair_grad[c], pair_away[c] = narrow_back_call(
            rows, down_all, bent[c], slope[c], core_ref, sharers
        )
        return pair_grad[c]

    line_gather(ffn_grad.astype(LOW), narrow_back)

    def give_rows():
        theirs = [sibling(part) for part in pair_away], [sibling(part) for part in ffn_grad_low]
        return contract(pair_grad[0], paired_all, 0, 0), theirs

    def give_down(gate, theirs):
        return weight_grad_call(
            [gate(part) for part in mixed], mixed_theirs, ffn_grad_low + theirs[1], core_ref
        )

    second_grad, (pair_theirs, _), down_grad, _ = line_scatter(
        contract(pair_grad[1], paired_all, 0, 0), give_rows, while_second=give_down
    )
    down_share = lax.psum_scatter(down_grad, "plane", scatter_dimension=0, tiled=True)

    def give_paired(gate):
        return weight_grad_call(
            [gate(part) for part in pair_grad], pair_theirs, normed_second + second_theirs, core_ref
        )

    hidden_part = norm_back(hidden, inverse_three, scales[2], second_grad)
    hidden_grad = upstream + hidden_part
    branch_grad = norm_back(branch_out, inverse_two, scales[1], hidden_grad)

    branch_grad_low, query_raw_low, prior = [None] * 2, [None] * 2, [None] * 2

    def attend_back(c, rows):
        branch_grad_low[c] = rows
        grads = contract(rows, output_all, 1, 1).astype(LOW)
        query_raw_low[c], prior[c] = attend_back_call(
            queries[c],
            grads,
            attn_full[c],
            pair_all,
            inverse_sums[c],
            positions[c][None, :],
            key_positions[:, None],
            *tables[c],
            prior[0],
            group_size,
        )
        return query_raw_low[c], prior[c]

    def give_three(gate):
        sums = [
            jnp.sum(hidden_grad * gate(branch_out) * inverse_two, axis=0),
            jnp.sum(second_grad * gate(hidden) * inverse_three, axis=0),
            jnp.sum(upstream * gate(ffn_out) * inverse_four, axis=0),
        ]
        return jnp.stack(sums, axis=0), down_share.astype(WIDE)

    _, _, paired_grad, (scale_three, down_share) = line_gather(
        branch_grad.astype(LOW), attend_back, while_first=give_paired, while_last=give_three
    )
    paired_share = lax.psum_scatter(paired_grad, "plane", scatter_dimension=0, tiled=True)

    per_chunk = plane_count * span
    both_grads = jnp.concatenate(
        [prior[1][c * per_chunk : (c + 1) * per_chunk].reshape(plane_count, span, -1) for c in chunks],
        axis=1,
    ).reshape(2 * per_chunk, -1)
    own_terms = plane_scatter(both_grads)

    def shard_parts(left, right, parts):
        if plane_count == 4:
            return shard_grad_call(left, right, parts, place_ref, plane_count)
        grad = contract(
            jnp.concatenate(left, axis=0), jnp.concatenate(right, axis=0), 0, 0
        ).astype(LOW)
        blocks = [
            grad[first : first + rows * sharers].reshape(sharers, rows, model)
            for first, rows in parts
        ]
        blocks = jnp.concatenate(blocks, axis=1).reshape(plane_count, fsdp_count, -1, model)
        near = lax.dynamic_index_in_dim(blocks, core, 1, keepdims=False)
        return near, lax.dynamic_index_in_dim(blocks, 1 - core, 1, keepdims=False)

    output_near, output_away = shard_parts(
        [tie(part, prior[1]) for part in attn_low], branch_grad_low, [(0, edge_four - edge_three)]
    )
    own_terms = tie(own_terms, output_near)

    raw_low, first_part = [None] * 2, [None] * 2

    def project_back(c):
        terms = [term[c * span : (c + 1) * span] for term in own_terms]
        raw_low[c], first_part[c] = project_back_call(
            query_raw_low[c], *terms, projection, *tables[c]
        )
        return first_part[c]

    all_count = devices * fsdp_count

    def give_projection():
        early = project_back(0)
        parts = shard_parts(
            [tie(part, early) for part in raw_low],
            normed_first,
            [
                (0, query_local),
                (query_width, key_local),
                (query_width + key_width, key_local),
            ],
        )
        return early, parts

    def give_total(gate, parts):
        near, away = parts
        total = jnp.concatenate(
            [
                near.astype(WIDE) + sibling(gate(away)).astype(WIDE),
                output_near.astype(WIDE) + sibling(gate(output_away)).astype(WIDE),
            ],
            axis=1,
        ).reshape(-1, model)
        scale_one = 0.0
        for c in chunks:
            wide_line = gate(tokens_line[c]).astype(WIDE)
            scale_one += jnp.sum(first_part[c] * (wide_line * inverse_root(wide_line)), axis=0)
        return total, scale_one

    def give_far(gate, held):
        total, scale_one = held
        scale_grads = jnp.concatenate([scale_one[None], scale_three], axis=0)
        scale_cut = (
            scale_grads.reshape(4, all_count, -1).transpose(1, 0, 2).reshape(all_count, -1)
        )
        if plane_count == 4:
            return scale_cut, plane_scatter_far(total)
        return scale_cut, total

    first_grad, _, _, (scale_cut, attn_sends) = line_scatter(
        project_back(1), give_projection, while_second=give_total, while_last=give_far
    )
    if plane_count == 4:
        own, send_one, send_two = attn_sends
        one, two = swap(send_one, 1), swap(send_two, 2)
    else:
        own, one, two = plane_scatter(attn_sends)

    input_part = norm_back(inputs, inverse_root(inputs), scales[0], first_grad)
    input_grad = hidden_grad + input_part

    scale_cut = lax.all_to_all(scale_cut, EVERY, 0, 0, tiled=True)
    scale_share = jnp.sum(scale_cut, axis=0).reshape(4, -1)
    gate_share = paired_share[:ff_local].T.astype(WIDE)
    up_share = paired_share[ff_local:].T.astype(WIDE)
    one, two = tie((one, two), input_grad, gate_share, up_share, scale_share)
    attn_share = own + one.astype(WIDE) + two.astype(WIDE)

    return (
        result.astype(LOW)[None],
        input_grad.astype(LOW)[None],
        attn_share[:edge_one].T,
        attn_share[edge_one:edge_two].T,
        attn_share[edge_two:edge_three].T,
        attn_share[edge_three:],
        gate_share,
        up_share,
        down_share,
        scale_share,
    )


def solution(mesh):
    devices, fsdp_count = mesh.devices.shape
    inner = Mesh(
        mesh.devices.reshape(KV_HEADS, devices // KV_HEADS, fsdp_count), EVERY
    )
    rows = P("fsdp", ("line", "plane"), None)
    return jax.shard_map(
        shards,
        mesh=inner,
        in_specs=(
            rows,
            rows,
            P(),
            P(None, EVERY),
            P(None, EVERY),
            P(None, EVERY),
            P(EVERY, None),
            P(None, EVERY),
            P(None, EVERY),
            P(EVERY, None),
            P(),
        ),
        out_specs=(
            rows,
            rows,
            P(None, EVERY),
            P(None, EVERY),
            P(None, EVERY),
            P(EVERY, None),
            P(None, EVERY),
            P(None, EVERY),
            P(EVERY, None),
            P(None, EVERY),
        ),
        check_vma=False,
    )
```

time: 778 us -> 694 us (0.89)
  Pallas kernels: 0 us -> 141 us
  waiting for transfers between devices: 350 us -> 262 us
  matrix products: 119 us -> 41.4 us
  local copies, waits for them, and re-layouts: 67.2 us -> 35.6 us
  between operations: 37.2 us -> 16 us
  blocking collectives: 12 us -> 0 us
  starting transfers between devices: 110 us -> 120 us
  other arithmetic: 76.8 us -> 68.2 us
    pallas_call x0 -> x16, Pallas kernels: none -> 141 us  [the longest x2 28.2 us: widen_call(): pl.pallas_call(functools.partial(widen_kernel, sharers // STEPS), grid_sp...]
    dot_general x18 -> x8, matrix products: 119 us -> 41.4 us  [contract(): lax.dot_general(left, right, (((left_dim,), (right_dim,)), ((), ())), pre...]
    reduce_scatter x3 -> x2, waiting for transfers between devices: 60.7 us -> 0.02 us  [the longest x1 0.02 us: shards(): lax.psum_scatter(down_grad, 'plane', scatter_dimension=0, tiled=True)]
    ppermute x48, waiting for transfers between devices: 238 us -> 186 us  [the longest x4 46.5 us: line_gather(): down_three = lax.ppermute(down_two, 'line', [(1, 0)])]
    all_gather x1, waiting for transfers between devices: 0.01 us -> 18.3 us  [shards(): lax.all_gather(down_weight, ('fsdp', 'plane'), axis=0, tiled=True)]
    all_to_all x1 -> x0, blocking collectives: 12 us -> none  [shards(): lax.all_to_all(scale_cut, EVERY, 0, 0, tiled=True)]
    all_to_all x0 -> x1, waiting for transfers between devices: none -> 10.3 us  [shards(): scale_cut = lax.all_to_all(scale_cut, EVERY, 0, 0, tiled=True)]
    convert_element_type x19 -> x14, other arithmetic: 29 us -> 18.9 us  [the longest x1 4.62 us: shards(): up_share = paired_share[ff_local:].T.astype(WIDE)]
  transfers between devices with their start and end apart: 66 -> 80, of which waited for: 38 -> 37; matrix products, arithmetic and copies ran while one was open for 24% -> 17% of each run, Pallas kernels for 0% -> 21%
where the time goes in v2:
time: 694 us; the launch traced here: 683 us
  waiting for transfers between devices  262 us (38%)
  Pallas kernels  141 us (20%)
  starting transfers between devices  120 us (17%)
  other arithmetic  68.2 us (10%)
  matrix products  41.4 us (6%)
  local copies, waits for them, and re-layouts  35.6 us (5%)
  between operations  16 us (2%)
    ppermute x4, waiting for transfers between devices, line_gather(): down_three = lax.ppermute(down_two, 'line', [(1, 0)])  46.5 us
    ppermute x16, waiting for transfers between devices, swap(): return lax.ppermute(value, 'plane', [(b, b ^ bits) for b in range(count)])  46 us
    dot_general x8, matrix products, contract(): lax.dot_general(left, right, (((left_dim,), (right_dim,)), ((), ())), pre...  41.4 us
    ppermute x4, waiting for transfers between devices, line_scatter(): up = lax.ppermute(sent_up, 'line', [(0, 1), (1, 2), (2, 3)])  30.9 us
    ppermute x4, starting transfers between devices, line_scatter(): up = lax.ppermute(sent_up, 'line', [(0, 1), (1, 2), (2, 3)])  29.5 us
    pallas_call x2, Pallas kernels, widen_call(): pl.pallas_call(functools.partial(widen_kernel, sharers // STEPS), grid_sp...  28.2 us
    pallas_call x2, Pallas kernels, weight_grad_call(): pl.pallas_call(weight_grad_kernel, grid_spec=pltpu.PrefetchScalarGridSpec...  26.5 us
    ppermute x4, waiting for transfers between devices, line_gather(): up = lax.ppermute(block, 'line', [(0, 1), (1, 2), (2, 3)])  26.3 us
  transfers between devices with their start and end apart: 80, of which 37 were waited for; matrix products, arithmetic and copies ran while one was open for 17% of the time, Pallas kernels for 21%

profile of v2, /device:TPU:0, one launch (start us, length us, event | category | flops | bytes accessed | tf_op | source)
XLA Modules:
  0.0 683.4 jit_solution(17518840398702276080)
XLA Ops:
  20.4 10.3 %collective-permute-done = bf16[128,2304]{1,0:T(8,128)(2,1)S(1)} collective-permute-done((bf16[128,2304]{1,0:T(8,128)(2,1)S(1)}, bf16[128,2304]{1,0:T(8,128)(2,1)S(1)}, u32[]{:S(2)}, u32[]{:S(2)}) %collective-permute-start) | collective-permute-done | bytes 589856 | tf_op jit(solution)/shard_map/ppermute | solution.py:484
  39.4 14.4 %collective-permute-done.3 = bf16[128,2304]{1,0:T(8,128)(2,1)S(1)} collective-permute-done((bf16[128,2304]{1,0:T(8,128)(2,1)S(1)}, bf16[128,2304]{1,0:T(8,128)(2,1)S(1)}, u32[]{:S(2)}, u32[]{:S(2)}) %collective-permute-start.3) | collective-permute-done | bytes 589856 | tf_op jit(solution)/shard_map/ppermute | solution.py:489
  55.9 13.7 %collective-permute-done.5 = bf16[128,2304]{1,0:T(8,128)(2,1)S(1)} collective-permute-done((bf16[128,2304]{1,0:T(8,128)(2,1)S(1)}, bf16[128,2304]{1,0:T(8,128)(2,1)S(1)}, u32[]{:S(2)}, u32[]{:S(2)}) %collective-permute-start.5) | collective-permute-done | bytes 589856 | tf_op jit(solution)/shard_map/ppermute | solution.py:493
  96.9 9.2 %collective-permute-done.11 = bf16[256,512]{1,0:T(8,128)(2,1)S(1)} collective-permute-done((bf16[256,512]{1,0:T(8,128)(2,1)}, bf16[256,512]{1,0:T(8,128)(2,1)S(1)}, u32[]{:S(2)}, u32[]{:S(2)}) %collective-permute-start.11) | collective-permute-done | bytes 262176 | tf_op jit(solution)/shard_map/ppermute | solution.py:542
  189.5 14.0 %shard_map.190 = (bf16[2304,256]{1,0:T(8,128)(2,1)}, bf16[1152,256]{1,0:T(8,128)(2,1)}, f32[2304,256]{1,0:T(8,128)}, f32[2304,256]{1,0:T(8,128)}) custom-call(s32[1]{0:T(128)} %bitcast.22.core_ref, bf16[256,2304]{1,0:T(8,128)(2,1)} %pad_maximum_fusion.5.rows_ref.refs_4_, bf16[4608,2304]{1,0:T(8,128)(2,1)} %all-gather.5.cloned.1.call-done.weight_ref), custom_call_target="tpu_custom_call" | custom-call | bytes 67108864 | tf_op jit(solution)/shard_map/pallas_call | solution.py:329
  206.7 12.7 %collective-permute-done.25 = bf16[128,2304]{1,0:T(8,128)(2,1)S(1)} collective-permute-done((bf16[128,2304]{1,0:T(8,128)(2,1)}, bf16[128,2304]{1,0:T(8,128)(2,1)S(1)}, u32[]{:S(2)}, u32[]{:S(2)}) %collective-permute-start.25) | collective-permute-done | bytes 589856 | tf_op jit(solution)/shard_map/ppermute | solution.py:493
  220.6 14.2 %shard_map.191 = (bf16[2304,256]{1,0:T(8,128)(2,1)}, bf16[1152,256]{1,0:T(8,128)(2,1)}, f32[2304,256]{1,0:T(8,128)}, f32[2304,256]{1,0:T(8,128)}) custom-call(s32[1]{0:T(128)} %bitcast.22.core_ref, bf16[256,2304]{1,0:T(8,128)(2,1)} %pad_maximum_fusion.6.rows_ref.refs_5_, bf16[4608,2304]{1,0:T(8,128)(2,1)} %all-gather.5.cloned.1.call-done.weight_ref), custom_call_target="tpu_custom_call" | custom-call | bytes 67108864 | tf_op jit(solution)/shard_map/pallas_call | solution.py:329
  234.8 18.3 %all-gather.7.cloned.1.call-done.weight_ref = bf16[2304,2304]{1,0:T(8,128)(2,1)} async-done(((bf16[288,2304]{1,0:T(8,128)(2,1)}), bf16[2304,2304]{1,0:T(8,128)(2,1)}) %all-gather.7.cloned.1.call-update) | async-done | bytes 10616848 | tf_op jit(solution)/shard_map/all_gather | solution.py:630
  267.0 9.2 %collective-permute-done.26 = bf16[128,2304]{1,0:T(8,128)(2,1)S(1)} collective-permute-done((bf16[128,2304]{1,0:T(8,128)(2,1)S(1)}, bf16[128,2304]{1,0:T(8,128)(2,1)S(1)}, u32[]{:S(2)}, u32[]{:S(2)}) %collective-permute-start.26) | collective-permute-done | bytes 589856 | tf_op jit(solution)/shard_map/ppermute | solution.py:519
  282.3 12.1 %collective-permute-done.28 = bf16[128,2304]{1,0:T(8,128)(2,1)S(1)} collective-permute-done((bf16[128,2304]{1,0:T(8,128)(2,1)S(1)}, bf16[128,2304]{1,0:T(8,128)(2,1)S(1)}, u32[]{:S(2)}, u32[]{:S(2)}) %collective-permute-start.28) | collective-permute-done | bytes 589856 | tf_op jit(solution)/shard_map/ppermute | solution.py:526
  305.3 11.1 %collective-permute-done.32 = bf16[128,2304]{1,0:T(8,128)(2,1)S(1)} collective-permute-done((bf16[128,2304]{1,0:T(8,128)(2,1)S(1)}, bf16[128,2304]{1,0:T(8,128)(2,1)S(1)}, u32[]{:S(2)}, u32[]{:S(2)}) %collective-permute-start.32) | collective-permute-done | bytes 589856 | tf_op jit(solution)/shard_map/ppermute | solution.py:533
  326.8 10.6 %collective-permute-done.36 = bf16[128,2304]{1,0:T(8,128)(2,1)S(1)} collective-permute-done((bf16[128,2304]{1,0:T(8,128)(2,1)S(1)}, bf16[128,2304]{1,0:T(8,128)(2,1)S(1)}, u32[]{:S(2)}, u32[]{:S(2)}) %collective-permute-start.36) | collective-permute-done | bytes 589856 | tf_op jit(solution)/shard_map/ppermute | solution.py:484
  344.7 9.2 %shard_map.192 = (bf16[4608,256]{1,0:T(8,128)(2,1)}, bf16[2304,256]{1,0:T(8,128)(2,1)}) custom-call(s32[1]{0:T(128)} %bitcast.22.core_ref, bf16[256,2304]{1,0:T(8,128)(2,1)} %copy-done.17, bf16[2304,2304]{1,0:T(8,128)(2,1)} %all-gather.7.cloned.1.call-done.weight_ref, f32[2304,256]{1,0:T(8,128)} %get-tuple-element.213.bent_ref, ...), custom_call_target="tpu_custom_call" | custom-call | bytes 67108864 | tf_op jit(solution)/shard_map/pallas_call | solution.py:373
  359.5 13.0 %collective-permute-done.41 = bf16[128,2304]{1,0:T(8,128)(2,1)S(1)} collective-permute-done((bf16[128,2304]{1,0:T(8,128)(2,1)S(1)}, bf16[128,2304]{1,0:T(8,128)(2,1)S(1)}, u32[]{:S(2)}, u32[]{:S(2)}) %collective-permute-start.41) | collective-permute-done | bytes 589856 | tf_op jit(solution)/shard_map/ppermute | solution.py:493
  373.7 9.2 %shard_map.193 = (bf16[4608,256]{1,0:T(8,128)(2,1)}, bf16[2304,256]{1,0:T(8,128)(2,1)}) custom-call(s32[1]{0:T(128)} %bitcast.22.core_ref, bf16[256,2304]{1,0:T(8,128)(2,1)} %pad_maximum_fusion.8.rows_ref.refs_5_, bf16[2304,2304]{1,0:T(8,128)(2,1)} %all-gather.7.cloned.1.call-done.weight_ref, f32[2304,256]{1,0:T(8,128)} %get-tuple-element.220.bent_ref, ...), custom_call_target="tpu_custom_call" | custom-call | bytes 67108864 | tf_op jit(solution)/shard_map/pallas_call | solution.py:373
  382.9 10.9 %fusion.34 = f32[256,2304]{1,0:T(8,128)S(1)} fusion(bf16[4608,256]{1,0:T(8,128)(2,1)} %get-tuple-element.243.refs_1_, bf16[4608,2304]{1,0:T(8,128)(2,1)} %all-gather.5.cloned.1.call-done.weight_ref), kind=kOutput, calls=%fused_computation.189 | convolution fusion | flops 5435817984 | bytes 25952256 | tf_op jit(solution)/shard_map/dot_general | solution.py:25
  397.2 11.4 %fusion.35 = f32[256,2304]{1,0:T(8,128)} fusion(bf16[4608,256]{1,0:T(8,128)(2,1)S(1)} %copy-done.14, bf16[4608,2304]{1,0:T(8,128)(2,1)} %all-gather.5.cloned.1.call-done.weight_ref), kind=kOutput, calls=%fused_computation.190 | convolution fusion | flops 5435817984 | bytes 25952256 | tf_op jit(solution)/shard_map/dot_general | solution.py:25
  412.8 10.2 %shard_map.194 = bf16[1152,2304]{1,0:T(8,128)(2,1)} custom-call(s32[1]{0:T(128)} %bitcast.22.core_ref, bf16[2304,256]{1,0:T(8,128)(2,1)} %get-tuple-element.230.refs_0_, bf16[2304,256]{1,0:T(8,128)(2,1)} %get-tuple-element.231.refs_1_, bf16[1152,256]{1,0:T(8,128)(2,1)} %copy-done.48, bf16[1152,256]{1,0:T(8,128)(2,1)} %copy-done.47, ...), custom_call_target="tpu_custom_call" | custom-call | bytes 67108864 | tf_op jit(solution)/shard_map/pallas_call | solution.py:414
  437.5 9.1 %collective-permute-done.50 = bf16[128,2304]{1,0:T(8,128)(2,1)S(1)} collective-permute-done((bf16[128,2304]{1,0:T(8,128)(2,1)S(1)}, bf16[128,2304]{1,0:T(8,128)(2,1)S(1)}, u32[]{:S(2)}, u32[]{:S(2)}) %collective-permute-start.50) | collective-permute-done | bytes 589856 | tf_op jit(solution)/shard_map/ppermute | solution.py:533
  457.7 16.3 %shard_map.195 = bf16[2304,2304]{1,0:T(8,128)(2,1)} custom-call(s32[1]{0:T(128)} %bitcast.22.core_ref, bf16[4608,256]{1,0:T(8,128)(2,1)} %get-tuple-element.242.refs_0_, bf16[4608,256]{1,0:T(8,128)(2,1)} %get-tuple-element.243.refs_1_, bf16[2304,256]{1,0:T(8,128)(2,1)} %copy-done.42, bf16[2304,256]{1,0:T(8,128)(2,1)} %copy-done.43, ...), custom_call_target="tpu_custom_call" | custom-call | bytes 67108864 | tf_op jit(solution)/shard_map/pallas_call | solution.py:414
  484.1 9.9 %shard_map.196 = (bf16[256,512]{1,0:T(8,128)(2,1)}, f32[2048,512]{1,0:T(8,128)}) custom-call(bf16[512,256]{1,0:T(8,128)(2,1)} %get-tuple-element.172.query_ref.refs_0_, bf16[256,512]{1,0:T(8,128)(2,1)} %convolution_convert_fusion.1.refs_1_, f32[256,512]{1,0:T(8,128)} %get-tuple-element.250.refs_2_, bf16[2048,512]{1,0:T(8,128)(2,1)} %copy-done.1, ...), custom_call_target="tpu_custom_call" | custom-call | bytes 67108864 | tf_op jit(solution)/shard_map/pallas_call | solution.py:224
  514.1 10.7 %shard_map.197 = (bf16[256,512]{1,0:T(8,128)(2,1)}, bf16[2048,512]{1,0:T(8,128)(2,1)}) custom-call(bf16[512,256]{1,0:T(8,128)(2,1)} %get-tuple-element.167.query_ref.refs_0_, bf16[256,512]{1,0:T(8,128)(2,1)} %convolution_convert_fusion.refs_1_, f32[256,512]{1,0:T(8,128)} %get-tuple-element.262.refs_2_, bf16[2048,512]{1,0:T(8,128)(2,1)} %copy-done.1, ...), custom_call_target="tpu_custom_call" | custom-call | bytes 67108864 | tf_op jit(solution)/shard_map/pallas_call | solution.py:224
  550.8 14.9 %collective-permute-done.61 = bf16[512,512]{1,0:T(8,128)(2,1)} collective-permute-done((bf16[512,512]{1,0:T(8,128)(2,1)}, bf16[512,512]{1,0:T(8,128)(2,1)}, u32[]{:S(2)}, u32[]{:S(2)}) %collective-permute-start.61) | collective-permute-done | bytes 524320 | tf_op jit(solution)/shard_map/ppermute | solution.py:542
  656.4 10.3 %all-to-all-done = f32[32,1,288]{2,1,0:T(1,128)} async-done(((f32[32,1,288]{2,1,0:T(1,128)}), f32[32,1,288]{2,1,0:T(1,128)}, u32[]{:S(2)}, u32[]{:S(2)}) %all-to-all-start) | async-done | bytes 36896 | tf_op jit(solution)/shard_map/all_to_all | solution.py:884
  (459 shorter events, 382.5 us)
Async XLA Ops:
  7.2 64.1 %all-gather.9.cloned.1.call-start = ((), (), s32[]{:S(2)}) async-start(), calls=%async_computation.7 | async-start | bytes 7962624 | tf_op jit(solution)/shard_map/all_gather | solution.py:625
  9.4 180.1 %all-gather.5.cloned.1.call-start = ((), (), s32[]{:S(2)}) async-start(), calls=%async_computation.3 | async-start | bytes 23887872 | tf_op jit(solution)/shard_map/all_gather | solution.py:629
  12.2 240.9 %all-gather.7.cloned.1.call-start = ((), (), s32[]{:S(2)}) async-start(), calls=%async_computation.4 | async-start | bytes 11943936 | tf_op jit(solution)/shard_map/all_gather | solution.py:630
  12.9 488.1 %reduce-scatter.3.cloned.1.call-start = ((), (), s32[]{:S(2)}) async-start(), calls=%async_computation.5 | async-start | bytes 6635520 | tf_op jit(solution)/shard_map/reduce_scatter | solution.py:754
  35.6 18.2 %collective-permute-start.3 = (bf16[128,2304]{1,0:T(8,128)(2,1)S(1)}, bf16[128,2304]{1,0:T(8,128)(2,1)S(1)}, u32[]{:S(2)}, u32[]{:S(2)}) collective-permute-start(bf16[128,2304]{1,0:T(8,128)(2,1)S(1)} %collective-permute-done.1), channel_id=1, source_target_pairs={{8,0},{16,8},{9,1},{17,9},{10,2},{18,10},{11,3},{19,11},{12,4},{20... | collective-permute-start | bytes 1769480 | tf_op jit(solution)/shard_map/ppermute | solution.py:489
  86.9 19.7 %collective-permute-start.10 = (bf16[256,512]{1,0:T(8,128)(2,1)}, bf16[256,512]{1,0:T(8,128)(2,1)S(1)}, u32[]{:S(2)}, u32[]{:S(2)}) collective-permute-start(bf16[256,512]{1,0:T(8,128)(2,1)} %get-tuple-element.169), channel_id=1, source_target_pairs={{0,2},{2,0},{4,6},{6,4},{1,3},{3,1},{5,7},{7,5},{8,10},{10,8},{12,... | collective-permute-start | bytes 786440 | tf_op jit(solution)/shard_map/ppermute | solution.py:542
  87.5 18.6 %collective-permute-start.11 = (bf16[256,512]{1,0:T(8,128)(2,1)}, bf16[256,512]{1,0:T(8,128)(2,1)S(1)}, u32[]{:S(2)}, u32[]{:S(2)}) collective-permute-start(bf16[256,512]{1,0:T(8,128)(2,1)} %get-tuple-element.169), channel_id=1, source_target_pairs={{0,4},{2,6},{4,0},{6,2},{1,5},{3,7},{5,1},{7,3},{8,12},{10,14},{12... | collective-permute-start | bytes 786440 | tf_op jit(solution)/shard_map/ppermute | solution.py:542
  185.6 17.9 %collective-permute-start.22 = (bf16[128,2304]{1,0:T(8,128)(2,1)}, bf16[128,2304]{1,0:T(8,128)(2,1)}, u32[]{:S(2)}, u32[]{:S(2)}) collective-permute-start(bf16[128,2304]{1,0:T(8,128)(2,1)} %collective-permute-done.20), channel_id=1, source_target_pairs={{8,16},{16,24},{9,17},{17,25},{10,18},{18,26},{11,19},{19,27},{12,... | collective-permute-start | bytes 1769480 | tf_op jit(solution)/shard_map/ppermute | solution.py:488
  294.8 25.8 %collective-permute-start.35 = (bf16[256,2304]{1,0:T(8,128)(2,1)S(1)}, bf16[256,2304]{1,0:T(8,128)(2,1)S(1)}, u32[]{:S(2)}, u32[]{:S(2)}) collective-permute-start(bf16[256,2304]{1,0:T(8,128)(2,1)S(1)} %copy-done.16), channel_id=1, source_target_pairs={{0,1},{1,0},{2,3},{3,2},{4,5},{5,4},{6,7},{7,6},{8,9},{9,8},{10,11... | collective-permute-start | bytes 3538952 | tf_op jit(solution)/shard_map/ppermute | solution.py:586
  294.9 25.7 %collective-permute-start.34 = (bf16[256,2304]{1,0:T(8,128)(2,1)S(1)}, bf16[256,2304]{1,0:T(8,128)(2,1)S(1)}, u32[]{:S(2)}, u32[]{:S(2)}) collective-permute-start(bf16[256,2304]{1,0:T(8,128)(2,1)S(1)} %copy-done.15), channel_id=1, source_target_pairs={{0,1},{1,0},{2,3},{3,2},{4,5},{5,4},{6,7},{7,6},{8,9},{9,8},{10,11... | collective-permute-start | bytes 3538952 | tf_op jit(solution)/shard_map/ppermute | solution.py:586
  295.4 21.0 %collective-permute-start.32 = (bf16[128,2304]{1,0:T(8,128)(2,1)S(1)}, bf16[128,2304]{1,0:T(8,128)(2,1)S(1)}, u32[]{:S(2)}, u32[]{:S(2)}) collective-permute-start(bf16[128,2304]{1,0:T(8,128)(2,1)S(1)} %get-tuple-element.205), channel_id=1, source_target_pairs={{0,8},{8,16},{16,24},{1,9},{9,17},{17,25},{2,10},{10,18},{18,26},{... | collective-permute-start | bytes 1769480 | tf_op jit(solution)/shard_map/ppermute | solution.py:533
  343.7 64.8 %collective-permute-start.46 = (bf16[256,2304]{1,0:T(8,128)(2,1)S(1)}, bf16[256,2304]{1,0:T(8,128)(2,1)S(1)}, u32[]{:S(2)}, u32[]{:S(2)}) collective-permute-start(bf16[256,2304]{1,0:T(8,128)(2,1)S(1)} %pad_maximum_fusion.7.rows_ref.refs_4_), channel_id=1, source_target_pairs={{0,1},{1,0},{2,3},{3,2},{4,5},{5,4},{6,7},{7,6},{8,9},{9,8},{10,11... | collective-permute-start | bytes 3538952 | tf_op jit(solution)/shard_map/ppermute | solution.py:586
  353.9 42.7 %collective-permute-start.44 = (bf16[2304,256]{1,0:T(8,128)(2,1)}, bf16[2304,256]{1,0:T(8,128)(2,1)S(1)}, u32[]{:S(2)}, u32[]{:S(2)}) collective-permute-start(bf16[2304,256]{1,0:T(8,128)(2,1)} %get-tuple-element.223), channel_id=1, source_target_pairs={{0,1},{1,0},{2,3},{3,2},{4,5},{5,4},{6,7},{7,6},{8,9},{9,8},{10,11... | collective-permute-start | bytes 3538952 | tf_op jit(solution)/shard_map/ppermute | solution.py:586
  425.8 242.5 %reduce-scatter.5.cloned.1.call-start = ((), (), s32[]{:S(2)}) async-start(), calls=%async_computation.6 | async-start | bytes 13271040 | tf_op jit(solution)/shard_map/reduce_scatter | solution.py:795
  427.9 18.7 %collective-permute-start.50 = (bf16[128,2304]{1,0:T(8,128)(2,1)S(1)}, bf16[128,2304]{1,0:T(8,128)(2,1)S(1)}, u32[]{:S(2)}, u32[]{:S(2)}) collective-permute-start(bf16[128,2304]{1,0:T(8,128)(2,1)S(1)} %get-tuple-element.238), channel_id=1, source_target_pairs={{0,8},{8,16},{16,24},{1,9},{9,17},{17,25},{2,10},{10,18},{18,26},{... | collective-permute-start | bytes 1769480 | tf_op jit(solution)/shard_map/ppermute | solution.py:533
  453.4 20.6 %collective-permute-start.52 = (bf16[128,2304]{1,0:T(8,128)(2,1)}, bf16[128,2304]{1,0:T(8,128)(2,1)}, u32[]{:S(2)}, u32[]{:S(2)}) collective-permute-start(bf16[128,2304]{1,0:T(8,128)(2,1)} %subtract_convert_fusion), channel_id=1, source_target_pairs={{0,8},{8,16},{16,24},{1,9},{9,17},{17,25},{2,10},{10,18},{18,26},{... | collective-permute-start | bytes 1769480 | tf_op jit(solution)/shard_map/ppermute | solution.py:484
  456.4 17.6 %collective-permute-start.53 = (bf16[128,2304]{1,0:T(8,128)(2,1)}, bf16[128,2304]{1,0:T(8,128)(2,1)}, u32[]{:S(2)}, u32[]{:S(2)}) collective-permute-start(bf16[128,2304]{1,0:T(8,128)(2,1)} %subtract_convert_fusion), channel_id=1, source_target_pairs={{8,0},{16,8},{24,16},{9,1},{17,9},{25,17},{10,2},{18,10},{26,18},{... | collective-permute-start | bytes 1769480 | tf_op jit(solution)/shard_map/ppermute | solution.py:485
  541.5 24.3 %collective-permute-start.61 = (bf16[512,512]{1,0:T(8,128)(2,1)}, bf16[512,512]{1,0:T(8,128)(2,1)}, u32[]{:S(2)}, u32[]{:S(2)}) collective-permute-start(bf16[512,512]{1,0:T(8,128)(2,1)} %pad_maximum_fusion.16), channel_id=1, source_target_pairs={{0,4},{2,6},{4,0},{6,2},{1,5},{3,7},{5,1},{7,3},{8,12},{10,14},{12... | collective-permute-start | bytes 1572872 | tf_op jit(solution)/shard_map/ppermute | solution.py:542
  543.1 24.1 %collective-permute-start.59 = (bf16[512,512]{1,0:T(8,128)(2,1)}, bf16[512,512]{1,0:T(8,128)(2,1)S(1)}, u32[]{:S(2)}, u32[]{:S(2)}) collective-permute-start(bf16[512,512]{1,0:T(8,128)(2,1)} %pad_maximum_fusion.15), channel_id=1, source_target_pairs={{0,2},{2,0},{4,6},{6,4},{1,3},{3,1},{5,7},{7,5},{8,10},{10,8},{12,... | collective-permute-start | bytes 1572872 | tf_op jit(solution)/shard_map/ppermute | solution.py:542
  613.9 17.9 %collective-permute-start.70 = (bf16[96,2304]{1,0:T(8,128)(2,1)}, bf16[96,2304]{1,0:T(8,128)(2,1)}, u32[]{:S(2)}, u32[]{:S(2)}) collective-permute-start(bf16[96,2304]{1,0:T(8,128)(2,1)} %get-tuple-element.344), channel_id=1, source_target_pairs={{0,4},{2,6},{4,0},{6,2},{1,5},{3,7},{5,1},{7,3},{8,12},{10,14},{12... | collective-permute-start | bytes 1327112 | tf_op jit(solution)/shard_map/ppermute | solution.py:542
  621.8 19.4 %collective-permute-start.68 = (bf16[128,2304]{1,0:T(8,128)(2,1)S(1)}, bf16[128,2304]{1,0:T(8,128)(2,1)}, u32[]{:S(2)}, u32[]{:S(2)}) collective-permute-start(bf16[128,2304]{1,0:T(8,128)(2,1)S(1)} %get-tuple-element.296), channel_id=1, source_target_pairs={{0,8},{8,16},{16,24},{1,9},{9,17},{17,25},{2,10},{10,18},{18,26},{... | collective-permute-start | bytes 1769480 | tf_op jit(solution)/shard_map/ppermute | solution.py:533
  646.2 26.6 %collective-permute-start.72 = (bf16[192,2304]{1,0:T(8,128)(2,1)}, bf16[192,2304]{1,0:T(8,128)(2,1)}, u32[]{:S(2)}, u32[]{:S(2)}) collective-permute-start(bf16[192,2304]{1,0:T(8,128)(2,1)} %pad_maximum_fusion.12), channel_id=1, source_target_pairs={{0,2},{2,0},{4,6},{6,4},{1,3},{3,1},{5,7},{7,5},{8,10},{10,8},{12,... | collective-permute-start | bytes 2654216 | tf_op jit(solution)/shard_map/ppermute | solution.py:542
  646.8 26.0 %collective-permute-start.73 = (bf16[192,2304]{1,0:T(8,128)(2,1)}, bf16[192,2304]{1,0:T(8,128)(2,1)}, u32[]{:S(2)}, u32[]{:S(2)}) collective-permute-start(bf16[192,2304]{1,0:T(8,128)(2,1)} %pad_maximum_fusion.13), channel_id=1, source_target_pairs={{0,4},{2,6},{4,0},{6,2},{1,5},{3,7},{5,1},{7,3},{8,12},{10,14},{12... | collective-permute-start | bytes 2654216 | tf_op jit(solution)/shard_map/ppermute | solution.py:542
  648.6 18.2 %all-to-all-start = ((f32[32,1,288]{2,1,0:T(1,128)}), f32[32,1,288]{2,1,0:T(1,128)}, u32[]{:S(2)}, u32[]{:S(2)}) async-start(f32[32,1,288]{2,1,0:T(1,128)} %copy.41), calls=%async_computation.2 | async-start | bytes 98304 | tf_op jit(solution)/shard_map/all_to_all | solution.py:884
  (133 other events, 1527.3 us)
Sparse Core Ops, SparseCore 0:
  10.5 51.5 all-gather.8
  64.5 122.7 all-gather.4
  189.2 63.8 all-gather.6
  425.9 64.7 reduce-scatter.2
  493.6 121.4 reduce-scatter.4

commit v3 on v2

--- a/solution.py
+++ b/solution.py
@@ -479,62 +479,52 @@
     return ()
 
 
-def line_gather(block, work, while_first=nothing, while_last=nothing):
-    place = lax.axis_index("line")
-    up = lax.ppermute(block, "line", [(0, 1), (1, 2), (2, 3)])
-    down = lax.ppermute(block, "line", [(1, 0), (2, 1), (3, 2)])
+def shift(value, step):
+    count = lax.axis_size("line")
+    return lax.ppermute(value, "line", [(at, (at + step) % count) for at in range(count)])
+
+
+def line_gather(block, work, while_first=nothing):
+    half = block.shape[0] // 2
+    up, down = shift(block, 1), shift(block, -1)
     done = while_first(lambda value: tie(value, block))
     up, down, done_first = lax.optimization_barrier((up, down, done))
-    up_two = lax.ppermute(up, "line", [(1, 2), (2, 3)])
-    down_two = lax.ppermute(down, "line", [(1, 0), (2, 1)])
-    first = work(0, jnp.concatenate([block, choose(place >= 1, up, down)], axis=0))
-    up_two, down_two = tie((up_two, down_two), first)
-    up_three = lax.ppermute(up_two, "line", [(2, 3)])
-    down_three = lax.ppermute(down_two, "line", [(1, 0)])
-    done = while_last(lambda value: tie(value, up_two, down_two))
-    up_three, down_three, done_last = lax.optimization_barrier((up_three, down_three, done))
-    third = choose(place >= 2, up_two, down_two)
-    fourth = choose(place == 0, down_three, choose(place == 3, up_three, down))
-    second = work(1, jnp.concatenate([third, fourth], axis=0))
-    return first, second, done_first, done_last
+    far_low, far_high = shift(down[:half], -1), shift(up[half:], 1)
+    first = work(0, jnp.concatenate([block, up], axis=0))
+    far_low, far_high = tie((far_low, far_high), first)
+    second = work(1, jnp.concatenate([down, far_low, far_high], axis=0))
+    return first, second, done_first
 
 
 def line_order():
-    place = lax.axis_index("line")
-    return jnp.stack(
-        [
-            place,
-            choose(place >= 1, place - 1, 1),
-            lax.rem(place + 2, 4),
-            choose(place >= 1, lax.rem(place + 1, 4), 3),
-        ]
-    ).astype(jnp.int32)
-
-
-def line_scatter(late, work, while_second=nothing, while_last=nothing):
-    place = lax.axis_index("line")
+    turns = jnp.array([0, 3, 1, 2], jnp.int32)
+    return lax.rem(lax.axis_index("line").astype(jnp.int32) + turns, 4)
+
+
+def line_scatter(late, work, while_last=nothing):
     rows = late.shape[0] // 2
-    third, fourth = late[:rows], late[rows:]
-    low_fourth = fourth.astype(LOW)
-    up = lax.ppermute(low_fourth, "line", [(0, 1)])
-    down = lax.ppermute(low_fourth, "line", [(3, 2)])
-    up, down, (early, done_first) = lax.optimization_barrier((up, down, work()))
-    own, second = early[:rows], early[rows:]
-    up = (third + up.astype(WIDE)).astype(LOW)
-    down = (third + down.astype(WIDE)).astype(LOW)
-    sent_up, sent_down = lax.optimization_barrier((up, down))
-    up = lax.ppermute(sent_up, "line", [(0, 1), (1, 2)])
-    down = lax.ppermute(sent_down, "line", [(3, 2), (2, 1)])
-    done = while_second(lambda value: tie(value, sent_up, sent_down), done_first)
-    up, down, done_second = lax.optimization_barrier((up, down, done))
-    up = (choose(place == 0, second, fourth) + up.astype(WIDE)).astype(LOW)
-    down = (second + down.astype(WIDE)).astype(LOW)
-    sent_up, sent_down = lax.optimization_barrier((up, down))
-    up = lax.ppermute(sent_up, "line", [(0, 1), (1, 2), (2, 3)])
-    down = lax.ppermute(sent_down, "line", [(3, 2), (2, 1), (1, 0)])
-    done = while_last(lambda value: tie(value, sent_up, sent_down), done_second)
-    up, down, done_last = lax.optimization_barrier((up, down, done))
-    return own + up.astype(WIDE) + down.astype(WIDE), done_first, done_second, done_last
+    half = rows // 2
+    following, far = late[:rows], late[rows:]
+    low_far = far.astype(LOW)
+    for_following, for_former = shift(low_far[:half], 1), shift(low_far[half:], -1)
+    for_following, for_former, (early, done_first) = lax.optimization_barrier(
+        (for_following, for_former, work())
+    )
+    own, former = early[:rows], early[rows:]
+    sends = lax.optimization_barrier(
+        (
+            jnp.concatenate(
+                [following[:half] + for_following.astype(WIDE), following[half:]], axis=0
+            ).astype(LOW),
+            jnp.concatenate(
+                [former[:half], former[half:] + for_former.astype(WIDE)], axis=0
+            ).astype(LOW),
+        )
+    )
+    terms = shift(sends[0], 1), shift(sends[1], -1)
+    done = while_last(lambda value: tie(value, *sends), done_first)
+    terms, done_last = lax.optimization_barrier((terms, done))
+    return own + sum(term.astype(WIDE) for term in terms), done_first, done_last
 
 
 def swap(value, bits):
@@ -653,6 +643,8 @@
     positions = [places(plane_place[None], c) for c in chunks]
     key_positions = jnp.concatenate([places(members, c) for c in chunks])
     tables = [rope_tables(positions[c]) for c in chunks]
+    key_column = key_positions[:, None]
+    tables, key_column = lax.optimization_barrier((tables, key_column))
     scales = norm_scales.astype(WIDE)
 
     tokens_own = tokens[0]
@@ -691,8 +683,8 @@
     def reorder(gate, _):
         return packed(gate(attn_flat))
 
-    branch_out, _, projection, _ = line_scatter(
-        attend(1), lambda: (attend(0), ()), while_second=reorder
+    branch_out, _, projection = line_scatter(
+        attend(1), lambda: (attend(0), ()), while_last=reorder
     )
 
     inputs = tokens_own.astype(WIDE)
@@ -710,17 +702,16 @@
 
     line_gather((hidden * inverse_three * scales[2]).astype(LOW), widen)
 
-    def keep_mixed(gate, _):
-        return [sibling(gate(part)) for part in mixed_away]
-
-    def keep_second(gate, _):
-        return [sibling(gate(part)) for part in normed_second]
-
-    ffn_out, _, mixed_theirs, second_theirs = line_scatter(
+    def keep(gate, _):
+        return (
+            [sibling(gate(part)) for part in mixed_away],
+            [sibling(gate(part)) for part in normed_second],
+        )
+
+    ffn_out, _, (mixed_theirs, second_theirs) = line_scatter(
         contract(mixed[1], down_all, 0, 0),
         lambda: (contract(mixed[0], down_all, 0, 0), ()),
-        while_second=keep_mixed,
-        while_last=keep_second,
+        while_last=keep,
     )
 
     inverse_four = inverse_root(ffn_out)
@@ -739,24 +730,28 @@
 
     line_gather(ffn_grad.astype(LOW), narrow_back)
 
-    def give_rows():
-        theirs = [sibling(part) for part in pair_away], [sibling(part) for part in ffn_grad_low]
-        return contract(pair_grad[0], paired_all, 0, 0), theirs
-
-    def give_down(gate, theirs):
-        return weight_grad_call(
-            [gate(part) for part in mixed], mixed_theirs, ffn_grad_low + theirs[1], core_ref
-        )
-
-    second_grad, (pair_theirs, _), down_grad, _ = line_scatter(
-        contract(pair_grad[1], paired_all, 0, 0), give_rows, while_second=give_down
-    )
-    down_share = lax.psum_scatter(down_grad, "plane", scatter_dimension=0, tiled=True)
-
-    def give_paired(gate):
+    pair_theirs = [sibling(part) for part in pair_away]
+    grad_theirs = [sibling(part) for part in ffn_grad_low]
+    second_part = contract(jnp.concatenate(pair_grad, axis=1), paired_all, 0, 0)
+
+    def give_down():
+        return second_part[:span], weight_grad_call(
+            [tie(part, second_part) for part in mixed],
+            mixed_theirs,
+            ffn_grad_low + grad_theirs,
+            core_ref,
+        )
+
+    def give_paired(gate, _):
         return weight_grad_call(
             [gate(part) for part in pair_grad], pair_theirs, normed_second + second_theirs, core_ref
         )
+
+    second_grad, down_grad, paired_grad = line_scatter(
+        second_part[span:], give_down, while_last=give_paired
+    )
+    down_share = lax.psum_scatter(down_grad, "plane", scatter_dimension=0, tiled=True)
+    paired_share = lax.psum_scatter(paired_grad, "plane", scatter_dimension=0, tiled=True)
 
     hidden_part = norm_back(hidden, inverse_three, scales[2], second_grad)
     hidden_grad = upstream + hidden_part
@@ -774,7 +769,7 @@
             pair_all,
             inverse_sums[c],
             positions[c][None, :],
-            key_positions[:, None],
+            key_column,
             *tables[c],
             prior[0],
             group_size,
@@ -787,12 +782,9 @@
             jnp.sum(second_grad * gate(hidden) * inverse_three, axis=0),
             jnp.sum(upstream * gate(ffn_out) * inverse_four, axis=0),
         ]
-        return jnp.stack(sums, axis=0), down_share.astype(WIDE)
-
-    _, _, paired_grad, (scale_three, down_share) = line_gather(
-        branch_grad.astype(LOW), attend_back, while_first=give_paired, while_last=give_three
-    )
-    paired_share = lax.psum_scatter(paired_grad, "plane", scatter_dimension=0, tiled=True)
+        return jnp.stack(sums, axis=0)
+
+    _, _, scale_three = line_gather(branch_grad.astype(LOW), attend_back, while_first=give_three)
 
     per_chunk = plane_count * span
     both_grads = jnp.concatenate(
@@ -844,7 +836,7 @@
         )
         return early, parts
 
-    def give_total(gate, parts):
+    def give_far(gate, parts):
         near, away = parts
         total = jnp.concatenate(
             [
@@ -857,10 +849,6 @@
         for c in chunks:
             wide_line = gate(tokens_line[c]).astype(WIDE)
             scale_one += jnp.sum(first_part[c] * (wide_line * inverse_root(wide_line)), axis=0)
-        return total, scale_one
-
-    def give_far(gate, held):
-        total, scale_one = held
         scale_grads = jnp.concatenate([scale_one[None], scale_three], axis=0)
         scale_cut = (
             scale_grads.reshape(4, all_count, -1).transpose(1, 0, 2).reshape(all_count, -1)
@@ -869,8 +857,8 @@
             return scale_cut, plane_scatter_far(total)
         return scale_cut, total
 
-    first_grad, _, _, (scale_cut, attn_sends) = line_scatter(
-        project_back(1), give_projection, while_second=give_total, while_last=give_far
+    first_grad, _, (scale_cut, attn_sends) = line_scatter(
+        project_back(1), give_projection, while_last=give_far
     )
     if plane_count == 4:
         own, send_one, send_two = attn_sends
@@ -882,9 +870,11 @@
     input_grad = hidden_grad + input_part
 
     scale_cut = lax.all_to_all(scale_cut, EVERY, 0, 0, tiled=True)
-    scale_share = jnp.sum(scale_cut, axis=0).reshape(4, -1)
     gate_share = paired_share[:ff_local].T.astype(WIDE)
     up_share = paired_share[ff_local:].T.astype(WIDE)
+    down_share = down_share.astype(WIDE)
+    scale_cut = tie(scale_cut, gate_share, up_share, down_share)
+    scale_share = jnp.sum(scale_cut, axis=0).reshape(4, -1)
     one, two = tie((one, two), input_grad, gate_share, up_share, scale_share)
     attn_share = own + one.astype(WIDE) + two.astype(WIDE)
 

time: 694 us -> 648 us (0.934)
  starting transfers between devices: 120 us -> 79.9 us
  local copies, waits for them, and re-layouts: 35.6 us -> 46.2 us
  matrix products: 41.4 us -> 31.7 us
  other arithmetic: 68.2 us -> 60.3 us
    ppermute x48 -> x32, starting transfers between devices: 97.7 us -> 56.9 us  [shift(): lax.ppermute(value, 'line', [(at, (at + step) % count) for at in range(co...]
    ppermute x16, waiting for transfers between devices: 46 us -> 60 us  [swap(): return lax.ppermute(value, 'plane', [(b, b ^ bits) for b in range(count)])]
    ppermute x48 -> x32, waiting for transfers between devices: 186 us -> 175 us  [shift(): lax.ppermute(value, 'line', [(at, (at + step) % count) for at in range(co...]
    all_to_all x1, waiting for transfers between devices: 10.3 us -> 0.01 us  [shards(): scale_cut = lax.all_to_all(scale_cut, EVERY, 0, 0, tiled=True)]
    dot_general x8 -> x7, matrix products: 41.4 us -> 31.7 us  [contract(): lax.dot_general(left, right, (((left_dim,), (right_dim,)), ((), ())), pre...]
    convert_element_type x9 -> x1, other arithmetic: 11.7 us -> 3 us  [shards(): down_share = down_share.astype(WIDE)]
    unnamed x163 -> x166, local copies, waits for them, and re-layouts: 11.1 us -> 19.5 us
    another operation x4 -> x13, other arithmetic: 2.94 us -> 9.92 us
  transfers between devices with their start and end apart: 80 -> 64, of which waited for: 37 -> 36; matrix products, arithmetic and copies ran while one was open for 17% -> 17% of each run, Pallas kernels for 21% -> 22%
where the time goes in v3:
time: 648 us; the launch traced here: 638 us
  waiting for transfers between devices  265 us (41%)
  Pallas kernels  140 us (22%)
  starting transfers between devices  79.9 us (12%)
  other arithmetic  60.3 us (9%)
  local copies, waits for them, and re-layouts  46.2 us (7%)
  matrix products  31.7 us (5%)
  between operations  15.2 us (2%)
    ppermute x32, waiting for transfers between devices, shift(): lax.ppermute(value, 'line', [(at, (at + step) % count) for at in range(co...  175 us
    ppermute x16, waiting for transfers between devices, swap(): return lax.ppermute(value, 'plane', [(b, b ^ bits) for b in range(count)])  60 us
    ppermute x32, starting transfers between devices, shift(): lax.ppermute(value, 'line', [(at, (at + step) % count) for at in range(co...  56.9 us
    dot_general x7, matrix products, contract(): lax.dot_general(left, right, (((left_dim,), (right_dim,)), ((), ())), pre...  31.7 us
    pallas_call x2, Pallas kernels, weight_grad_call(): pl.pallas_call(weight_grad_kernel, grid_spec=pltpu.PrefetchScalarGridSpec...  26.7 us
    pallas_call x2, Pallas kernels, widen_call(): pl.pallas_call(functools.partial(widen_kernel, sharers // STEPS), grid_sp...  26.2 us
    all_gather x1, waiting for transfers between devices, shards(): lax.all_gather(down_weight, ('fsdp', 'plane'), axis=0, tiled=True)  23.6 us
    pallas_call x2, Pallas kernels, attend_back_call(): pl.pallas_call(attend_back_kernel, grid=(keys // block, group_size), in_s...  20.5 us
  transfers between devices with their start and end apart: 64, of which 36 were waited for; matrix products, arithmetic and copies ran while one was open for 17% of the time, Pallas kernels for 22%

profile of v3, /device:TPU:0, one launch (start us, length us, event | category | flops | bytes accessed | tf_op | source)
XLA Modules:
  0.0 638.3 jit_solution(11189725618131482022)
XLA Ops:
  22.4 10.1 %collective-permute-done = bf16[128,2304]{1,0:T(8,128)(2,1)S(1)} collective-permute-done((bf16[128,2304]{1,0:T(8,128)(2,1)S(1)}, bf16[128,2304]{1,0:T(8,128)(2,1)S(1)}, u32[]{:S(2)}, u32[]{:S(2)}) %collective-permute-start) | collective-permute-done | bytes 589856 | tf_op jit(solution)/shard_map/ppermute | solution.py:484
  32.5 11.2 %collective-permute-done.1 = bf16[128,2304]{1,0:T(8,128)(2,1)S(1)} collective-permute-done((bf16[128,2304]{1,0:T(8,128)(2,1)S(1)}, bf16[128,2304]{1,0:T(8,128)(2,1)S(1)}, u32[]{:S(2)}, u32[]{:S(2)}) %collective-permute-start.1) | collective-permute-done | bytes 589856 | tf_op jit(solution)/shard_map/ppermute | solution.py:484
  137.3 11.3 %collective-permute-done.14 = bf16[128,2304]{1,0:T(8,128)(2,1)S(1)} collective-permute-done((bf16[128,2304]{1,0:T(8,128)(2,1)S(1)}, bf16[128,2304]{1,0:T(8,128)(2,1)S(1)}, u32[]{:S(2)}, u32[]{:S(2)}) %collective-permute-start.14) | collective-permute-done | bytes 589856 | tf_op jit(solution)/shard_map/ppermute | solution.py:484
  148.6 10.7 %collective-permute-done.15 = bf16[128,2304]{1,0:T(8,128)(2,1)S(1)} collective-permute-done((bf16[128,2304]{1,0:T(8,128)(2,1)S(1)}, bf16[128,2304]{1,0:T(8,128)(2,1)S(1)}, u32[]{:S(2)}, u32[]{:S(2)}) %collective-permute-start.15) | collective-permute-done | bytes 589856 | tf_op jit(solution)/shard_map/ppermute | solution.py:484
  165.3 14.3 %collective-permute-done.16 = bf16[128,2304]{1,0:T(8,128)(2,1)} collective-permute-done((bf16[128,2304]{1,0:T(8,128)(2,1)S(1)}, bf16[128,2304]{1,0:T(8,128)(2,1)}, u32[]{:S(2)}, u32[]{:S(2)}) %collective-permute-start.16) | collective-permute-done | bytes 589856 | tf_op jit(solution)/shard_map/ppermute | solution.py:484
  179.6 10.1 %collective-permute-done.17 = bf16[128,2304]{1,0:T(8,128)(2,1)S(1)} collective-permute-done((bf16[128,2304]{1,0:T(8,128)(2,1)S(1)}, bf16[128,2304]{1,0:T(8,128)(2,1)S(1)}, u32[]{:S(2)}, u32[]{:S(2)}) %collective-permute-start.17) | collective-permute-done | bytes 589856 | tf_op jit(solution)/shard_map/ppermute | solution.py:484
  197.8 13.0 %shard_map.199 = (bf16[2304,256]{1,0:T(8,128)(2,1)}, bf16[1152,256]{1,0:T(8,128)(2,1)}, f32[2304,256]{1,0:T(8,128)}, f32[2304,256]{1,0:T(8,128)}) custom-call(s32[1]{0:T(128)} %bitcast.19.core_ref, bf16[256,2304]{1,0:T(8,128)(2,1)} %pad_maximum_fusion.4.rows_ref.refs_4_, bf16[4608,2304]{1,0:T(8,128)(2,1)} %all-gather.5.cloned.1.call-done.weight_ref), custom_call_target="tpu_custom_call" | custom-call | bytes 67108864 | tf_op jit(solution)/shard_map/pallas_call | solution.py:329
  213.8 13.2 %shard_map.200 = (bf16[2304,256]{1,0:T(8,128)(2,1)}, bf16[1152,256]{1,0:T(8,128)(2,1)}, f32[2304,256]{1,0:T(8,128)}, f32[2304,256]{1,0:T(8,128)}) custom-call(s32[1]{0:T(128)} %bitcast.19.core_ref, bf16[256,2304]{1,0:T(8,128)(2,1)} %copy-done.19, bf16[4608,2304]{1,0:T(8,128)(2,1)} %all-gather.5.cloned.1.call-done.weight_ref), custom_call_target="tpu_custom_call" | custom-call | bytes 67108864 | tf_op jit(solution)/shard_map/pallas_call | solution.py:329
  227.0 23.6 %all-gather.7.cloned.1.call-done.weight_ref = bf16[2304,2304]{1,0:T(8,128)(2,1)} async-done(((bf16[288,2304]{1,0:T(8,128)(2,1)}), bf16[2304,2304]{1,0:T(8,128)(2,1)}) %all-gather.7.cloned.1.call-update) | async-done | bytes 10616848 | tf_op jit(solution)/shard_map/all_gather | solution.py:620
  282.2 12.1 %collective-permute-done.22 = bf16[128,2304]{1,0:T(8,128)(2,1)S(1)} collective-permute-done((bf16[128,2304]{1,0:T(8,128)(2,1)S(1)}, bf16[128,2304]{1,0:T(8,128)(2,1)S(1)}, u32[]{:S(2)}, u32[]{:S(2)}) %collective-permute-start.22) | collective-permute-done | bytes 589856 | tf_op jit(solution)/shard_map/ppermute | solution.py:484
  294.3 11.8 %collective-permute-done.23 = bf16[128,2304]{1,0:T(8,128)(2,1)S(1)} collective-permute-done((bf16[128,2304]{1,0:T(8,128)(2,1)S(1)}, bf16[128,2304]{1,0:T(8,128)(2,1)S(1)}, u32[]{:S(2)}, u32[]{:S(2)}) %collective-permute-start.23) | collective-permute-done | bytes 589856 | tf_op jit(solution)/shard_map/ppermute | solution.py:484
  313.9 14.2 %collective-permute-done.28 = bf16[128,2304]{1,0:T(8,128)(2,1)S(1)} collective-permute-done((bf16[128,2304]{1,0:T(8,128)(2,1)S(1)}, bf16[128,2304]{1,0:T(8,128)(2,1)S(1)}, u32[]{:S(2)}, u32[]{:S(2)}) %collective-permute-start.28) | collective-permute-done | bytes 589856 | tf_op jit(solution)/shard_map/ppermute | solution.py:484
  328.1 10.2 %collective-permute-done.29 = bf16[128,2304]{1,0:T(8,128)(2,1)S(1)} collective-permute-done((bf16[128,2304]{1,0:T(8,128)(2,1)S(1)}, bf16[128,2304]{1,0:T(8,128)(2,1)S(1)}, u32[]{:S(2)}, u32[]{:S(2)}) %collective-permute-start.29) | collective-permute-done | bytes 589856 | tf_op jit(solution)/shard_map/ppermute | solution.py:484
  340.8 9.2 %shard_map.201 = (bf16[4608,256]{1,0:T(8,128)(2,1)}, bf16[2304,256]{1,0:T(8,128)(2,1)}) custom-call(s32[1]{0:T(128)} %bitcast.19.core_ref, bf16[256,2304]{1,0:T(8,128)(2,1)} %copy-done.11, bf16[2304,2304]{1,0:T(8,128)(2,1)} %all-gather.7.cloned.1.call-done.weight_ref, f32[2304,256]{1,0:T(8,128)} %get-tuple-element.179.bent_ref, ...), custom_call_target="tpu_custom_call" | custom-call | bytes 67108864 | tf_op jit(solution)/shard_map/pallas_call | solution.py:373
  355.5 9.3 %shard_map.202 = (bf16[4608,256]{1,0:T(8,128)(2,1)}, bf16[2304,256]{1,0:T(8,128)(2,1)}) custom-call(s32[1]{0:T(128)} %bitcast.19.core_ref, bf16[256,2304]{1,0:T(8,128)(2,1)} %copy-done.21, bf16[2304,2304]{1,0:T(8,128)(2,1)} %all-gather.7.cloned.1.call-done.weight_ref, f32[2304,256]{1,0:T(8,128)} %get-tuple-element.185.bent_ref, ...), custom_call_target="tpu_custom_call" | custom-call | bytes 67108864 | tf_op jit(solution)/shard_map/pallas_call | solution.py:373
  364.8 15.5 %fusion.54 = (bf16[512,2304]{1,0:T(8,128)(2,1)S(1)}, f32[512,2304]{1,0:T(8,128)S(1)}) fusion(bf16[4608,2304]{1,0:T(8,128)(2,1)} %all-gather.5.cloned.1.call-done.weight_ref, bf16[4608,256]{1,0:T(8,128)(2,1)} %get-tuple-element.198.refs_1_, bf16[4608,256]{1,0:T(8,128)(2,1)S(1)} %copy-done.30), kind=kOutput, calls=%fused_computation.215 | convolution fusion | flops 10882252800 | bytes 33030144 | tf_op jit(solution)/shard_map/dot_general | solution.py:25
  385.9 10.1 %shard_map.203 = bf16[1152,2304]{1,0:T(8,128)(2,1)} custom-call(s32[1]{0:T(128)} %bitcast.19.core_ref, bf16[2304,256]{1,0:T(8,128)(2,1)} %get-tuple-element.188.refs_0_, bf16[2304,256]{1,0:T(8,128)(2,1)} %get-tuple-element.189.refs_1_, bf16[1152,256]{1,0:T(8,128)(2,1)} %copy-done.47, bf16[1152,256]{1,0:T(8,128)(2,1)} %collective-permute-done.25.refs_3_, ...), custom_call_target="tpu_custom_call" | custom-call | bytes 67108864 | tf_op jit(solution)/shard_map/pallas_call | solution.py:414
  407.7 16.6 %shard_map.204 = bf16[2304,2304]{1,0:T(8,128)(2,1)} custom-call(s32[1]{0:T(128)} %bitcast.19.core_ref, bf16[4608,256]{1,0:T(8,128)(2,1)} %get-tuple-element.197.refs_0_, bf16[4608,256]{1,0:T(8,128)(2,1)} %get-tuple-element.198.refs_1_, bf16[2304,256]{1,0:T(8,128)(2,1)} %copy-done.44, bf16[2304,256]{1,0:T(8,128)(2,1)} %copy-done.45, ...), custom_call_target="tpu_custom_call" | custom-call | bytes 67108864 | tf_op jit(solution)/shard_map/pallas_call | solution.py:414
  443.9 11.4 %collective-permute-done.40 = bf16[128,2304]{1,0:T(8,128)(2,1)S(1)} collective-permute-done((bf16[128,2304]{1,0:T(8,128)(2,1)S(1)}, bf16[128,2304]{1,0:T(8,128)(2,1)S(1)}, u32[]{:S(2)}, u32[]{:S(2)}) %collective-permute-start.40) | collective-permute-done | bytes 589856 | tf_op jit(solution)/shard_map/ppermute | solution.py:484
  455.3 10.7 %collective-permute-done.41 = bf16[128,2304]{1,0:T(8,128)(2,1)S(1)} collective-permute-done((bf16[128,2304]{1,0:T(8,128)(2,1)S(1)}, bf16[128,2304]{1,0:T(8,128)(2,1)S(1)}, u32[]{:S(2)}, u32[]{:S(2)}) %collective-permute-start.41) | collective-permute-done | bytes 589856 | tf_op jit(solution)/shard_map/ppermute | solution.py:484
  471.0 9.8 %shard_map.205 = (bf16[256,512]{1,0:T(8,128)(2,1)}, f32[2048,512]{1,0:T(8,128)}) custom-call(bf16[512,256]{1,0:T(8,128)(2,1)} %get-tuple-element.149.query_ref.refs_0_, bf16[256,512]{1,0:T(8,128)(2,1)} %convolution_convert_fusion.1.refs_1_, f32[256,512]{1,0:T(8,128)} %get-tuple-element.210.refs_2_, bf16[2048,512]{1,0:T(8,128)(2,1)} %copy-done, ...), custom_call_target="tpu_custom_call" | custom-call | bytes 67108864 | tf_op jit(solution)/shard_map/pallas_call | solution.py:224
  483.7 10.7 %shard_map.206 = (bf16[256,512]{1,0:T(8,128)(2,1)}, bf16[2048,512]{1,0:T(8,128)(2,1)}) custom-call(bf16[512,256]{1,0:T(8,128)(2,1)} %get-tuple-element.142.query_ref.refs_0_, bf16[256,512]{1,0:T(8,128)(2,1)} %convolution_convert_fusion.refs_1_, f32[256,512]{1,0:T(8,128)} %get-tuple-element.217.refs_2_, bf16[2048,512]{1,0:T(8,128)(2,1)} %copy-done, ...), custom_call_target="tpu_custom_call" | custom-call | bytes 67108864 | tf_op jit(solution)/shard_map/pallas_call | solution.py:224
  498.7 11.2 %collective-permute-done.44 = bf16[256,512]{1,0:T(8,128)(2,1)S(1)} collective-permute-done((bf16[256,512]{1,0:T(8,128)(2,1)S(1)}, bf16[256,512]{1,0:T(8,128)(2,1)S(1)}, u32[]{:S(2)}, u32[]{:S(2)}) %collective-permute-start.44) | collective-permute-done | bytes 262176 | tf_op jit(solution)/shard_map/ppermute | solution.py:532
  520.3 15.7 %collective-permute-done.47 = bf16[512,512]{1,0:T(8,128)(2,1)S(1)} collective-permute-done((bf16[512,512]{1,0:T(8,128)(2,1)S(1)}, bf16[512,512]{1,0:T(8,128)(2,1)S(1)}, u32[]{:S(2)}, u32[]{:S(2)}) %collective-permute-start.47) | collective-permute-done | bytes 524320 | tf_op jit(solution)/shard_map/ppermute | solution.py:532
  (440 shorter events, 327.0 us)
Async XLA Ops:
  7.2 55.0 %all-gather.9.cloned.1.call-start = ((), (), s32[]{:S(2)}) async-start(), calls=%async_computation.7 | async-start | bytes 7962624 | tf_op jit(solution)/shard_map/all_gather | solution.py:615
  9.4 188.3 %all-gather.5.cloned.1.call-start = ((), (), s32[]{:S(2)}) async-start(), calls=%async_computation.3 | async-start | bytes 23887872 | tf_op jit(solution)/shard_map/all_gather | solution.py:619
  12.2 238.4 %all-gather.7.cloned.1.call-start = ((), (), s32[]{:S(2)}) async-start(), calls=%async_computation.4 | async-start | bytes 11943936 | tf_op jit(solution)/shard_map/all_gather | solution.py:620
  13.0 599.8 %reduce-scatter.5.cloned.1.call-start = ((), (), s32[]{:S(2)}) async-start(), calls=%async_computation.6 | async-start | bytes 6635520 | tf_op jit(solution)/shard_map/reduce_scatter | solution.py:753
  16.3 27.4 %collective-permute-start.1 = (bf16[128,2304]{1,0:T(8,128)(2,1)S(1)}, bf16[128,2304]{1,0:T(8,128)(2,1)S(1)}, u32[]{:S(2)}, u32[]{:S(2)}) collective-permute-start(bf16[128,2304]{1,0:T(8,128)(2,1)S(1)} %bitcast.114), channel_id=1, source_target_pairs={{0,24},{8,0},{16,8},{24,16},{1,25},{9,1},{17,9},{25,17},{2,26},{10... | collective-permute-start | bytes 1769480 | tf_op jit(solution)/shard_map/ppermute | solution.py:484
  131.9 27.4 %collective-permute-start.15 = (bf16[128,2304]{1,0:T(8,128)(2,1)S(1)}, bf16[128,2304]{1,0:T(8,128)(2,1)S(1)}, u32[]{:S(2)}, u32[]{:S(2)}) collective-permute-start(bf16[128,2304]{1,0:T(8,128)(2,1)S(1)} %pad_maximum_fusion.11), channel_id=1, source_target_pairs={{0,24},{8,0},{16,8},{24,16},{1,25},{9,1},{17,9},{25,17},{2,26},{10... | collective-permute-start | bytes 1769480 | tf_op jit(solution)/shard_map/ppermute | solution.py:484
  162.0 27.7 %collective-permute-start.17 = (bf16[128,2304]{1,0:T(8,128)(2,1)S(1)}, bf16[128,2304]{1,0:T(8,128)(2,1)S(1)}, u32[]{:S(2)}, u32[]{:S(2)}) collective-permute-start(bf16[128,2304]{1,0:T(8,128)(2,1)S(1)} %multiply_convert_fusion), channel_id=1, source_target_pairs={{0,24},{8,0},{16,8},{24,16},{1,25},{9,1},{17,9},{25,17},{2,26},{10... | collective-permute-start | bytes 1769480 | tf_op jit(solution)/shard_map/ppermute | solution.py:484
  190.5 20.3 %collective-permute-start.18 = (bf16[64,2304]{1,0:T(8,128)(2,1)}, bf16[64,2304]{1,0:T(8,128)(2,1)}, u32[]{:S(2)}, u32[]{:S(2)}) collective-permute-start(bf16[64,2304]{1,0:T(8,128)(2,1)} %slice.402), channel_id=1, source_target_pairs={{0,24},{8,0},{16,8},{24,16},{1,25},{9,1},{17,9},{25,17},{2,26},{10... | collective-permute-start | bytes 884744 | tf_op jit(solution)/shard_map/ppermute | solution.py:484
  275.4 30.7 %collective-permute-start.27 = (bf16[256,2304]{1,0:T(8,128)(2,1)S(1)}, bf16[256,2304]{1,0:T(8,128)(2,1)S(1)}, u32[]{:S(2)}, u32[]{:S(2)}) collective-permute-start(bf16[256,2304]{1,0:T(8,128)(2,1)S(1)} %copy-done.20), channel_id=1, source_target_pairs={{0,1},{1,0},{2,3},{3,2},{4,5},{5,4},{6,7},{7,6},{8,9},{9,8},{10,11... | collective-permute-start | bytes 3538952 | tf_op jit(solution)/shard_map/ppermute | solution.py:576
  275.9 30.2 %collective-permute-start.26 = (bf16[256,2304]{1,0:T(8,128)(2,1)S(1)}, bf16[256,2304]{1,0:T(8,128)(2,1)S(1)}, u32[]{:S(2)}, u32[]{:S(2)}) collective-permute-start(bf16[256,2304]{1,0:T(8,128)(2,1)S(1)} %copy-done.10), channel_id=1, source_target_pairs={{0,1},{1,0},{2,3},{3,2},{4,5},{5,4},{6,7},{7,6},{8,9},{9,8},{10,11... | collective-permute-start | bytes 3538952 | tf_op jit(solution)/shard_map/ppermute | solution.py:576
  280.1 26.0 %collective-permute-start.23 = (bf16[128,2304]{1,0:T(8,128)(2,1)S(1)}, bf16[128,2304]{1,0:T(8,128)(2,1)S(1)}, u32[]{:S(2)}, u32[]{:S(2)}) collective-permute-start(bf16[128,2304]{1,0:T(8,128)(2,1)S(1)} %pad_maximum_fusion.13), channel_id=1, source_target_pairs={{0,24},{8,0},{16,8},{24,16},{1,25},{9,1},{17,9},{25,17},{2,26},{10... | collective-permute-start | bytes 1769480 | tf_op jit(solution)/shard_map/ppermute | solution.py:484
  310.6 27.6 %collective-permute-start.29 = (bf16[128,2304]{1,0:T(8,128)(2,1)S(1)}, bf16[128,2304]{1,0:T(8,128)(2,1)S(1)}, u32[]{:S(2)}, u32[]{:S(2)}) collective-permute-start(bf16[128,2304]{1,0:T(8,128)(2,1)S(1)} %get-tuple-element.308), channel_id=1, source_target_pairs={{0,24},{8,0},{16,8},{24,16},{1,25},{9,1},{17,9},{25,17},{2,26},{10... | collective-permute-start | bytes 1769480 | tf_op jit(solution)/shard_map/ppermute | solution.py:484
  340.7 45.1 %collective-permute-start.34 = (bf16[256,2304]{1,0:T(8,128)(2,1)S(1)}, bf16[256,2304]{1,0:T(8,128)(2,1)}, u32[]{:S(2)}, u32[]{:S(2)}) collective-permute-start(bf16[256,2304]{1,0:T(8,128)(2,1)S(1)} %pad_maximum_fusion.5.rows_ref.refs_4_), channel_id=1, source_target_pairs={{0,1},{1,0},{2,3},{3,2},{4,5},{5,4},{6,7},{7,6},{8,9},{9,8},{10,11... | collective-permute-start | bytes 3538952 | tf_op jit(solution)/shard_map/ppermute | solution.py:576
  354.5 31.4 %collective-permute-start.35 = (bf16[256,2304]{1,0:T(8,128)(2,1)S(1)}, bf16[256,2304]{1,0:T(8,128)(2,1)}, u32[]{:S(2)}, u32[]{:S(2)}) collective-permute-start(bf16[256,2304]{1,0:T(8,128)(2,1)S(1)} %constant_dynamic-update-slice_fusion.16.rows_ref.refs_5_), channel_id=1, source_target_pairs={{0,1},{1,0},{2,3},{3,2},{4,5},{5,4},{6,7},{7,6},{8,9},{9,8},{10,11... | collective-permute-start | bytes 3538952 | tf_op jit(solution)/shard_map/ppermute | solution.py:576
  396.1 219.6 %reduce-scatter.3.cloned.1.call-start = ((), (), s32[]{:S(2)}) async-start(), calls=%async_computation.5 | async-start | bytes 13271040 | tf_op jit(solution)/shard_map/reduce_scatter | solution.py:754
  401.8 22.4 %collective-permute-start.36 = (bf16[128,2304]{1,0:T(8,128)(2,1)}, bf16[128,2304]{1,0:T(8,128)(2,1)S(1)}, u32[]{:S(2)}, u32[]{:S(2)}) collective-permute-start(bf16[128,2304]{1,0:T(8,128)(2,1)} %pad_maximum_fusion.14), channel_id=1, source_target_pairs={{0,8},{8,16},{16,24},{24,0},{1,9},{9,17},{17,25},{25,1},{2,10},{10... | collective-permute-start | bytes 1769480 | tf_op jit(solution)/shard_map/ppermute | solution.py:484
  402.5 28.0 %collective-permute-start.37 = (bf16[128,2304]{1,0:T(8,128)(2,1)}, bf16[128,2304]{1,0:T(8,128)(2,1)S(1)}, u32[]{:S(2)}, u32[]{:S(2)}) collective-permute-start(bf16[128,2304]{1,0:T(8,128)(2,1)} %pad_maximum_fusion.15), channel_id=1, source_target_pairs={{0,24},{8,0},{16,8},{24,16},{1,25},{9,1},{17,9},{25,17},{2,26},{10... | collective-permute-start | bytes 1769480 | tf_op jit(solution)/shard_map/ppermute | solution.py:484
  438.9 27.1 %collective-permute-start.41 = (bf16[128,2304]{1,0:T(8,128)(2,1)S(1)}, bf16[128,2304]{1,0:T(8,128)(2,1)S(1)}, u32[]{:S(2)}, u32[]{:S(2)}) collective-permute-start(bf16[128,2304]{1,0:T(8,128)(2,1)S(1)} %subtract_convert_fusion), channel_id=1, source_target_pairs={{0,24},{8,0},{16,8},{24,16},{1,25},{9,1},{17,9},{25,17},{2,26},{10... | collective-permute-start | bytes 1769480 | tf_op jit(solution)/shard_map/ppermute | solution.py:484
  511.1 24.8 %collective-permute-start.47 = (bf16[512,512]{1,0:T(8,128)(2,1)S(1)}, bf16[512,512]{1,0:T(8,128)(2,1)S(1)}, u32[]{:S(2)}, u32[]{:S(2)}) collective-permute-start(bf16[512,512]{1,0:T(8,128)(2,1)S(1)} %pad_maximum_fusion.20), channel_id=1, source_target_pairs={{0,4},{2,6},{4,0},{6,2},{1,5},{3,7},{5,1},{7,3},{8,12},{10,14},{12... | collective-permute-start | bytes 1572872 | tf_op jit(solution)/shard_map/ppermute | solution.py:532
  512.2 24.7 %collective-permute-start.45 = (bf16[512,512]{1,0:T(8,128)(2,1)S(1)}, bf16[512,512]{1,0:T(8,128)(2,1)S(1)}, u32[]{:S(2)}, u32[]{:S(2)}) collective-permute-start(bf16[512,512]{1,0:T(8,128)(2,1)S(1)} %pad_maximum_fusion.19), channel_id=1, source_target_pairs={{0,2},{2,0},{4,6},{6,4},{1,3},{3,1},{5,7},{7,5},{8,10},{10,8},{12,... | collective-permute-start | bytes 1572872 | tf_op jit(solution)/shard_map/ppermute | solution.py:532
  570.5 29.2 %collective-permute-start.50 = (bf16[128,2304]{1,0:T(8,128)(2,1)}, bf16[128,2304]{1,0:T(8,128)(2,1)}, u32[]{:S(2)}, u32[]{:S(2)}) collective-permute-start(bf16[128,2304]{1,0:T(8,128)(2,1)} %pad_maximum_fusion.16), channel_id=1, source_target_pairs={{0,8},{8,16},{16,24},{24,0},{1,9},{9,17},{17,25},{25,1},{2,10},{10... | collective-permute-start | bytes 1769480 | tf_op jit(solution)/shard_map/ppermute | solution.py:484
  570.8 28.8 %collective-permute-start.51 = (bf16[128,2304]{1,0:T(8,128)(2,1)}, bf16[128,2304]{1,0:T(8,128)(2,1)}, u32[]{:S(2)}, u32[]{:S(2)}) collective-permute-start(bf16[128,2304]{1,0:T(8,128)(2,1)} %pad_maximum_fusion.17), channel_id=1, source_target_pairs={{0,24},{8,0},{16,8},{24,16},{1,25},{9,1},{17,9},{25,17},{2,26},{10... | collective-permute-start | bytes 1769480 | tf_op jit(solution)/shard_map/ppermute | solution.py:484
  604.1 22.6 %collective-permute-start.56 = (bf16[192,2304]{1,0:T(8,128)(2,1)}, bf16[192,2304]{1,0:T(8,128)(2,1)}, u32[]{:S(2)}, u32[]{:S(2)}) collective-permute-start(bf16[192,2304]{1,0:T(8,128)(2,1)} %pad_maximum_fusion.8), channel_id=1, source_target_pairs={{0,2},{2,0},{4,6},{6,4},{1,3},{3,1},{5,7},{7,5},{8,10},{10,8},{12,... | collective-permute-start | bytes 2654216 | tf_op jit(solution)/shard_map/ppermute | solution.py:532
  605.9 22.1 %collective-permute-start.57 = (bf16[192,2304]{1,0:T(8,128)(2,1)}, bf16[192,2304]{1,0:T(8,128)(2,1)}, u32[]{:S(2)}, u32[]{:S(2)}) collective-permute-start(bf16[192,2304]{1,0:T(8,128)(2,1)} %pad_maximum_fusion.9), channel_id=1, source_target_pairs={{0,4},{2,6},{4,0},{6,2},{1,5},{3,7},{5,1},{7,3},{8,12},{10,14},{12... | collective-permute-start | bytes 2654216 | tf_op jit(solution)/shard_map/ppermute | solution.py:532
  (114 other events, 1172.5 us)
Sparse Core Ops, SparseCore 0:
  10.5 51.6 all-gather.8
  64.6 120.1 all-gather.4
  186.7 63.8 all-gather.6
  396.2 60.5 reduce-scatter.4
  459.7 121.4 reduce-scatter.2

commit v4 on v3

--- a/solution.py
+++ b/solution.py
@@ -159,7 +159,7 @@
 
 
 def attend_back_kernel(*refs):
-    query_ref, grad_ref, out_ref, pair_ref, inverse_ref, place_ref, key_place_ref = refs[:7]
+    query_ref, grad_ref, out_ref, pair_ref, inverse_ref, place_ref, base_ref = refs[:7]
     cos_ref, sin_ref, *prior_refs, query_grad_ref, pair_grad_ref, total_ref, held_ref = refs[7:]
     part, head = pl.program_id(0), pl.program_id(1)
     keys = pair_ref[:, :HEAD]
@@ -168,7 +168,13 @@
     grads = grad_ref[...]
     inner = as_row(jnp.sum(grads.astype(WIDE) * out_ref[...], axis=-1, keepdims=True))
     bounded = jnp.tanh(contract(keys, queries, 1, 1) * (1.0 / SOFT_CAP))
-    allowed = key_place_ref[...] <= place_ref[...]
+    blocks = base_ref.shape[0] // pl.num_programs(0)
+    rows = keys.shape[0] // blocks
+    offsets = lax.broadcasted_iota(jnp.int32, (rows, 1), 0)
+    key_places = jnp.concatenate(
+        [base_ref[part * blocks + block] + offsets for block in range(blocks)], axis=0
+    )
+    allowed = key_places <= place_ref[...]
     weights = jnp.where(allowed, jnp.exp(SOFT_CAP * bounded) * inverse_ref[...], 0.0)
     weight_grad = contract(values, grads, 1, 1)
     score_grad = (weights * (weight_grad - inner) * (1.0 - bounded * bounded)).astype(LOW)
@@ -211,7 +217,7 @@
 
 
 def attend_back_call(
-    queries, grads, out, pair, inverse, places_row, key_places_column, cosine, sine_table, prior, group_size
+    queries, grads, out, pair, inverse, places_row, key_bases, cosine, sine_table, prior, group_size
 ):
     count = queries.shape[0]
     span = count // group_size
@@ -231,7 +237,7 @@
             by_keys,
             pl.BlockSpec((1, span), lambda k, h: (0, h)),
             pl.BlockSpec((1, span), lambda k, h: (0, 0)),
-            pl.BlockSpec((block, 1), lambda k, h: (k, 0)),
+            pl.BlockSpec(memory_space=pltpu.SMEM),
             table,
             table,
         ]
@@ -247,11 +253,11 @@
         ],
         compiler_params=params(),
         cost_estimate=COST,
-    )(queries, grads, out, pair, inverse, places_row, key_places_column, cosine, sine_table, *extra)
+    )(queries, grads, out, pair, inverse, places_row, key_bases, cosine, sine_table, *extra)
 
 
 def project_back_kernel(
-    query_ref, own_ref, one_ref, two_ref, weight_ref, cos_ref, sin_ref, raw_ref, part_ref
+    query_ref, own_ref, one_ref, two_ref, weight_ref, cos_ref, sin_ref, raw_ref, part_ref, low_ref
 ):
     query_width = query_ref.shape[1]
     total = own_ref[...].astype(WIDE) + one_ref[...].astype(WIDE) + two_ref[...].astype(WIDE)
@@ -264,7 +270,9 @@
         second * cosine - first * sine_table
     ).astype(LOW)
     raw_ref[:, query_width + HEAD :] = total[:, HEAD:].astype(LOW)
-    part_ref[...] = contract(raw_ref[...], weight_ref[...], 1, 0)
+    part = contract(raw_ref[...], weight_ref[...], 1, 0)
+    part_ref[...] = part
+    low_ref[...] = part[part.shape[0] // 2 :].astype(LOW)
 
 
 def project_back_call(query_grad, own, one, two, weights, cosine, sine_table):
@@ -275,6 +283,7 @@
         out_shape=(
             jax.ShapeDtypeStruct((span, width), LOW),
             jax.ShapeDtypeStruct((span, model), WIDE),
+            jax.ShapeDtypeStruct((span // 2, model), LOW),
         ),
         compiler_params=params(),
         cost_estimate=COST,
@@ -396,12 +405,21 @@
 
 
 def weight_grad_kernel(core_ref, *refs):
-    *pairs, out_ref = refs
+    *pairs, out_ref, left_ref, right_ref = refs
     half = len(pairs) // 2
-    total = contract(pairs[0][...], pairs[half][...], 1, 0)
-    for left, right in zip(pairs[1:half], pairs[half + 1 :]):
-        total += contract(left[...], right[...], 1, 0)
-    out_ref[...] = total.astype(LOW)
+
+    @pl.when(pl.program_id(0) == 0)
+    def _():
+        first = 0
+        for part in pairs[half:]:
+            right_ref[first : first + part.shape[0]] = part[...]
+            first += part.shape[0]
+
+    first = 0
+    for part in pairs[:half]:
+        left_ref[:, first : first + part.shape[1]] = part[...]
+        first += part.shape[1]
+    out_ref[...] = contract(left_ref[...], right_ref[...], 1, 0).astype(LOW)
 
 
 def weight_grad_call(own, away, rows, core):
@@ -418,6 +436,10 @@
             grid=(STEPS,),
             in_specs=[mine] * len(own) + [theirs] * len(away) + [whole] * len(rows),
             out_specs=pl.BlockSpec((block, model), lambda j, core_ref: (j, 0)),
+            scratch_shapes=[
+                pltpu.VMEM((block, len(rows) * span), LOW),
+                pltpu.VMEM((len(rows) * span, model), LOW),
+            ],
         ),
         out_shape=jax.ShapeDtypeStruct((amount, model), LOW),
         compiler_params=params(),
@@ -501,11 +523,11 @@
     return lax.rem(lax.axis_index("line").astype(jnp.int32) + turns, 4)
 
 
-def line_scatter(late, work, while_last=nothing):
+def line_scatter(late, work, while_last=nothing, low_far=None):
     rows = late.shape[0] // 2
     half = rows // 2
     following, far = late[:rows], late[rows:]
-    low_far = far.astype(LOW)
+    low_far = far.astype(LOW) if low_far is None else low_far
     for_following, for_former = shift(low_far[:half], 1), shift(low_far[half:], -1)
     for_following, for_former, (early, done_first) = lax.optimization_barrier(
         (for_following, for_former, work())
@@ -643,8 +665,8 @@
     positions = [places(plane_place[None], c) for c in chunks]
     key_positions = jnp.concatenate([places(members, c) for c in chunks])
     tables = [rope_tables(positions[c]) for c in chunks]
-    key_column = key_positions[:, None]
-    tables, key_column = lax.optimization_barrier((tables, key_column))
+    key_bases = key_positions.reshape(-1, half_rows)[:, 0]
+    tables, key_bases = lax.optimization_barrier((tables, key_bases))
     scales = norm_scales.astype(WIDE)
 
     tokens_own = tokens[0]
@@ -769,7 +791,7 @@
             pair_all,
             inverse_sums[c],
             positions[c][None, :],
-            key_column,
+            key_bases,
             *tables[c],
             prior[0],
             group_size,
@@ -812,11 +834,11 @@
     )
     own_terms = tie(own_terms, output_near)
 
-    raw_low, first_part = [None] * 2, [None] * 2
+    raw_low, first_part, low_part = [None] * 2, [None] * 2, [None] * 2
 
     def project_back(c):
         terms = [term[c * span : (c + 1) * span] for term in own_terms]
-        raw_low[c], first_part[c] = project_back_call(
+        raw_low[c], first_part[c], low_part[c] = project_back_call(
             query_raw_low[c], *terms, projection, *tables[c]
         )
         return first_part[c]
@@ -858,7 +880,7 @@
         return scale_cut, total
 
     first_grad, _, (scale_cut, attn_sends) = line_scatter(
-        project_back(1), give_projection, while_last=give_far
+        project_back(1), give_projection, while_last=give_far, low_far=low_part[1]
     )
     if plane_count == 4:
         own, send_one, send_two = attn_sends
@@ -869,13 +891,13 @@
     input_part = norm_back(inputs, inverse_root(inputs), scales[0], first_grad)
     input_grad = hidden_grad + input_part
 
-    scale_cut = lax.all_to_all(scale_cut, EVERY, 0, 0, tiled=True)
     gate_share = paired_share[:ff_local].T.astype(WIDE)
     up_share = paired_share[ff_local:].T.astype(WIDE)
     down_share = down_share.astype(WIDE)
     scale_cut = tie(scale_cut, gate_share, up_share, down_share)
+    scale_cut = lax.all_to_all(scale_cut, EVERY, 0, 0, tiled=True)
     scale_share = jnp.sum(scale_cut, axis=0).reshape(4, -1)
-    one, two = tie((one, two), input_grad, gate_share, up_share, scale_share)
+    one, two = tie((one, two), input_grad, gate_share, up_share, down_share)
     attn_share = own + one.astype(WIDE) + two.astype(WIDE)
 
     return (

time: 648 us -> 641 us (0.989)
  starting transfers between devices: 79.9 us -> 72.4 us
    unnamed x166 -> x153, local copies, waits for them, and re-layouts: 19.5 us -> 17.7 us
  transfers between devices with their start and end apart: 64 -> 64, of which waited for: 36 -> 35; matrix products, arithmetic and copies ran while one was open for 17% -> 17% of each run, Pallas kernels for 22% -> 22%
where the time goes in v4:
time: 641 us; the launch traced here: 632 us
  waiting for transfers between devices  271 us (42%)
  Pallas kernels  140 us (22%)
  starting transfers between devices  72.4 us (11%)
  other arithmetic  57.7 us (9%)
  local copies, waits for them, and re-layouts  44.3 us (7%)
  matrix products  31.6 us (5%)
  between operations  15.3 us (2%)
    ppermute x32, waiting for transfers between devices, shift(): lax.ppermute(value, 'line', [(at, (at + step) % count) for at in range(co...  181 us
    ppermute x16, waiting for transfers between devices, swap(): return lax.ppermute(value, 'plane', [(b, b ^ bits) for b in range(count)])  61.1 us
    ppermute x32, starting transfers between devices, shift(): lax.ppermute(value, 'line', [(at, (at + step) % count) for at in range(co...  51.5 us
    dot_general x7, matrix products, contract(): lax.dot_general(left, right, (((left_dim,), (right_dim,)), ((), ())), pre...  31.6 us
    pallas_call x2, Pallas kernels, weight_grad_call(): pl.pallas_call(weight_grad_kernel, grid_spec=pltpu.PrefetchScalarGridSpec...  27.2 us
    pallas_call x2, Pallas kernels, widen_call(): pl.pallas_call(functools.partial(widen_kernel, sharers // STEPS), grid_sp...  26.2 us
    all_gather x1, waiting for transfers between devices, shards(): lax.all_gather(down_weight, ('fsdp', 'plane'), axis=0, tiled=True)  23.7 us
    pallas_call x2, Pallas kernels, attend_back_call(): pl.pallas_call(attend_back_kernel, grid=(keys // block, group_size), in_s...  19.7 us
  transfers between devices with their start and end apart: 64, of which 35 were waited for; matrix products, arithmetic and copies ran while one was open for 17% of the time, Pallas kernels for 22%

profile of v4, /device:TPU:0, one launch (start us, length us, event | category | flops | bytes accessed | tf_op | source)
XLA Modules:
  0.0 631.6 jit_solution(3630920342013807407)
XLA Ops:
  23.2 8.8 %collective-permute-done.1 = bf16[128,2304]{1,0:T(8,128)(2,1)S(1)} collective-permute-done((bf16[128,2304]{1,0:T(8,128)(2,1)S(1)}, bf16[128,2304]{1,0:T(8,128)(2,1)S(1)}, u32[]{:S(2)}, u32[]{:S(2)}) %collective-permute-start.1) | collective-permute-done | bytes 589856 | tf_op jit(solution)/shard_map/ppermute | solution.py:506
  32.0 12.4 %collective-permute-done = bf16[128,2304]{1,0:T(8,128)(2,1)S(1)} collective-permute-done((bf16[128,2304]{1,0:T(8,128)(2,1)S(1)}, bf16[128,2304]{1,0:T(8,128)(2,1)S(1)}, u32[]{:S(2)}, u32[]{:S(2)}) %collective-permute-start) | collective-permute-done | bytes 589856 | tf_op jit(solution)/shard_map/ppermute | solution.py:506
  96.3 7.6 %collective-permute-done.6 = bf16[128,512]{1,0:T(8,128)(2,1)S(1)} collective-permute-done((bf16[128,512]{1,0:T(8,128)(2,1)S(1)}, bf16[128,512]{1,0:T(8,128)(2,1)S(1)}, u32[]{:S(2)}, u32[]{:S(2)}) %collective-permute-start.6) | collective-permute-done | bytes 131104 | tf_op jit(solution)/shard_map/ppermute | solution.py:554
  138.2 11.3 %collective-permute-done.14 = bf16[128,2304]{1,0:T(8,128)(2,1)S(1)} collective-permute-done((bf16[128,2304]{1,0:T(8,128)(2,1)S(1)}, bf16[128,2304]{1,0:T(8,128)(2,1)S(1)}, u32[]{:S(2)}, u32[]{:S(2)}) %collective-permute-start.14) | collective-permute-done | bytes 589856 | tf_op jit(solution)/shard_map/ppermute | solution.py:506
  149.5 8.7 %collective-permute-done.15 = bf16[128,2304]{1,0:T(8,128)(2,1)S(1)} collective-permute-done((bf16[128,2304]{1,0:T(8,128)(2,1)S(1)}, bf16[128,2304]{1,0:T(8,128)(2,1)S(1)}, u32[]{:S(2)}, u32[]{:S(2)}) %collective-permute-start.15) | collective-permute-done | bytes 589856 | tf_op jit(solution)/shard_map/ppermute | solution.py:506
  162.5 25.5 %collective-permute-done.17 = bf16[128,2304]{1,0:T(8,128)(2,1)S(1)} collective-permute-done((bf16[128,2304]{1,0:T(8,128)(2,1)S(1)}, bf16[128,2304]{1,0:T(8,128)(2,1)S(1)}, u32[]{:S(2)}, u32[]{:S(2)}) %collective-permute-start.17) | collective-permute-done | bytes 589856 | tf_op jit(solution)/shard_map/ppermute | solution.py:506
  197.7 13.0 %shard_map.199 = (bf16[2304,256]{1,0:T(8,128)(2,1)}, bf16[1152,256]{1,0:T(8,128)(2,1)}, f32[2304,256]{1,0:T(8,128)}, f32[2304,256]{1,0:T(8,128)}) custom-call(s32[1]{0:T(128)} %bitcast.19.core_ref, bf16[256,2304]{1,0:T(8,128)(2,1)} %pad_maximum_fusion.4.rows_ref.refs_4_, bf16[4608,2304]{1,0:T(8,128)(2,1)} %all-gather.5.cloned.1.call-done.weight_ref), custom_call_target="tpu_custom_call" | custom-call | bytes 67108864 | tf_op jit(solution)/shard_map/pallas_call | solution.py:338
  213.7 13.2 %shard_map.200 = (bf16[2304,256]{1,0:T(8,128)(2,1)}, bf16[1152,256]{1,0:T(8,128)(2,1)}, f32[2304,256]{1,0:T(8,128)}, f32[2304,256]{1,0:T(8,128)}) custom-call(s32[1]{0:T(128)} %bitcast.19.core_ref, bf16[256,2304]{1,0:T(8,128)(2,1)} %copy-done.18, bf16[4608,2304]{1,0:T(8,128)(2,1)} %all-gather.5.cloned.1.call-done.weight_ref), custom_call_target="tpu_custom_call" | custom-call | bytes 67108864 | tf_op jit(solution)/shard_map/pallas_call | solution.py:338
  226.9 23.7 %all-gather.7.cloned.1.call-done.weight_ref = bf16[2304,2304]{1,0:T(8,128)(2,1)} async-done(((bf16[288,2304]{1,0:T(8,128)(2,1)}), bf16[2304,2304]{1,0:T(8,128)(2,1)}) %all-gather.7.cloned.1.call-update) | async-done | bytes 10616848 | tf_op jit(solution)/shard_map/all_gather | solution.py:642
  282.6 12.3 %collective-permute-done.22 = bf16[128,2304]{1,0:T(8,128)(2,1)S(1)} collective-permute-done((bf16[128,2304]{1,0:T(8,128)(2,1)S(1)}, bf16[128,2304]{1,0:T(8,128)(2,1)S(1)}, u32[]{:S(2)}, u32[]{:S(2)}) %collective-permute-start.22) | collective-permute-done | bytes 589856 | tf_op jit(solution)/shard_map/ppermute | solution.py:506
  294.9 12.1 %collective-permute-done.23 = bf16[128,2304]{1,0:T(8,128)(2,1)S(1)} collective-permute-done((bf16[128,2304]{1,0:T(8,128)(2,1)S(1)}, bf16[128,2304]{1,0:T(8,128)(2,1)S(1)}, u32[]{:S(2)}, u32[]{:S(2)}) %collective-permute-start.23) | collective-permute-done | bytes 589856 | tf_op jit(solution)/shard_map/ppermute | solution.py:506
  313.0 25.9 %collective-permute-done.29 = bf16[128,2304]{1,0:T(8,128)(2,1)S(1)} collective-permute-done((bf16[128,2304]{1,0:T(8,128)(2,1)S(1)}, bf16[128,2304]{1,0:T(8,128)(2,1)S(1)}, u32[]{:S(2)}, u32[]{:S(2)}) %collective-permute-start.29) | collective-permute-done | bytes 589856 | tf_op jit(solution)/shard_map/ppermute | solution.py:506
  341.3 9.2 %shard_map.201 = (bf16[4608,256]{1,0:T(8,128)(2,1)}, bf16[2304,256]{1,0:T(8,128)(2,1)}) custom-call(s32[1]{0:T(128)} %bitcast.19.core_ref, bf16[256,2304]{1,0:T(8,128)(2,1)} %copy-done.10, bf16[2304,2304]{1,0:T(8,128)(2,1)} %all-gather.7.cloned.1.call-done.weight_ref, f32[2304,256]{1,0:T(8,128)} %get-tuple-element.180.bent_ref, ...), custom_call_target="tpu_custom_call" | custom-call | bytes 67108864 | tf_op jit(solution)/shard_map/pallas_call | solution.py:382
  356.3 9.3 %shard_map.202 = (bf16[4608,256]{1,0:T(8,128)(2,1)}, bf16[2304,256]{1,0:T(8,128)(2,1)}) custom-call(s32[1]{0:T(128)} %bitcast.19.core_ref, bf16[256,2304]{1,0:T(8,128)(2,1)} %copy-done.20, bf16[2304,2304]{1,0:T(8,128)(2,1)} %all-gather.7.cloned.1.call-done.weight_ref, f32[2304,256]{1,0:T(8,128)} %get-tuple-element.186.bent_ref, ...), custom_call_target="tpu_custom_call" | custom-call | bytes 67108864 | tf_op jit(solution)/shard_map/pallas_call | solution.py:382
  365.6 15.5 %fusion.55 = (bf16[512,2304]{1,0:T(8,128)(2,1)S(1)}, f32[512,2304]{1,0:T(8,128)S(1)}) fusion(bf16[4608,2304]{1,0:T(8,128)(2,1)} %all-gather.5.cloned.1.call-done.weight_ref, bf16[4608,256]{1,0:T(8,128)(2,1)} %get-tuple-element.199.refs_1_, bf16[4608,256]{1,0:T(8,128)(2,1)S(1)} %copy-done.29), kind=kOutput, calls=%fused_computation.221 | convolution fusion | flops 10882252800 | bytes 33030144 | tf_op jit(solution)/shard_map/dot_general | solution.py:25
  384.9 10.4 %shard_map.203 = bf16[1152,2304]{1,0:T(8,128)(2,1)} custom-call(s32[1]{0:T(128)} %bitcast.19.core_ref, bf16[2304,256]{1,0:T(8,128)(2,1)} %get-tuple-element.189.refs_0_, bf16[2304,256]{1,0:T(8,128)(2,1)} %get-tuple-element.190.refs_1_, bf16[1152,256]{1,0:T(8,128)(2,1)} %collective-permute-done.24.refs_2_, bf16[1152,256]{1,0:T(8,128)(2,1)} %copy-done.42, ...), custom_call_target="tpu_custom_call" | custom-call | bytes 67108864 | tf_op jit(solution)/shard_map/pallas_call | solution.py:432
  408.0 16.7 %shard_map.204 = bf16[2304,2304]{1,0:T(8,128)(2,1)} custom-call(s32[1]{0:T(128)} %bitcast.19.core_ref, bf16[4608,256]{1,0:T(8,128)(2,1)} %get-tuple-element.198.refs_0_, bf16[4608,256]{1,0:T(8,128)(2,1)} %get-tuple-element.199.refs_1_, bf16[2304,256]{1,0:T(8,128)(2,1)} %copy-done.39, bf16[2304,256]{1,0:T(8,128)(2,1)} %copy-done.40, ...), custom_call_target="tpu_custom_call" | custom-call | bytes 67108864 | tf_op jit(solution)/shard_map/pallas_call | solution.py:432
  440.8 11.8 %collective-permute-done.41 = bf16[128,2304]{1,0:T(8,128)(2,1)S(1)} collective-permute-done((bf16[128,2304]{1,0:T(8,128)(2,1)S(1)}, bf16[128,2304]{1,0:T(8,128)(2,1)S(1)}, u32[]{:S(2)}, u32[]{:S(2)}) %collective-permute-start.41) | collective-permute-done | bytes 589856 | tf_op jit(solution)/shard_map/ppermute | solution.py:506
  452.7 12.1 %collective-permute-done.40 = bf16[128,2304]{1,0:T(8,128)(2,1)S(1)} collective-permute-done((bf16[128,2304]{1,0:T(8,128)(2,1)S(1)}, bf16[128,2304]{1,0:T(8,128)(2,1)S(1)}, u32[]{:S(2)}, u32[]{:S(2)}) %collective-permute-start.40) | collective-permute-done | bytes 589856 | tf_op jit(solution)/shard_map/ppermute | solution.py:506
  470.2 9.5 %shard_map.205 = (bf16[256,512]{1,0:T(8,128)(2,1)}, f32[2048,512]{1,0:T(8,128)}) custom-call(bf16[512,256]{1,0:T(8,128)(2,1)} %get-tuple-element.150.query_ref.refs_0_, bf16[256,512]{1,0:T(8,128)(2,1)} %convolution_convert_fusion.1.refs_1_, f32[256,512]{1,0:T(8,128)} %get-tuple-element.211.refs_2_, bf16[2048,512]{1,0:T(8,128)(2,1)} %copy-done, ...), custom_call_target="tpu_custom_call" | custom-call | bytes 67108864 | tf_op jit(solution)/shard_map/pallas_call | solution.py:230
  481.3 10.2 %shard_map.206 = (bf16[256,512]{1,0:T(8,128)(2,1)}, bf16[2048,512]{1,0:T(8,128)(2,1)}) custom-call(bf16[512,256]{1,0:T(8,128)(2,1)} %get-tuple-element.143.query_ref.refs_0_, bf16[256,512]{1,0:T(8,128)(2,1)} %convolution_convert_fusion.refs_1_, f32[256,512]{1,0:T(8,128)} %get-tuple-element.218.refs_2_, bf16[2048,512]{1,0:T(8,128)(2,1)} %copy-done, ...), custom_call_target="tpu_custom_call" | custom-call | bytes 67108864 | tf_op jit(solution)/shard_map/pallas_call | solution.py:230
  495.6 11.6 %collective-permute-done.46 = bf16[256,512]{1,0:T(8,128)(2,1)S(1)} collective-permute-done((bf16[256,512]{1,0:T(8,128)(2,1)S(1)}, bf16[256,512]{1,0:T(8,128)(2,1)S(1)}, u32[]{:S(2)}, u32[]{:S(2)}) %collective-permute-start.46) | collective-permute-done | bytes 262176 | tf_op jit(solution)/shard_map/ppermute | solution.py:554
  517.0 16.9 %collective-permute-done.45 = bf16[512,512]{1,0:T(8,128)(2,1)S(1)} collective-permute-done((bf16[512,512]{1,0:T(8,128)(2,1)S(1)}, bf16[512,512]{1,0:T(8,128)(2,1)S(1)}, u32[]{:S(2)}, u32[]{:S(2)}) %collective-permute-start.45) | collective-permute-done | bytes 524320 | tf_op jit(solution)/shard_map/ppermute | solution.py:554
  582.6 9.9 %collective-permute-done.55 = bf16[96,2304]{1,0:T(8,128)(2,1)S(1)} collective-permute-done((bf16[96,2304]{1,0:T(8,128)(2,1)S(1)}, bf16[96,2304]{1,0:T(8,128)(2,1)S(1)}, u32[]{:S(2)}, u32[]{:S(2)}) %collective-permute-start.55) | collective-permute-done | bytes 442400 | tf_op jit(solution)/shard_map/ppermute | solution.py:554
  (441 shorter events, 298.5 us)
Async XLA Ops:
  7.2 55.0 %all-gather.9.cloned.1.call-start = ((), (), s32[]{:S(2)}) async-start(), calls=%async_computation.7 | async-start | bytes 7962624 | tf_op jit(solution)/shard_map/all_gather | solution.py:637
  9.4 188.3 %all-gather.5.cloned.1.call-start = ((), (), s32[]{:S(2)}) async-start(), calls=%async_computation.3 | async-start | bytes 23887872 | tf_op jit(solution)/shard_map/all_gather | solution.py:641
  12.2 238.4 %all-gather.7.cloned.1.call-start = ((), (), s32[]{:S(2)}) async-start(), calls=%async_computation.4 | async-start | bytes 11943936 | tf_op jit(solution)/shard_map/all_gather | solution.py:642
  13.0 590.7 %reduce-scatter.5.cloned.1.call-start = ((), (), s32[]{:S(2)}) async-start(), calls=%async_computation.6 | async-start | bytes 6635520 | tf_op jit(solution)/shard_map/reduce_scatter | solution.py:775
  18.3 26.1 %collective-permute-start = (bf16[128,2304]{1,0:T(8,128)(2,1)S(1)}, bf16[128,2304]{1,0:T(8,128)(2,1)S(1)}, u32[]{:S(2)}, u32[]{:S(2)}) collective-permute-start(bf16[128,2304]{1,0:T(8,128)(2,1)S(1)} %bitcast.111), channel_id=1, source_target_pairs={{0,8},{8,16},{16,24},{24,0},{1,9},{9,17},{17,25},{25,1},{2,10},{10... | collective-permute-start | bytes 1769480 | tf_op jit(solution)/shard_map/ppermute | solution.py:506
  133.0 25.2 %collective-permute-start.15 = (bf16[128,2304]{1,0:T(8,128)(2,1)S(1)}, bf16[128,2304]{1,0:T(8,128)(2,1)S(1)}, u32[]{:S(2)}, u32[]{:S(2)}) collective-permute-start(bf16[128,2304]{1,0:T(8,128)(2,1)S(1)} %pad_maximum_fusion.11), channel_id=1, source_target_pairs={{0,24},{8,0},{16,8},{24,16},{1,25},{9,1},{17,9},{25,17},{2,26},{10... | collective-permute-start | bytes 1769480 | tf_op jit(solution)/shard_map/ppermute | solution.py:506
  160.4 27.6 %collective-permute-start.17 = (bf16[128,2304]{1,0:T(8,128)(2,1)S(1)}, bf16[128,2304]{1,0:T(8,128)(2,1)S(1)}, u32[]{:S(2)}, u32[]{:S(2)}) collective-permute-start(bf16[128,2304]{1,0:T(8,128)(2,1)S(1)} %multiply_convert_fusion), channel_id=1, source_target_pairs={{0,24},{8,0},{16,8},{24,16},{1,25},{9,1},{17,9},{25,17},{2,26},{10... | collective-permute-start | bytes 1769480 | tf_op jit(solution)/shard_map/ppermute | solution.py:506
  162.4 25.6 %collective-permute-start.16 = (bf16[128,2304]{1,0:T(8,128)(2,1)S(1)}, bf16[128,2304]{1,0:T(8,128)(2,1)}, u32[]{:S(2)}, u32[]{:S(2)}) collective-permute-start(bf16[128,2304]{1,0:T(8,128)(2,1)S(1)} %multiply_convert_fusion), channel_id=1, source_target_pairs={{0,8},{8,16},{16,24},{24,0},{1,9},{9,17},{17,25},{25,1},{2,10},{10... | collective-permute-start | bytes 1769480 | tf_op jit(solution)/shard_map/ppermute | solution.py:506
  276.4 30.7 %collective-permute-start.26 = (bf16[256,2304]{1,0:T(8,128)(2,1)S(1)}, bf16[256,2304]{1,0:T(8,128)(2,1)S(1)}, u32[]{:S(2)}, u32[]{:S(2)}) collective-permute-start(bf16[256,2304]{1,0:T(8,128)(2,1)S(1)} %copy-done.9), channel_id=1, source_target_pairs={{0,1},{1,0},{2,3},{3,2},{4,5},{5,4},{6,7},{7,6},{8,9},{9,8},{10,11... | collective-permute-start | bytes 3538952 | tf_op jit(solution)/shard_map/ppermute | solution.py:598
  276.9 30.2 %collective-permute-start.27 = (bf16[256,2304]{1,0:T(8,128)(2,1)S(1)}, bf16[256,2304]{1,0:T(8,128)(2,1)S(1)}, u32[]{:S(2)}, u32[]{:S(2)}) collective-permute-start(bf16[256,2304]{1,0:T(8,128)(2,1)S(1)} %copy-done.19), channel_id=1, source_target_pairs={{0,1},{1,0},{2,3},{3,2},{4,5},{5,4},{6,7},{7,6},{8,9},{9,8},{10,11... | collective-permute-start | bytes 3538952 | tf_op jit(solution)/shard_map/ppermute | solution.py:598
  279.3 27.8 %collective-permute-start.23 = (bf16[128,2304]{1,0:T(8,128)(2,1)S(1)}, bf16[128,2304]{1,0:T(8,128)(2,1)S(1)}, u32[]{:S(2)}, u32[]{:S(2)}) collective-permute-start(bf16[128,2304]{1,0:T(8,128)(2,1)S(1)} %pad_maximum_fusion.13), channel_id=1, source_target_pairs={{0,24},{8,0},{16,8},{24,16},{1,25},{9,1},{17,9},{25,17},{2,26},{10... | collective-permute-start | bytes 1769480 | tf_op jit(solution)/shard_map/ppermute | solution.py:506
  311.0 27.9 %collective-permute-start.29 = (bf16[128,2304]{1,0:T(8,128)(2,1)S(1)}, bf16[128,2304]{1,0:T(8,128)(2,1)S(1)}, u32[]{:S(2)}, u32[]{:S(2)}) collective-permute-start(bf16[128,2304]{1,0:T(8,128)(2,1)S(1)} %get-tuple-element.311), channel_id=1, source_target_pairs={{0,24},{8,0},{16,8},{24,16},{1,25},{9,1},{17,9},{25,17},{2,26},{10... | collective-permute-start | bytes 1769480 | tf_op jit(solution)/shard_map/ppermute | solution.py:506
  312.5 26.4 %collective-permute-start.28 = (bf16[128,2304]{1,0:T(8,128)(2,1)S(1)}, bf16[128,2304]{1,0:T(8,128)(2,1)S(1)}, u32[]{:S(2)}, u32[]{:S(2)}) collective-permute-start(bf16[128,2304]{1,0:T(8,128)(2,1)S(1)} %get-tuple-element.311), channel_id=1, source_target_pairs={{0,8},{8,16},{16,24},{24,0},{1,9},{9,17},{17,25},{25,1},{2,10},{10... | collective-permute-start | bytes 1769480 | tf_op jit(solution)/shard_map/ppermute | solution.py:506
  341.3 43.5 %collective-permute-start.34 = (bf16[256,2304]{1,0:T(8,128)(2,1)S(1)}, bf16[256,2304]{1,0:T(8,128)(2,1)}, u32[]{:S(2)}, u32[]{:S(2)}) collective-permute-start(bf16[256,2304]{1,0:T(8,128)(2,1)S(1)} %pad_maximum_fusion.5.rows_ref.refs_4_), channel_id=1, source_target_pairs={{0,1},{1,0},{2,3},{3,2},{4,5},{5,4},{6,7},{7,6},{8,9},{9,8},{10,11... | collective-permute-start | bytes 3538952 | tf_op jit(solution)/shard_map/ppermute | solution.py:598
  355.3 29.6 %collective-permute-start.35 = (bf16[256,2304]{1,0:T(8,128)(2,1)S(1)}, bf16[256,2304]{1,0:T(8,128)(2,1)}, u32[]{:S(2)}, u32[]{:S(2)}) collective-permute-start(bf16[256,2304]{1,0:T(8,128)(2,1)S(1)} %constant_dynamic-update-slice_fusion.16.rows_ref.refs_5_), channel_id=1, source_target_pairs={{0,1},{1,0},{2,3},{3,2},{4,5},{5,4},{6,7},{7,6},{8,9},{9,8},{10,11... | collective-permute-start | bytes 3538952 | tf_op jit(solution)/shard_map/ppermute | solution.py:598
  396.3 210.3 %reduce-scatter.3.cloned.1.call-start = ((), (), s32[]{:S(2)}) async-start(), calls=%async_computation.5 | async-start | bytes 13271040 | tf_op jit(solution)/shard_map/reduce_scatter | solution.py:776
  402.1 22.6 %collective-permute-start.36 = (bf16[128,2304]{1,0:T(8,128)(2,1)}, bf16[128,2304]{1,0:T(8,128)(2,1)S(1)}, u32[]{:S(2)}, u32[]{:S(2)}) collective-permute-start(bf16[128,2304]{1,0:T(8,128)(2,1)} %pad_maximum_fusion.14), channel_id=1, source_target_pairs={{0,8},{8,16},{16,24},{24,0},{1,9},{9,17},{17,25},{25,1},{2,10},{10... | collective-permute-start | bytes 1769480 | tf_op jit(solution)/shard_map/ppermute | solution.py:506
  403.5 27.9 %collective-permute-start.37 = (bf16[128,2304]{1,0:T(8,128)(2,1)}, bf16[128,2304]{1,0:T(8,128)(2,1)S(1)}, u32[]{:S(2)}, u32[]{:S(2)}) collective-permute-start(bf16[128,2304]{1,0:T(8,128)(2,1)} %pad_maximum_fusion.15), channel_id=1, source_target_pairs={{0,24},{8,0},{16,8},{24,16},{1,25},{9,1},{17,9},{25,17},{2,26},{10... | collective-permute-start | bytes 1769480 | tf_op jit(solution)/shard_map/ppermute | solution.py:506
  438.9 25.9 %collective-permute-start.40 = (bf16[128,2304]{1,0:T(8,128)(2,1)S(1)}, bf16[128,2304]{1,0:T(8,128)(2,1)S(1)}, u32[]{:S(2)}, u32[]{:S(2)}) collective-permute-start(bf16[128,2304]{1,0:T(8,128)(2,1)S(1)} %subtract_convert_fusion), channel_id=1, source_target_pairs={{0,8},{8,16},{16,24},{24,0},{1,9},{9,17},{17,25},{25,1},{2,10},{10... | collective-permute-start | bytes 1769480 | tf_op jit(solution)/shard_map/ppermute | solution.py:506
  508.8 25.1 %collective-permute-start.45 = (bf16[512,512]{1,0:T(8,128)(2,1)S(1)}, bf16[512,512]{1,0:T(8,128)(2,1)S(1)}, u32[]{:S(2)}, u32[]{:S(2)}) collective-permute-start(bf16[512,512]{1,0:T(8,128)(2,1)S(1)} %pad_maximum_fusion.19), channel_id=1, source_target_pairs={{0,2},{2,0},{4,6},{6,4},{1,3},{3,1},{5,7},{7,5},{8,10},{10,8},{12,... | collective-permute-start | bytes 1572872 | tf_op jit(solution)/shard_map/ppermute | solution.py:554
  509.4 25.1 %collective-permute-start.47 = (bf16[512,512]{1,0:T(8,128)(2,1)S(1)}, bf16[512,512]{1,0:T(8,128)(2,1)S(1)}, u32[]{:S(2)}, u32[]{:S(2)}) collective-permute-start(bf16[512,512]{1,0:T(8,128)(2,1)S(1)} %pad_maximum_fusion.20), channel_id=1, source_target_pairs={{0,4},{2,6},{4,0},{6,2},{1,5},{3,7},{5,1},{7,3},{8,12},{10,14},{12... | collective-permute-start | bytes 1572872 | tf_op jit(solution)/shard_map/ppermute | solution.py:554
  566.9 28.9 %collective-permute-start.50 = (bf16[128,2304]{1,0:T(8,128)(2,1)}, bf16[128,2304]{1,0:T(8,128)(2,1)}, u32[]{:S(2)}, u32[]{:S(2)}) collective-permute-start(bf16[128,2304]{1,0:T(8,128)(2,1)} %pad_maximum_fusion.16), channel_id=1, source_target_pairs={{0,8},{8,16},{16,24},{24,0},{1,9},{9,17},{17,25},{25,1},{2,10},{10... | collective-permute-start | bytes 1769480 | tf_op jit(solution)/shard_map/ppermute | solution.py:506
  568.6 28.6 %collective-permute-start.51 = (bf16[128,2304]{1,0:T(8,128)(2,1)}, bf16[128,2304]{1,0:T(8,128)(2,1)}, u32[]{:S(2)}, u32[]{:S(2)}) collective-permute-start(bf16[128,2304]{1,0:T(8,128)(2,1)} %pad_maximum_fusion.17), channel_id=1, source_target_pairs={{0,24},{8,0},{16,8},{24,16},{1,25},{9,1},{17,9},{25,17},{2,26},{10... | collective-permute-start | bytes 1769480 | tf_op jit(solution)/shard_map/ppermute | solution.py:506
  598.7 21.8 %collective-permute-start.57 = (bf16[192,2304]{1,0:T(8,128)(2,1)}, bf16[192,2304]{1,0:T(8,128)(2,1)}, u32[]{:S(2)}, u32[]{:S(2)}) collective-permute-start(bf16[192,2304]{1,0:T(8,128)(2,1)} %pad_maximum_fusion.9), channel_id=1, source_target_pairs={{0,4},{2,6},{4,0},{6,2},{1,5},{3,7},{5,1},{7,3},{8,12},{10,14},{12... | collective-permute-start | bytes 2654216 | tf_op jit(solution)/shard_map/ppermute | solution.py:554
  (108 other events, 1104.5 us)
Sparse Core Ops, SparseCore 0:
  10.5 51.6 all-gather.8
  64.6 120.1 all-gather.4
  186.7 63.7 all-gather.6
  396.5 60.3 reduce-scatter.4
  459.8 121.4 reduce-scatter.2

commit v5 on v4

--- a/solution.py
+++ b/solution.py
@@ -535,12 +535,8 @@
     own, former = early[:rows], early[rows:]
     sends = lax.optimization_barrier(
         (
-            jnp.concatenate(
-                [following[:half] + for_following.astype(WIDE), following[half:]], axis=0
-            ).astype(LOW),
-            jnp.concatenate(
-                [former[:half], former[half:] + for_former.astype(WIDE)], axis=0
-            ).astype(LOW),
+            (following + jnp.pad(for_following, ((0, half), (0, 0))).astype(WIDE)).astype(LOW),
+            (former + jnp.pad(for_former, ((half, 0), (0, 0))).astype(WIDE)).astype(LOW),
         )
     )
     terms = shift(sends[0], 1), shift(sends[1], -1)
@@ -580,8 +576,8 @@
     low_far = far.astype(LOW)
     for_two = swap(low_far[:half], 1).astype(WIDE)
     for_one = swap(low_far[half:], 2).astype(WIDE)
-    send_one = jnp.concatenate([one[:half], one[half:] + for_one], axis=0).astype(LOW)
-    send_two = jnp.concatenate([two[:half] + for_two, two[half:]], axis=0).astype(LOW)
+    send_one = (one + jnp.pad(for_one, ((half, 0), (0, 0)))).astype(LOW)
+    send_two = (two + jnp.pad(for_two, ((0, half), (0, 0)))).astype(LOW)
     return own, send_one, send_two
 
 

time: 641 us -> 637 us (level)
  waiting for transfers between devices: 271 us -> 263 us
    convert_element_type x0 -> x10, other arithmetic: none -> 10.2 us  [the longest x4 4.21 us: line_scatter(): (following + jnp.pad(for_following, ((0, half), (0, 0))).astype(WIDE)).as...]
    ppermute x16, waiting for transfers between devices: 61.1 us -> 53.5 us  [swap(): return lax.ppermute(value, 'plane', [(b, b ^ bits) for b in range(count)])]
    another operation x11 -> x1, other arithmetic: 7.51 us -> 0.36 us
    unnamed x153 -> x161, local copies, waits for them, and re-layouts: 17.7 us -> 17.5 us
where the time goes in v5:
time: 637 us; the launch traced here: 628 us
  waiting for transfers between devices  263 us (41%)
  Pallas kernels  141 us (22%)
  starting transfers between devices  73.9 us (12%)
  other arithmetic  58.7 us (9%)
  local copies, waits for them, and re-layouts  44.4 us (7%)
  matrix products  31.8 us (5%)
  between operations  15.4 us (2%)
    ppermute x32, waiting for transfers between devices, shift(): lax.ppermute(value, 'line', [(at, (at + step) % count) for at in range(co...  180 us
    ppermute x16, waiting for transfers between devices, swap(): return lax.ppermute(value, 'plane', [(b, b ^ bits) for b in range(count)])  53.5 us
    ppermute x32, starting transfers between devices, shift(): lax.ppermute(value, 'line', [(at, (at + step) % count) for at in range(co...  52 us
    dot_general x7, matrix products, contract(): lax.dot_general(left, right, (((left_dim,), (right_dim,)), ((), ())), pre...  31.8 us
    pallas_call x2, Pallas kernels, weight_grad_call(): pl.pallas_call(weight_grad_kernel, grid_spec=pltpu.PrefetchScalarGridSpec...  27.2 us
    pallas_call x2, Pallas kernels, widen_call(): pl.pallas_call(functools.partial(widen_kernel, sharers // STEPS), grid_sp...  26.4 us
    all_gather x1, waiting for transfers between devices, shards(): lax.all_gather(down_weight, ('fsdp', 'plane'), axis=0, tiled=True)  23.7 us
    pallas_call x2, Pallas kernels, attend_back_call(): pl.pallas_call(attend_back_kernel, grid=(keys // block, group_size), in_s...  19.9 us
  transfers between devices with their start and end apart: 64, of which 35 were waited for; matrix products, arithmetic and copies ran while one was open for 17% of the time, Pallas kernels for 22%

profile of v5, /device:TPU:0, one launch (start us, length us, event | category | flops | bytes accessed | tf_op | source)
XLA Modules:
  0.0 627.8 jit_solution(15570717945096332992)
XLA Ops:
  23.2 8.9 %collective-permute-done.1 = bf16[128,2304]{1,0:T(8,128)(2,1)S(1)} collective-permute-done((bf16[128,2304]{1,0:T(8,128)(2,1)S(1)}, bf16[128,2304]{1,0:T(8,128)(2,1)S(1)}, u32[]{:S(2)}, u32[]{:S(2)}) %collective-permute-start.1) | collective-permute-done | bytes 589856 | tf_op jit(solution)/shard_map/ppermute | solution.py:506
  32.0 12.4 %collective-permute-done = bf16[128,2304]{1,0:T(8,128)(2,1)S(1)} collective-permute-done((bf16[128,2304]{1,0:T(8,128)(2,1)S(1)}, bf16[128,2304]{1,0:T(8,128)(2,1)S(1)}, u32[]{:S(2)}, u32[]{:S(2)}) %collective-permute-start) | collective-permute-done | bytes 589856 | tf_op jit(solution)/shard_map/ppermute | solution.py:506
  96.3 7.6 %collective-permute-done.6 = bf16[128,512]{1,0:T(8,128)(2,1)S(1)} collective-permute-done((bf16[128,512]{1,0:T(8,128)(2,1)S(1)}, bf16[128,512]{1,0:T(8,128)(2,1)S(1)}, u32[]{:S(2)}, u32[]{:S(2)}) %collective-permute-start.6) | collective-permute-done | bytes 131104 | tf_op jit(solution)/shard_map/ppermute | solution.py:550
  137.5 11.0 %collective-permute-done.14 = bf16[128,2304]{1,0:T(8,128)(2,1)S(1)} collective-permute-done((bf16[128,2304]{1,0:T(8,128)(2,1)S(1)}, bf16[128,2304]{1,0:T(8,128)(2,1)S(1)}, u32[]{:S(2)}, u32[]{:S(2)}) %collective-permute-start.14) | collective-permute-done | bytes 589856 | tf_op jit(solution)/shard_map/ppermute | solution.py:506
  148.5 8.9 %collective-permute-done.15 = bf16[128,2304]{1,0:T(8,128)(2,1)S(1)} collective-permute-done((bf16[128,2304]{1,0:T(8,128)(2,1)S(1)}, bf16[128,2304]{1,0:T(8,128)(2,1)S(1)}, u32[]{:S(2)}, u32[]{:S(2)}) %collective-permute-start.15) | collective-permute-done | bytes 589856 | tf_op jit(solution)/shard_map/ppermute | solution.py:506
  161.7 25.8 %collective-permute-done.17 = bf16[128,2304]{1,0:T(8,128)(2,1)S(1)} collective-permute-done((bf16[128,2304]{1,0:T(8,128)(2,1)S(1)}, bf16[128,2304]{1,0:T(8,128)(2,1)S(1)}, u32[]{:S(2)}, u32[]{:S(2)}) %collective-permute-start.17) | collective-permute-done | bytes 589856 | tf_op jit(solution)/shard_map/ppermute | solution.py:506
  197.3 13.0 %shard_map.199 = (bf16[2304,256]{1,0:T(8,128)(2,1)}, bf16[1152,256]{1,0:T(8,128)(2,1)}, f32[2304,256]{1,0:T(8,128)}, f32[2304,256]{1,0:T(8,128)}) custom-call(s32[1]{0:T(128)} %bitcast.19.core_ref, bf16[256,2304]{1,0:T(8,128)(2,1)} %pad_maximum_fusion.4.rows_ref.refs_4_, bf16[4608,2304]{1,0:T(8,128)(2,1)} %all-gather.5.cloned.1.call-done.weight_ref), custom_call_target="tpu_custom_call" | custom-call | bytes 67108864 | tf_op jit(solution)/shard_map/pallas_call | solution.py:338
  213.4 13.4 %shard_map.200 = (bf16[2304,256]{1,0:T(8,128)(2,1)}, bf16[1152,256]{1,0:T(8,128)(2,1)}, f32[2304,256]{1,0:T(8,128)}, f32[2304,256]{1,0:T(8,128)}) custom-call(s32[1]{0:T(128)} %bitcast.19.core_ref, bf16[256,2304]{1,0:T(8,128)(2,1)} %copy-done.19, bf16[4608,2304]{1,0:T(8,128)(2,1)} %all-gather.5.cloned.1.call-done.weight_ref), custom_call_target="tpu_custom_call" | custom-call | bytes 67108864 | tf_op jit(solution)/shard_map/pallas_call | solution.py:338
  226.8 23.7 %all-gather.7.cloned.1.call-done.weight_ref = bf16[2304,2304]{1,0:T(8,128)(2,1)} async-done(((bf16[288,2304]{1,0:T(8,128)(2,1)}), bf16[2304,2304]{1,0:T(8,128)(2,1)}) %all-gather.7.cloned.1.call-update) | async-done | bytes 10616848 | tf_op jit(solution)/shard_map/all_gather | solution.py:638
  281.8 12.7 %collective-permute-done.22 = bf16[128,2304]{1,0:T(8,128)(2,1)S(1)} collective-permute-done((bf16[128,2304]{1,0:T(8,128)(2,1)S(1)}, bf16[128,2304]{1,0:T(8,128)(2,1)S(1)}, u32[]{:S(2)}, u32[]{:S(2)}) %collective-permute-start.22) | collective-permute-done | bytes 589856 | tf_op jit(solution)/shard_map/ppermute | solution.py:506
  294.5 11.9 %collective-permute-done.23 = bf16[128,2304]{1,0:T(8,128)(2,1)S(1)} collective-permute-done((bf16[128,2304]{1,0:T(8,128)(2,1)S(1)}, bf16[128,2304]{1,0:T(8,128)(2,1)S(1)}, u32[]{:S(2)}, u32[]{:S(2)}) %collective-permute-start.23) | collective-permute-done | bytes 589856 | tf_op jit(solution)/shard_map/ppermute | solution.py:506
  312.4 25.8 %collective-permute-done.29 = bf16[128,2304]{1,0:T(8,128)(2,1)S(1)} collective-permute-done((bf16[128,2304]{1,0:T(8,128)(2,1)S(1)}, bf16[128,2304]{1,0:T(8,128)(2,1)S(1)}, u32[]{:S(2)}, u32[]{:S(2)}) %collective-permute-start.29) | collective-permute-done | bytes 589856 | tf_op jit(solution)/shard_map/ppermute | solution.py:506
  340.5 9.2 %shard_map.201 = (bf16[4608,256]{1,0:T(8,128)(2,1)}, bf16[2304,256]{1,0:T(8,128)(2,1)}) custom-call(s32[1]{0:T(128)} %bitcast.19.core_ref, bf16[256,2304]{1,0:T(8,128)(2,1)} %copy-done.13, bf16[2304,2304]{1,0:T(8,128)(2,1)} %all-gather.7.cloned.1.call-done.weight_ref, f32[2304,256]{1,0:T(8,128)} %get-tuple-element.180.bent_ref, ...), custom_call_target="tpu_custom_call" | custom-call | bytes 67108864 | tf_op jit(solution)/shard_map/pallas_call | solution.py:382
  355.9 9.3 %shard_map.202 = (bf16[4608,256]{1,0:T(8,128)(2,1)}, bf16[2304,256]{1,0:T(8,128)(2,1)}) custom-call(s32[1]{0:T(128)} %bitcast.19.core_ref, bf16[256,2304]{1,0:T(8,128)(2,1)} %copy-done.21, bf16[2304,2304]{1,0:T(8,128)(2,1)} %all-gather.7.cloned.1.call-done.weight_ref, f32[2304,256]{1,0:T(8,128)} %get-tuple-element.186.bent_ref, ...), custom_call_target="tpu_custom_call" | custom-call | bytes 67108864 | tf_op jit(solution)/shard_map/pallas_call | solution.py:382
  365.2 15.6 %fusion.58 = (bf16[512,2304]{1,0:T(8,128)(2,1)S(1)}, f32[512,2304]{1,0:T(8,128)S(1)}) fusion(bf16[4608,2304]{1,0:T(8,128)(2,1)} %all-gather.5.cloned.1.call-done.weight_ref, bf16[4608,256]{1,0:T(8,128)(2,1)} %get-tuple-element.199.refs_1_, bf16[4608,256]{1,0:T(8,128)(2,1)S(1)} %copy-done.28), kind=kOutput, calls=%fused_computation.208 | convolution fusion | flops 10882252800 | bytes 33030144 | tf_op jit(solution)/shard_map/dot_general | solution.py:25
  385.4 10.4 %shard_map.203 = bf16[1152,2304]{1,0:T(8,128)(2,1)} custom-call(s32[1]{0:T(128)} %bitcast.19.core_ref, bf16[2304,256]{1,0:T(8,128)(2,1)} %get-tuple-element.189.refs_0_, bf16[2304,256]{1,0:T(8,128)(2,1)} %get-tuple-element.190.refs_1_, bf16[1152,256]{1,0:T(8,128)(2,1)} %copy-done.41, bf16[1152,256]{1,0:T(8,128)(2,1)} %copy-done.42, ...), custom_call_target="tpu_custom_call" | custom-call | bytes 67108864 | tf_op jit(solution)/shard_map/pallas_call | solution.py:432
  408.0 16.8 %shard_map.204 = bf16[2304,2304]{1,0:T(8,128)(2,1)} custom-call(s32[1]{0:T(128)} %bitcast.19.core_ref, bf16[4608,256]{1,0:T(8,128)(2,1)} %get-tuple-element.198.refs_0_, bf16[4608,256]{1,0:T(8,128)(2,1)} %get-tuple-element.199.refs_1_, bf16[2304,256]{1,0:T(8,128)(2,1)} %copy-done.39, bf16[2304,256]{1,0:T(8,128)(2,1)} %copy-done.40, ...), custom_call_target="tpu_custom_call" | custom-call | bytes 67108864 | tf_op jit(solution)/shard_map/pallas_call | solution.py:432
  441.8 10.5 %collective-permute-done.41 = bf16[128,2304]{1,0:T(8,128)(2,1)S(1)} collective-permute-done((bf16[128,2304]{1,0:T(8,128)(2,1)S(1)}, bf16[128,2304]{1,0:T(8,128)(2,1)S(1)}, u32[]{:S(2)}, u32[]{:S(2)}) %collective-permute-start.41) | collective-permute-done | bytes 589856 | tf_op jit(solution)/shard_map/ppermute | solution.py:506
  452.3 12.1 %collective-permute-done.40 = bf16[128,2304]{1,0:T(8,128)(2,1)S(1)} collective-permute-done((bf16[128,2304]{1,0:T(8,128)(2,1)S(1)}, bf16[128,2304]{1,0:T(8,128)(2,1)S(1)}, u32[]{:S(2)}, u32[]{:S(2)}) %collective-permute-start.40) | collective-permute-done | bytes 589856 | tf_op jit(solution)/shard_map/ppermute | solution.py:506
  469.8 9.5 %shard_map.205 = (bf16[256,512]{1,0:T(8,128)(2,1)}, f32[2048,512]{1,0:T(8,128)}) custom-call(bf16[512,256]{1,0:T(8,128)(2,1)} %get-tuple-element.150.query_ref.refs_0_, bf16[256,512]{1,0:T(8,128)(2,1)} %convolution_convert_fusion.1.refs_1_, f32[256,512]{1,0:T(8,128)} %get-tuple-element.211.refs_2_, bf16[2048,512]{1,0:T(8,128)(2,1)} %copy-done.1, ...), custom_call_target="tpu_custom_call" | custom-call | bytes 67108864 | tf_op jit(solution)/shard_map/pallas_call | solution.py:230
  481.0 10.4 %shard_map.206 = (bf16[256,512]{1,0:T(8,128)(2,1)}, bf16[2048,512]{1,0:T(8,128)(2,1)}) custom-call(bf16[512,256]{1,0:T(8,128)(2,1)} %get-tuple-element.143.query_ref.refs_0_, bf16[256,512]{1,0:T(8,128)(2,1)} %convolution_convert_fusion.refs_1_, f32[256,512]{1,0:T(8,128)} %get-tuple-element.218.refs_2_, bf16[2048,512]{1,0:T(8,128)(2,1)} %copy-done.1, ...), custom_call_target="tpu_custom_call" | custom-call | bytes 67108864 | tf_op jit(solution)/shard_map/pallas_call | solution.py:230
  496.5 10.2 %collective-permute-done.46 = bf16[256,512]{1,0:T(8,128)(2,1)S(1)} collective-permute-done((bf16[256,512]{1,0:T(8,128)(2,1)S(1)}, bf16[256,512]{1,0:T(8,128)(2,1)S(1)}, u32[]{:S(2)}, u32[]{:S(2)}) %collective-permute-start.46) | collective-permute-done | bytes 262176 | tf_op jit(solution)/shard_map/ppermute | solution.py:550
  517.2 16.2 %collective-permute-done.47 = bf16[512,512]{1,0:T(8,128)(2,1)S(1)} collective-permute-done((bf16[512,512]{1,0:T(8,128)(2,1)S(1)}, bf16[512,512]{1,0:T(8,128)(2,1)S(1)}, u32[]{:S(2)}, u32[]{:S(2)}) %collective-permute-start.47) | collective-permute-done | bytes 524320 | tf_op jit(solution)/shard_map/ppermute | solution.py:550
  582.2 7.7 %collective-permute-done.55 = bf16[96,2304]{1,0:T(8,128)(2,1)} collective-permute-done((bf16[96,2304]{1,0:T(8,128)(2,1)}, bf16[96,2304]{1,0:T(8,128)(2,1)}, u32[]{:S(2)}, u32[]{:S(2)}) %collective-permute-start.55) | collective-permute-done | bytes 442400 | tf_op jit(solution)/shard_map/ppermute | solution.py:550
  (432 shorter events, 299.2 us)
Async XLA Ops:
  7.2 55.0 %all-gather.9.cloned.1.call-start = ((), (), s32[]{:S(2)}) async-start(), calls=%async_computation.7 | async-start | bytes 7962624 | tf_op jit(solution)/shard_map/all_gather | solution.py:633
  9.4 187.9 %all-gather.5.cloned.1.call-start = ((), (), s32[]{:S(2)}) async-start(), calls=%async_computation.3 | async-start | bytes 23887872 | tf_op jit(solution)/shard_map/all_gather | solution.py:637
  12.2 238.3 %all-gather.7.cloned.1.call-start = ((), (), s32[]{:S(2)}) async-start(), calls=%async_computation.4 | async-start | bytes 11943936 | tf_op jit(solution)/shard_map/all_gather | solution.py:638
  13.0 586.5 %reduce-scatter.5.cloned.1.call-start = ((), (), s32[]{:S(2)}) async-start(), calls=%async_computation.6 | async-start | bytes 6635520 | tf_op jit(solution)/shard_map/reduce_scatter | solution.py:771
  18.3 26.1 %collective-permute-start = (bf16[128,2304]{1,0:T(8,128)(2,1)S(1)}, bf16[128,2304]{1,0:T(8,128)(2,1)S(1)}, u32[]{:S(2)}, u32[]{:S(2)}) collective-permute-start(bf16[128,2304]{1,0:T(8,128)(2,1)S(1)} %bitcast.123), channel_id=1, source_target_pairs={{0,8},{8,16},{16,24},{24,0},{1,9},{9,17},{17,25},{25,1},{2,10},{10... | collective-permute-start | bytes 1769480 | tf_op jit(solution)/shard_map/ppermute | solution.py:506
  132.0 25.5 %collective-permute-start.15 = (bf16[128,2304]{1,0:T(8,128)(2,1)S(1)}, bf16[128,2304]{1,0:T(8,128)(2,1)S(1)}, u32[]{:S(2)}, u32[]{:S(2)}) collective-permute-start(bf16[128,2304]{1,0:T(8,128)(2,1)S(1)} %add_convert_fusion.5), channel_id=1, source_target_pairs={{0,24},{8,0},{16,8},{24,16},{1,25},{9,1},{17,9},{25,17},{2,26},{10... | collective-permute-start | bytes 1769480 | tf_op jit(solution)/shard_map/ppermute | solution.py:506
  159.6 27.9 %collective-permute-start.17 = (bf16[128,2304]{1,0:T(8,128)(2,1)S(1)}, bf16[128,2304]{1,0:T(8,128)(2,1)S(1)}, u32[]{:S(2)}, u32[]{:S(2)}) collective-permute-start(bf16[128,2304]{1,0:T(8,128)(2,1)S(1)} %multiply_convert_fusion), channel_id=1, source_target_pairs={{0,24},{8,0},{16,8},{24,16},{1,25},{9,1},{17,9},{25,17},{2,26},{10... | collective-permute-start | bytes 1769480 | tf_op jit(solution)/shard_map/ppermute | solution.py:506
  161.3 26.2 %collective-permute-start.16 = (bf16[128,2304]{1,0:T(8,128)(2,1)S(1)}, bf16[128,2304]{1,0:T(8,128)(2,1)}, u32[]{:S(2)}, u32[]{:S(2)}) collective-permute-start(bf16[128,2304]{1,0:T(8,128)(2,1)S(1)} %multiply_convert_fusion), channel_id=1, source_target_pairs={{0,8},{8,16},{16,24},{24,0},{1,9},{9,17},{17,25},{25,1},{2,10},{10... | collective-permute-start | bytes 1769480 | tf_op jit(solution)/shard_map/ppermute | solution.py:506
  276.0 30.4 %collective-permute-start.26 = (bf16[256,2304]{1,0:T(8,128)(2,1)S(1)}, bf16[256,2304]{1,0:T(8,128)(2,1)S(1)}, u32[]{:S(2)}, u32[]{:S(2)}) collective-permute-start(bf16[256,2304]{1,0:T(8,128)(2,1)S(1)} %copy-done.12), channel_id=1, source_target_pairs={{0,1},{1,0},{2,3},{3,2},{4,5},{5,4},{6,7},{7,6},{8,9},{9,8},{10,11... | collective-permute-start | bytes 3538952 | tf_op jit(solution)/shard_map/ppermute | solution.py:594
  276.3 30.1 %collective-permute-start.27 = (bf16[256,2304]{1,0:T(8,128)(2,1)S(1)}, bf16[256,2304]{1,0:T(8,128)(2,1)S(1)}, u32[]{:S(2)}, u32[]{:S(2)}) collective-permute-start(bf16[256,2304]{1,0:T(8,128)(2,1)S(1)} %copy-done.20), channel_id=1, source_target_pairs={{0,1},{1,0},{2,3},{3,2},{4,5},{5,4},{6,7},{7,6},{8,9},{9,8},{10,11... | collective-permute-start | bytes 3538952 | tf_op jit(solution)/shard_map/ppermute | solution.py:594
  278.1 28.3 %collective-permute-start.23 = (bf16[128,2304]{1,0:T(8,128)(2,1)S(1)}, bf16[128,2304]{1,0:T(8,128)(2,1)S(1)}, u32[]{:S(2)}, u32[]{:S(2)}) collective-permute-start(bf16[128,2304]{1,0:T(8,128)(2,1)S(1)} %add_convert_fusion.4), channel_id=1, source_target_pairs={{0,24},{8,0},{16,8},{24,16},{1,25},{9,1},{17,9},{25,17},{2,26},{10... | collective-permute-start | bytes 1769480 | tf_op jit(solution)/shard_map/ppermute | solution.py:506
  310.4 27.8 %collective-permute-start.29 = (bf16[128,2304]{1,0:T(8,128)(2,1)S(1)}, bf16[128,2304]{1,0:T(8,128)(2,1)S(1)}, u32[]{:S(2)}, u32[]{:S(2)}) collective-permute-start(bf16[128,2304]{1,0:T(8,128)(2,1)S(1)} %get-tuple-element.307), channel_id=1, source_target_pairs={{0,24},{8,0},{16,8},{24,16},{1,25},{9,1},{17,9},{25,17},{2,26},{10... | collective-permute-start | bytes 1769480 | tf_op jit(solution)/shard_map/ppermute | solution.py:506
  312.0 26.2 %collective-permute-start.28 = (bf16[128,2304]{1,0:T(8,128)(2,1)S(1)}, bf16[128,2304]{1,0:T(8,128)(2,1)S(1)}, u32[]{:S(2)}, u32[]{:S(2)}) collective-permute-start(bf16[128,2304]{1,0:T(8,128)(2,1)S(1)} %get-tuple-element.307), channel_id=1, source_target_pairs={{0,8},{8,16},{16,24},{24,0},{1,9},{9,17},{17,25},{25,1},{2,10},{10... | collective-permute-start | bytes 1769480 | tf_op jit(solution)/shard_map/ppermute | solution.py:506
  340.5 44.8 %collective-permute-start.34 = (bf16[256,2304]{1,0:T(8,128)(2,1)S(1)}, bf16[256,2304]{1,0:T(8,128)(2,1)}, u32[]{:S(2)}, u32[]{:S(2)}) collective-permute-start(bf16[256,2304]{1,0:T(8,128)(2,1)S(1)} %pad_maximum_fusion.5.rows_ref.refs_4_), channel_id=1, source_target_pairs={{0,1},{1,0},{2,3},{3,2},{4,5},{5,4},{6,7},{7,6},{8,9},{9,8},{10,11... | collective-permute-start | bytes 3538952 | tf_op jit(solution)/shard_map/ppermute | solution.py:594
  354.9 30.5 %collective-permute-start.35 = (bf16[256,2304]{1,0:T(8,128)(2,1)S(1)}, bf16[256,2304]{1,0:T(8,128)(2,1)}, u32[]{:S(2)}, u32[]{:S(2)}) collective-permute-start(bf16[256,2304]{1,0:T(8,128)(2,1)S(1)} %constant_dynamic-update-slice_fusion.16.rows_ref.refs_5_), channel_id=1, source_target_pairs={{0,1},{1,0},{2,3},{3,2},{4,5},{5,4},{6,7},{7,6},{8,9},{9,8},{10,11... | collective-permute-start | bytes 3538952 | tf_op jit(solution)/shard_map/ppermute | solution.py:594
  397.1 205.3 %reduce-scatter.3.cloned.1.call-start = ((), (), s32[]{:S(2)}) async-start(), calls=%async_computation.5 | async-start | bytes 13271040 | tf_op jit(solution)/shard_map/reduce_scatter | solution.py:772
  402.1 22.7 %collective-permute-start.36 = (bf16[128,2304]{1,0:T(8,128)(2,1)}, bf16[128,2304]{1,0:T(8,128)(2,1)}, u32[]{:S(2)}, u32[]{:S(2)}) collective-permute-start(bf16[128,2304]{1,0:T(8,128)(2,1)} %fusion.33), channel_id=1, source_target_pairs={{0,8},{8,16},{16,24},{24,0},{1,9},{9,17},{17,25},{25,1},{2,10},{10... | collective-permute-start | bytes 1769480 | tf_op jit(solution)/shard_map/ppermute | solution.py:506
  403.4 28.0 %collective-permute-start.37 = (bf16[128,2304]{1,0:T(8,128)(2,1)}, bf16[128,2304]{1,0:T(8,128)(2,1)}, u32[]{:S(2)}, u32[]{:S(2)}) collective-permute-start(bf16[128,2304]{1,0:T(8,128)(2,1)} %add_convert_fusion.2), channel_id=1, source_target_pairs={{0,24},{8,0},{16,8},{24,16},{1,25},{9,1},{17,9},{25,17},{2,26},{10... | collective-permute-start | bytes 1769480 | tf_op jit(solution)/shard_map/ppermute | solution.py:506
  438.5 25.9 %collective-permute-start.40 = (bf16[128,2304]{1,0:T(8,128)(2,1)S(1)}, bf16[128,2304]{1,0:T(8,128)(2,1)S(1)}, u32[]{:S(2)}, u32[]{:S(2)}) collective-permute-start(bf16[128,2304]{1,0:T(8,128)(2,1)S(1)} %subtract_convert_fusion), channel_id=1, source_target_pairs={{0,8},{8,16},{16,24},{24,0},{1,9},{9,17},{17,25},{25,1},{2,10},{10... | collective-permute-start | bytes 1769480 | tf_op jit(solution)/shard_map/ppermute | solution.py:506
  508.3 25.1 %collective-permute-start.47 = (bf16[512,512]{1,0:T(8,128)(2,1)S(1)}, bf16[512,512]{1,0:T(8,128)(2,1)S(1)}, u32[]{:S(2)}, u32[]{:S(2)}) collective-permute-start(bf16[512,512]{1,0:T(8,128)(2,1)S(1)} %get-tuple-element.297), channel_id=1, source_target_pairs={{0,4},{2,6},{4,0},{6,2},{1,5},{3,7},{5,1},{7,3},{8,12},{10,14},{12... | collective-permute-start | bytes 1572872 | tf_op jit(solution)/shard_map/ppermute | solution.py:550
  508.9 24.9 %collective-permute-start.45 = (bf16[512,512]{1,0:T(8,128)(2,1)S(1)}, bf16[512,512]{1,0:T(8,128)(2,1)S(1)}, u32[]{:S(2)}, u32[]{:S(2)}) collective-permute-start(bf16[512,512]{1,0:T(8,128)(2,1)S(1)} %get-tuple-element.298), channel_id=1, source_target_pairs={{0,2},{2,0},{4,6},{6,4},{1,3},{3,1},{5,7},{7,5},{8,10},{10,8},{12,... | collective-permute-start | bytes 1572872 | tf_op jit(solution)/shard_map/ppermute | solution.py:550
  562.0 30.7 %collective-permute-start.50 = (bf16[128,2304]{1,0:T(8,128)(2,1)}, bf16[128,2304]{1,0:T(8,128)(2,1)}, u32[]{:S(2)}, u32[]{:S(2)}) collective-permute-start(bf16[128,2304]{1,0:T(8,128)(2,1)} %add_convert_fusion.1), channel_id=1, source_target_pairs={{0,8},{8,16},{16,24},{24,0},{1,9},{9,17},{17,25},{25,1},{2,10},{10... | collective-permute-start | bytes 1769480 | tf_op jit(solution)/shard_map/ppermute | solution.py:506
  563.6 29.1 %collective-permute-start.51 = (bf16[128,2304]{1,0:T(8,128)(2,1)}, bf16[128,2304]{1,0:T(8,128)(2,1)}, u32[]{:S(2)}, u32[]{:S(2)}) collective-permute-start(bf16[128,2304]{1,0:T(8,128)(2,1)} %add_convert_fusion), channel_id=1, source_target_pairs={{0,24},{8,0},{16,8},{24,16},{1,25},{9,1},{17,9},{25,17},{2,26},{10... | collective-permute-start | bytes 1769480 | tf_op jit(solution)/shard_map/ppermute | solution.py:506
  592.7 21.6 %collective-permute-start.56 = (bf16[192,2304]{1,0:T(8,128)(2,1)}, bf16[192,2304]{1,0:T(8,128)(2,1)S(1)}, u32[]{:S(2)}, u32[]{:S(2)}) collective-permute-start(bf16[192,2304]{1,0:T(8,128)(2,1)} %get-tuple-element.256), channel_id=1, source_target_pairs={{0,2},{2,0},{4,6},{6,4},{1,3},{3,1},{5,7},{7,5},{8,10},{10,8},{12,... | collective-permute-start | bytes 2654216 | tf_op jit(solution)/shard_map/ppermute | solution.py:550
  (112 other events, 1223.2 us)
Sparse Core Ops, SparseCore 0:
  10.5 51.6 all-gather.8
  64.6 120.1 all-gather.4
  186.7 63.8 all-gather.6
  397.2 60.1 reduce-scatter.4
  460.4 121.9 reduce-scatter.2

commit v6 on v5

--- a/solution.py
+++ b/solution.py
@@ -720,16 +720,11 @@
 
     line_gather((hidden * inverse_three * scales[2]).astype(LOW), widen)
 
-    def keep(gate, _):
-        return (
-            [sibling(gate(part)) for part in mixed_away],
-            [sibling(gate(part)) for part in normed_second],
-        )
-
-    ffn_out, _, (mixed_theirs, second_theirs) = line_scatter(
-        contract(mixed[1], down_all, 0, 0),
-        lambda: (contract(mixed[0], down_all, 0, 0), ()),
-        while_last=keep,
+    mixed_theirs = [sibling(part) for part in mixed_away]
+    second_theirs = [sibling(part) for part in normed_second]
+    mixed[1] = tie(mixed[1], mixed_theirs, second_theirs)
+    ffn_out, _, _ = line_scatter(
+        contract(mixed[1], down_all, 0, 0), lambda: (contract(mixed[0], down_all, 0, 0), ())
     )
 
     inverse_four = inverse_root(ffn_out)

time: 637 us -> 631 us (level)
    unnamed x161 -> x157, local copies, waits for them, and re-layouts: 17.5 us -> 15.3 us
  transfers between devices with their start and end apart: 64 -> 64, of which waited for: 35 -> 35; matrix products, arithmetic and copies ran while one was open for 17% -> 17% of each run, Pallas kernels for 22% -> 23%
where the time goes in v6:
time: 631 us; the launch traced here: 622 us
  waiting for transfers between devices  259 us (41%)
  Pallas kernels  141 us (22%)
  starting transfers between devices  74.6 us (12%)
  other arithmetic  58.1 us (9%)
  local copies, waits for them, and re-layouts  42.1 us (7%)
  matrix products  31.9 us (5%)
  between operations  15.4 us (2%)
    ppermute x32, waiting for transfers between devices, shift(): lax.ppermute(value, 'line', [(at, (at + step) % count) for at in range(co...  179 us
    ppermute x16, waiting for transfers between devices, swap(): return lax.ppermute(value, 'plane', [(b, b ^ bits) for b in range(count)])  53.6 us
    ppermute x32, starting transfers between devices, shift(): lax.ppermute(value, 'line', [(at, (at + step) % count) for at in range(co...  52.1 us
    dot_general x7, matrix products, contract(): lax.dot_general(left, right, (((left_dim,), (right_dim,)), ((), ())), pre...  31.9 us
    pallas_call x2, Pallas kernels, weight_grad_call(): pl.pallas_call(weight_grad_kernel, grid_spec=pltpu.PrefetchScalarGridSpec...  27.2 us
    pallas_call x2, Pallas kernels, widen_call(): pl.pallas_call(functools.partial(widen_kernel, sharers // STEPS), grid_sp...  26.6 us
    all_gather x1, waiting for transfers between devices, shards(): lax.all_gather(down_weight, ('fsdp', 'plane'), axis=0, tiled=True)  20 us
    pallas_call x2, Pallas kernels, attend_back_call(): pl.pallas_call(attend_back_kernel, grid=(keys // block, group_size), in_s...  20 us
  transfers between devices with their start and end apart: 64, of which 35 were waited for; matrix products, arithmetic and copies ran while one was open for 17% of the time, Pallas kernels for 23%

profile of v6, /device:TPU:0, one launch (start us, length us, event | category | flops | bytes accessed | tf_op | source)
XLA Modules:
  0.0 621.9 jit_solution(17769690833326451473)
XLA Ops:
  23.2 8.9 %collective-permute-done.1 = bf16[128,2304]{1,0:T(8,128)(2,1)S(1)} collective-permute-done((bf16[128,2304]{1,0:T(8,128)(2,1)S(1)}, bf16[128,2304]{1,0:T(8,128)(2,1)S(1)}, u32[]{:S(2)}, u32[]{:S(2)}) %collective-permute-start.1) | collective-permute-done | bytes 589856 | tf_op jit(solution)/shard_map/ppermute | solution.py:506
  32.0 12.4 %collective-permute-done = bf16[128,2304]{1,0:T(8,128)(2,1)S(1)} collective-permute-done((bf16[128,2304]{1,0:T(8,128)(2,1)S(1)}, bf16[128,2304]{1,0:T(8,128)(2,1)S(1)}, u32[]{:S(2)}, u32[]{:S(2)}) %collective-permute-start) | collective-permute-done | bytes 589856 | tf_op jit(solution)/shard_map/ppermute | solution.py:506
  96.4 7.6 %collective-permute-done.6 = bf16[128,512]{1,0:T(8,128)(2,1)S(1)} collective-permute-done((bf16[128,512]{1,0:T(8,128)(2,1)S(1)}, bf16[128,512]{1,0:T(8,128)(2,1)S(1)}, u32[]{:S(2)}, u32[]{:S(2)}) %collective-permute-start.6) | collective-permute-done | bytes 131104 | tf_op jit(solution)/shard_map/ppermute | solution.py:550
  137.6 11.0 %collective-permute-done.14 = bf16[128,2304]{1,0:T(8,128)(2,1)S(1)} collective-permute-done((bf16[128,2304]{1,0:T(8,128)(2,1)S(1)}, bf16[128,2304]{1,0:T(8,128)(2,1)S(1)}, u32[]{:S(2)}, u32[]{:S(2)}) %collective-permute-start.14) | collective-permute-done | bytes 589856 | tf_op jit(solution)/shard_map/ppermute | solution.py:506
  148.6 8.9 %collective-permute-done.15 = bf16[128,2304]{1,0:T(8,128)(2,1)S(1)} collective-permute-done((bf16[128,2304]{1,0:T(8,128)(2,1)S(1)}, bf16[128,2304]{1,0:T(8,128)(2,1)S(1)}, u32[]{:S(2)}, u32[]{:S(2)}) %collective-permute-start.15) | collective-permute-done | bytes 589856 | tf_op jit(solution)/shard_map/ppermute | solution.py:506
  161.8 25.8 %collective-permute-done.17 = bf16[128,2304]{1,0:T(8,128)(2,1)S(1)} collective-permute-done((bf16[128,2304]{1,0:T(8,128)(2,1)S(1)}, bf16[128,2304]{1,0:T(8,128)(2,1)S(1)}, u32[]{:S(2)}, u32[]{:S(2)}) %collective-permute-start.17) | collective-permute-done | bytes 589856 | tf_op jit(solution)/shard_map/ppermute | solution.py:506
  196.8 13.1 %shard_map.199 = (bf16[2304,256]{1,0:T(8,128)(2,1)}, bf16[1152,256]{1,0:T(8,128)(2,1)}, f32[2304,256]{1,0:T(8,128)}, f32[2304,256]{1,0:T(8,128)}) custom-call(s32[1]{0:T(128)} %bitcast.19.core_ref, bf16[256,2304]{1,0:T(8,128)(2,1)} %copy-done.13, bf16[4608,2304]{1,0:T(8,128)(2,1)} %all-gather.5.cloned.1.call-done.weight_ref), custom_call_target="tpu_custom_call" | custom-call | bytes 67108864 | tf_op jit(solution)/shard_map/pallas_call | solution.py:338
  212.9 13.6 %shard_map.200 = (bf16[2304,256]{1,0:T(8,128)(2,1)}, bf16[1152,256]{1,0:T(8,128)(2,1)}, f32[2304,256]{1,0:T(8,128)}, f32[2304,256]{1,0:T(8,128)}) custom-call(s32[1]{0:T(128)} %bitcast.19.core_ref, bf16[256,2304]{1,0:T(8,128)(2,1)} %copy-done.21, bf16[4608,2304]{1,0:T(8,128)(2,1)} %all-gather.5.cloned.1.call-done.weight_ref), custom_call_target="tpu_custom_call" | custom-call | bytes 67108864 | tf_op jit(solution)/shard_map/pallas_call | solution.py:338
  230.6 20.0 %all-gather.7.cloned.1.call-done.weight_ref = bf16[2304,2304]{1,0:T(8,128)(2,1)} async-done(((bf16[288,2304]{1,0:T(8,128)(2,1)}), bf16[2304,2304]{1,0:T(8,128)(2,1)}) %all-gather.7.cloned.1.call-update) | async-done | bytes 10616848 | tf_op jit(solution)/shard_map/all_gather | solution.py:638
  278.6 14.2 %collective-permute-done.26 = bf16[128,2304]{1,0:T(8,128)(2,1)S(1)} collective-permute-done((bf16[128,2304]{1,0:T(8,128)(2,1)S(1)}, bf16[128,2304]{1,0:T(8,128)(2,1)S(1)}, u32[]{:S(2)}, u32[]{:S(2)}) %collective-permute-start.26) | collective-permute-done | bytes 589856 | tf_op jit(solution)/shard_map/ppermute | solution.py:506
  292.8 10.5 %collective-permute-done.27 = bf16[128,2304]{1,0:T(8,128)(2,1)S(1)} collective-permute-done((bf16[128,2304]{1,0:T(8,128)(2,1)S(1)}, bf16[128,2304]{1,0:T(8,128)(2,1)S(1)}, u32[]{:S(2)}, u32[]{:S(2)}) %collective-permute-start.27) | collective-permute-done | bytes 589856 | tf_op jit(solution)/shard_map/ppermute | solution.py:506
  307.3 25.1 %collective-permute-done.29 = bf16[128,2304]{1,0:T(8,128)(2,1)S(1)} collective-permute-done((bf16[128,2304]{1,0:T(8,128)(2,1)S(1)}, bf16[128,2304]{1,0:T(8,128)(2,1)S(1)}, u32[]{:S(2)}, u32[]{:S(2)}) %collective-permute-start.29) | collective-permute-done | bytes 589856 | tf_op jit(solution)/shard_map/ppermute | solution.py:506
  334.8 9.2 %shard_map.201 = (bf16[4608,256]{1,0:T(8,128)(2,1)}, bf16[2304,256]{1,0:T(8,128)(2,1)}) custom-call(s32[1]{0:T(128)} %bitcast.19.core_ref, bf16[256,2304]{1,0:T(8,128)(2,1)} %copy-done.14, bf16[2304,2304]{1,0:T(8,128)(2,1)} %all-gather.7.cloned.1.call-done.weight_ref, f32[2304,256]{1,0:T(8,128)} %get-tuple-element.170.bent_ref, ...), custom_call_target="tpu_custom_call" | custom-call | bytes 67108864 | tf_op jit(solution)/shard_map/pallas_call | solution.py:382
  349.1 9.3 %shard_map.202 = (bf16[4608,256]{1,0:T(8,128)(2,1)}, bf16[2304,256]{1,0:T(8,128)(2,1)}) custom-call(s32[1]{0:T(128)} %bitcast.19.core_ref, bf16[256,2304]{1,0:T(8,128)(2,1)} %copy-done.22, bf16[2304,2304]{1,0:T(8,128)(2,1)} %all-gather.7.cloned.1.call-done.weight_ref, f32[2304,256]{1,0:T(8,128)} %get-tuple-element.176.bent_ref, ...), custom_call_target="tpu_custom_call" | custom-call | bytes 67108864 | tf_op jit(solution)/shard_map/pallas_call | solution.py:382
  358.4 15.7 %fusion.58 = (bf16[512,2304]{1,0:T(8,128)(2,1)S(1)}, f32[512,2304]{1,0:T(8,128)S(1)}) fusion(bf16[4608,2304]{1,0:T(8,128)(2,1)} %all-gather.5.cloned.1.call-done.weight_ref, bf16[4608,256]{1,0:T(8,128)(2,1)} %get-tuple-element.187.refs_1_, bf16[4608,256]{1,0:T(8,128)(2,1)S(1)} %copy-done.29), kind=kOutput, calls=%fused_computation.208 | convolution fusion | flops 10882252800 | bytes 33030144 | tf_op jit(solution)/shard_map/dot_general | solution.py:25
  378.7 10.4 %shard_map.203 = bf16[1152,2304]{1,0:T(8,128)(2,1)} custom-call(s32[1]{0:T(128)} %bitcast.19.core_ref, bf16[2304,256]{1,0:T(8,128)(2,1)} %get-tuple-element.179.refs_0_, bf16[2304,256]{1,0:T(8,128)(2,1)} %get-tuple-element.180.refs_1_, bf16[1152,256]{1,0:T(8,128)(2,1)} %copy-done.43, bf16[1152,256]{1,0:T(8,128)(2,1)} %copy-done.44, ...), custom_call_target="tpu_custom_call" | custom-call | bytes 67108864 | tf_op jit(solution)/shard_map/pallas_call | solution.py:432
  401.9 16.8 %shard_map.204 = bf16[2304,2304]{1,0:T(8,128)(2,1)} custom-call(s32[1]{0:T(128)} %bitcast.19.core_ref, bf16[4608,256]{1,0:T(8,128)(2,1)} %get-tuple-element.186.refs_0_, bf16[4608,256]{1,0:T(8,128)(2,1)} %get-tuple-element.187.refs_1_, bf16[2304,256]{1,0:T(8,128)(2,1)} %copy-done.41, bf16[2304,256]{1,0:T(8,128)(2,1)} %copy-done.42, ...), custom_call_target="tpu_custom_call" | custom-call | bytes 67108864 | tf_op jit(solution)/shard_map/pallas_call | solution.py:432
  435.8 10.5 %collective-permute-done.41 = bf16[128,2304]{1,0:T(8,128)(2,1)S(1)} collective-permute-done((bf16[128,2304]{1,0:T(8,128)(2,1)S(1)}, bf16[128,2304]{1,0:T(8,128)(2,1)S(1)}, u32[]{:S(2)}, u32[]{:S(2)}) %collective-permute-start.41) | collective-permute-done | bytes 589856 | tf_op jit(solution)/shard_map/ppermute | solution.py:506
  446.3 11.9 %collective-permute-done.40 = bf16[128,2304]{1,0:T(8,128)(2,1)S(1)} collective-permute-done((bf16[128,2304]{1,0:T(8,128)(2,1)S(1)}, bf16[128,2304]{1,0:T(8,128)(2,1)S(1)}, u32[]{:S(2)}, u32[]{:S(2)}) %collective-permute-start.40) | collective-permute-done | bytes 589856 | tf_op jit(solution)/shard_map/ppermute | solution.py:506
  463.7 9.6 %shard_map.205 = (bf16[256,512]{1,0:T(8,128)(2,1)}, f32[2048,512]{1,0:T(8,128)}) custom-call(bf16[512,256]{1,0:T(8,128)(2,1)} %get-tuple-element.143.query_ref.refs_0_, bf16[256,512]{1,0:T(8,128)(2,1)} %convolution_convert_fusion.1.refs_1_, f32[256,512]{1,0:T(8,128)} %get-tuple-element.197.refs_2_, bf16[2048,512]{1,0:T(8,128)(2,1)} %copy-done.2, ...), custom_call_target="tpu_custom_call" | custom-call | bytes 67108864 | tf_op jit(solution)/shard_map/pallas_call | solution.py:230
  474.9 10.4 %shard_map.206 = (bf16[256,512]{1,0:T(8,128)(2,1)}, bf16[2048,512]{1,0:T(8,128)(2,1)}) custom-call(bf16[512,256]{1,0:T(8,128)(2,1)} %get-tuple-element.136.query_ref.refs_0_, bf16[256,512]{1,0:T(8,128)(2,1)} %convolution_convert_fusion.refs_1_, f32[256,512]{1,0:T(8,128)} %get-tuple-element.204.refs_2_, bf16[2048,512]{1,0:T(8,128)(2,1)} %copy-done.2, ...), custom_call_target="tpu_custom_call" | custom-call | bytes 67108864 | tf_op jit(solution)/shard_map/pallas_call | solution.py:230
  490.4 10.4 %collective-permute-done.46 = bf16[256,512]{1,0:T(8,128)(2,1)S(1)} collective-permute-done((bf16[256,512]{1,0:T(8,128)(2,1)S(1)}, bf16[256,512]{1,0:T(8,128)(2,1)S(1)}, u32[]{:S(2)}, u32[]{:S(2)}) %collective-permute-start.46) | collective-permute-done | bytes 262176 | tf_op jit(solution)/shard_map/ppermute | solution.py:550
  511.2 16.3 %collective-permute-done.47 = bf16[512,512]{1,0:T(8,128)(2,1)S(1)} collective-permute-done((bf16[512,512]{1,0:T(8,128)(2,1)S(1)}, bf16[512,512]{1,0:T(8,128)(2,1)S(1)}, u32[]{:S(2)}, u32[]{:S(2)}) %collective-permute-start.47) | collective-permute-done | bytes 524320 | tf_op jit(solution)/shard_map/ppermute | solution.py:550
  576.3 7.5 %collective-permute-done.55 = bf16[96,2304]{1,0:T(8,128)(2,1)} collective-permute-done((bf16[96,2304]{1,0:T(8,128)(2,1)}, bf16[96,2304]{1,0:T(8,128)(2,1)}, u32[]{:S(2)}, u32[]{:S(2)}) %collective-permute-start.55) | collective-permute-done | bytes 442400 | tf_op jit(solution)/shard_map/ppermute | solution.py:550
  (427 shorter events, 297.3 us)
Async XLA Ops:
  7.2 55.0 %all-gather.9.cloned.1.call-start = ((), (), s32[]{:S(2)}) async-start(), calls=%async_computation.7 | async-start | bytes 7962624 | tf_op jit(solution)/shard_map/all_gather | solution.py:633
  9.4 187.2 %all-gather.5.cloned.1.call-start = ((), (), s32[]{:S(2)}) async-start(), calls=%async_computation.3 | async-start | bytes 23887872 | tf_op jit(solution)/shard_map/all_gather | solution.py:637
  12.2 238.3 %all-gather.7.cloned.1.call-start = ((), (), s32[]{:S(2)}) async-start(), calls=%async_computation.4 | async-start | bytes 11943936 | tf_op jit(solution)/shard_map/all_gather | solution.py:638
  13.0 580.6 %reduce-scatter.5.cloned.1.call-start = ((), (), s32[]{:S(2)}) async-start(), calls=%async_computation.6 | async-start | bytes 6635520 | tf_op jit(solution)/shard_map/reduce_scatter | solution.py:766
  18.3 26.1 %collective-permute-start = (bf16[128,2304]{1,0:T(8,128)(2,1)S(1)}, bf16[128,2304]{1,0:T(8,128)(2,1)S(1)}, u32[]{:S(2)}, u32[]{:S(2)}) collective-permute-start(bf16[128,2304]{1,0:T(8,128)(2,1)S(1)} %bitcast.121), channel_id=1, source_target_pairs={{0,8},{8,16},{16,24},{24,0},{1,9},{9,17},{17,25},{25,1},{2,10},{10... | collective-permute-start | bytes 1769480 | tf_op jit(solution)/shard_map/ppermute | solution.py:506
  132.0 25.5 %collective-permute-start.15 = (bf16[128,2304]{1,0:T(8,128)(2,1)S(1)}, bf16[128,2304]{1,0:T(8,128)(2,1)S(1)}, u32[]{:S(2)}, u32[]{:S(2)}) collective-permute-start(bf16[128,2304]{1,0:T(8,128)(2,1)S(1)} %add_convert_fusion.5), channel_id=1, source_target_pairs={{0,24},{8,0},{16,8},{24,16},{1,25},{9,1},{17,9},{25,17},{2,26},{10... | collective-permute-start | bytes 1769480 | tf_op jit(solution)/shard_map/ppermute | solution.py:506
  159.7 27.9 %collective-permute-start.17 = (bf16[128,2304]{1,0:T(8,128)(2,1)S(1)}, bf16[128,2304]{1,0:T(8,128)(2,1)S(1)}, u32[]{:S(2)}, u32[]{:S(2)}) collective-permute-start(bf16[128,2304]{1,0:T(8,128)(2,1)S(1)} %multiply_convert_fusion), channel_id=1, source_target_pairs={{0,24},{8,0},{16,8},{24,16},{1,25},{9,1},{17,9},{25,17},{2,26},{10... | collective-permute-start | bytes 1769480 | tf_op jit(solution)/shard_map/ppermute | solution.py:506
  161.4 26.2 %collective-permute-start.16 = (bf16[128,2304]{1,0:T(8,128)(2,1)S(1)}, bf16[128,2304]{1,0:T(8,128)(2,1)}, u32[]{:S(2)}, u32[]{:S(2)}) collective-permute-start(bf16[128,2304]{1,0:T(8,128)(2,1)S(1)} %multiply_convert_fusion), channel_id=1, source_target_pairs={{0,8},{8,16},{16,24},{24,0},{1,9},{9,17},{17,25},{25,1},{2,10},{10... | collective-permute-start | bytes 1769480 | tf_op jit(solution)/shard_map/ppermute | solution.py:506
  195.5 31.3 %collective-permute-start.22 = (bf16[256,2304]{1,0:T(8,128)(2,1)S(1)}, bf16[256,2304]{1,0:T(8,128)(2,1)}, u32[]{:S(2)}, u32[]{:S(2)}) collective-permute-start(bf16[256,2304]{1,0:T(8,128)(2,1)S(1)} %pad_maximum_fusion.4.rows_ref.refs_4_), channel_id=1, source_target_pairs={{0,1},{1,0},{2,3},{3,2},{4,5},{5,4},{6,7},{7,6},{8,9},{9,8},{10,11... | collective-permute-start | bytes 3538952 | tf_op jit(solution)/shard_map/ppermute | solution.py:594
  276.3 27.0 %collective-permute-start.27 = (bf16[128,2304]{1,0:T(8,128)(2,1)S(1)}, bf16[128,2304]{1,0:T(8,128)(2,1)S(1)}, u32[]{:S(2)}, u32[]{:S(2)}) collective-permute-start(bf16[128,2304]{1,0:T(8,128)(2,1)S(1)} %add_convert_fusion.4), channel_id=1, source_target_pairs={{0,24},{8,0},{16,8},{24,16},{1,25},{9,1},{17,9},{25,17},{2,26},{10... | collective-permute-start | bytes 1769480 | tf_op jit(solution)/shard_map/ppermute | solution.py:506
  305.2 27.2 %collective-permute-start.29 = (bf16[128,2304]{1,0:T(8,128)(2,1)S(1)}, bf16[128,2304]{1,0:T(8,128)(2,1)S(1)}, u32[]{:S(2)}, u32[]{:S(2)}) collective-permute-start(bf16[128,2304]{1,0:T(8,128)(2,1)S(1)} %get-tuple-element.293), channel_id=1, source_target_pairs={{0,24},{8,0},{16,8},{24,16},{1,25},{9,1},{17,9},{25,17},{2,26},{10... | collective-permute-start | bytes 1769480 | tf_op jit(solution)/shard_map/ppermute | solution.py:506
  307.3 25.1 %collective-permute-start.28 = (bf16[128,2304]{1,0:T(8,128)(2,1)S(1)}, bf16[128,2304]{1,0:T(8,128)(2,1)S(1)}, u32[]{:S(2)}, u32[]{:S(2)}) collective-permute-start(bf16[128,2304]{1,0:T(8,128)(2,1)S(1)} %get-tuple-element.293), channel_id=1, source_target_pairs={{0,8},{8,16},{16,24},{24,0},{1,9},{9,17},{17,25},{25,1},{2,10},{10... | collective-permute-start | bytes 1769480 | tf_op jit(solution)/shard_map/ppermute | solution.py:506
  334.8 43.9 %collective-permute-start.34 = (bf16[256,2304]{1,0:T(8,128)(2,1)S(1)}, bf16[256,2304]{1,0:T(8,128)(2,1)}, u32[]{:S(2)}, u32[]{:S(2)}) collective-permute-start(bf16[256,2304]{1,0:T(8,128)(2,1)S(1)} %pad_maximum_fusion.5.rows_ref.refs_4_), channel_id=1, source_target_pairs={{0,1},{1,0},{2,3},{3,2},{4,5},{5,4},{6,7},{7,6},{8,9},{9,8},{10,11... | collective-permute-start | bytes 3538952 | tf_op jit(solution)/shard_map/ppermute | solution.py:594
  348.1 30.6 %collective-permute-start.35 = (bf16[256,2304]{1,0:T(8,128)(2,1)S(1)}, bf16[256,2304]{1,0:T(8,128)(2,1)}, u32[]{:S(2)}, u32[]{:S(2)}) collective-permute-start(bf16[256,2304]{1,0:T(8,128)(2,1)S(1)} %constant_dynamic-update-slice_fusion.16.rows_ref.refs_5_), channel_id=1, source_target_pairs={{0,1},{1,0},{2,3},{3,2},{4,5},{5,4},{6,7},{7,6},{8,9},{9,8},{10,11... | collective-permute-start | bytes 3538952 | tf_op jit(solution)/shard_map/ppermute | solution.py:594
  391.0 205.5 %reduce-scatter.3.cloned.1.call-start = ((), (), s32[]{:S(2)}) async-start(), calls=%async_computation.5 | async-start | bytes 13271040 | tf_op jit(solution)/shard_map/reduce_scatter | solution.py:767
  396.0 22.7 %collective-permute-start.36 = (bf16[128,2304]{1,0:T(8,128)(2,1)}, bf16[128,2304]{1,0:T(8,128)(2,1)}, u32[]{:S(2)}, u32[]{:S(2)}) collective-permute-start(bf16[128,2304]{1,0:T(8,128)(2,1)} %fusion.33), channel_id=1, source_target_pairs={{0,8},{8,16},{16,24},{24,0},{1,9},{9,17},{17,25},{25,1},{2,10},{10... | collective-permute-start | bytes 1769480 | tf_op jit(solution)/shard_map/ppermute | solution.py:506
  397.5 28.0 %collective-permute-start.37 = (bf16[128,2304]{1,0:T(8,128)(2,1)}, bf16[128,2304]{1,0:T(8,128)(2,1)}, u32[]{:S(2)}, u32[]{:S(2)}) collective-permute-start(bf16[128,2304]{1,0:T(8,128)(2,1)} %add_convert_fusion.2), channel_id=1, source_target_pairs={{0,24},{8,0},{16,8},{24,16},{1,25},{9,1},{17,9},{25,17},{2,26},{10... | collective-permute-start | bytes 1769480 | tf_op jit(solution)/shard_map/ppermute | solution.py:506
  432.5 25.7 %collective-permute-start.40 = (bf16[128,2304]{1,0:T(8,128)(2,1)S(1)}, bf16[128,2304]{1,0:T(8,128)(2,1)S(1)}, u32[]{:S(2)}, u32[]{:S(2)}) collective-permute-start(bf16[128,2304]{1,0:T(8,128)(2,1)S(1)} %subtract_convert_fusion), channel_id=1, source_target_pairs={{0,8},{8,16},{16,24},{24,0},{1,9},{9,17},{17,25},{25,1},{2,10},{10... | collective-permute-start | bytes 1769480 | tf_op jit(solution)/shard_map/ppermute | solution.py:506
  502.3 25.2 %collective-permute-start.47 = (bf16[512,512]{1,0:T(8,128)(2,1)S(1)}, bf16[512,512]{1,0:T(8,128)(2,1)S(1)}, u32[]{:S(2)}, u32[]{:S(2)}) collective-permute-start(bf16[512,512]{1,0:T(8,128)(2,1)S(1)} %get-tuple-element.283), channel_id=1, source_target_pairs={{0,4},{2,6},{4,0},{6,2},{1,5},{3,7},{5,1},{7,3},{8,12},{10,14},{12... | collective-permute-start | bytes 1572872 | tf_op jit(solution)/shard_map/ppermute | solution.py:550
  502.9 25.0 %collective-permute-start.45 = (bf16[512,512]{1,0:T(8,128)(2,1)S(1)}, bf16[512,512]{1,0:T(8,128)(2,1)S(1)}, u32[]{:S(2)}, u32[]{:S(2)}) collective-permute-start(bf16[512,512]{1,0:T(8,128)(2,1)S(1)} %get-tuple-element.284), channel_id=1, source_target_pairs={{0,2},{2,0},{4,6},{6,4},{1,3},{3,1},{5,7},{7,5},{8,10},{10,8},{12,... | collective-permute-start | bytes 1572872 | tf_op jit(solution)/shard_map/ppermute | solution.py:550
  556.1 30.7 %collective-permute-start.50 = (bf16[128,2304]{1,0:T(8,128)(2,1)}, bf16[128,2304]{1,0:T(8,128)(2,1)}, u32[]{:S(2)}, u32[]{:S(2)}) collective-permute-start(bf16[128,2304]{1,0:T(8,128)(2,1)} %add_convert_fusion.1), channel_id=1, source_target_pairs={{0,8},{8,16},{16,24},{24,0},{1,9},{9,17},{17,25},{25,1},{2,10},{10... | collective-permute-start | bytes 1769480 | tf_op jit(solution)/shard_map/ppermute | solution.py:506
  556.6 30.2 %collective-permute-start.51 = (bf16[128,2304]{1,0:T(8,128)(2,1)}, bf16[128,2304]{1,0:T(8,128)(2,1)}, u32[]{:S(2)}, u32[]{:S(2)}) collective-permute-start(bf16[128,2304]{1,0:T(8,128)(2,1)} %add_convert_fusion), channel_id=1, source_target_pairs={{0,24},{8,0},{16,8},{24,16},{1,25},{9,1},{17,9},{25,17},{2,26},{10... | collective-permute-start | bytes 1769480 | tf_op jit(solution)/shard_map/ppermute | solution.py:506
  586.8 21.5 %collective-permute-start.56 = (bf16[192,2304]{1,0:T(8,128)(2,1)}, bf16[192,2304]{1,0:T(8,128)(2,1)S(1)}, u32[]{:S(2)}, u32[]{:S(2)}) collective-permute-start(bf16[192,2304]{1,0:T(8,128)(2,1)} %get-tuple-element.242), channel_id=1, source_target_pairs={{0,2},{2,0},{4,6},{6,4},{1,3},{3,1},{5,7},{7,5},{8,10},{10,8},{12,... | collective-permute-start | bytes 2654216 | tf_op jit(solution)/shard_map/ppermute | solution.py:550
  588.0 21.4 %collective-permute-start.57 = (bf16[192,2304]{1,0:T(8,128)(2,1)}, bf16[192,2304]{1,0:T(8,128)(2,1)S(1)}, u32[]{:S(2)}, u32[]{:S(2)}) collective-permute-start(bf16[192,2304]{1,0:T(8,128)(2,1)} %get-tuple-element.243), channel_id=1, source_target_pairs={{0,4},{2,6},{4,0},{6,2},{1,5},{3,7},{5,1},{7,3},{8,12},{10,14},{12... | collective-permute-start | bytes 2654216 | tf_op jit(solution)/shard_map/ppermute | solution.py:550
  (110 other events, 1167.7 us)
Sparse Core Ops, SparseCore 0:
  10.5 51.6 all-gather.8
  64.6 120.1 all-gather.4
  186.7 63.8 all-gather.6
  391.1 60.3 reduce-scatter.4
  454.5 121.9 reduce-scatter.2

commit v7 on v6

--- a/solution.py
+++ b/solution.py
@@ -316,9 +316,10 @@
     bent = gate * rise
     mixed = (bent * up).astype(LOW)
     mixed_ref[...] = mixed
-    bent_ref[...] = bent
+    bent_ref[...] = bent.astype(LOW)
     steep = GELU_ROOT * (1.0 + 3.0 * GELU_CUBE * square)
-    slope_ref[...] = up * (rise + 0.5 * gate * (1.0 - curve * curve) * steep)
+    slope = up * (rise + 0.5 * gate * (1.0 - curve * curve) * steep)
+    slope_ref[...] = slope.astype(LOW)
 
     @pl.when(step // (STEPS // 2) != core_ref[0])
     def _():
@@ -349,8 +350,8 @@
         out_shape=(
             jax.ShapeDtypeStruct((amount, span), LOW),
             jax.ShapeDtypeStruct((amount // 2, span), LOW),
-            jax.ShapeDtypeStruct((amount, span), WIDE),
-            jax.ShapeDtypeStruct((amount, span), WIDE),
+            jax.ShapeDtypeStruct((amount, span), LOW),
+            jax.ShapeDtypeStruct((amount, span), LOW),
         ),
         compiler_params=params(),
         cost_estimate=COST,
@@ -362,7 +363,8 @@
 ):
     step = pl.program_id(0)
     mixed_grad = contract(weight_ref[...], rows_ref[...], 1, 1)
-    gate, up = mixed_grad * slope_ref[...], mixed_grad * bent_ref[...]
+    gate = mixed_grad * slope_ref[...].astype(WIDE)
+    up = mixed_grad * bent_ref[...].astype(WIDE)
     rows = gate.shape[0] // parts
     grad = jnp.concatenate(
         [part[p * rows : (p + 1) * rows] for p in range(parts) for part in (gate, up)], axis=0

time: 631 us -> 630 us (level)
  transfers between devices with their start and end apart: 64 -> 64, of which waited for: 35 -> 35; matrix products, arithmetic and copies ran while one was open for 17% -> 17% of each run, Pallas kernels for 23% -> 22%
where the time goes in v7:
time: 630 us; the launch traced here: 621 us
  waiting for transfers between devices  260 us (41%)
  Pallas kernels  139 us (22%)
  starting transfers between devices  74.5 us (12%)
  other arithmetic  58.1 us (9%)
  local copies, waits for them, and re-layouts  42.3 us (7%)
  matrix products  31.9 us (5%)
  between operations  15.4 us (2%)
    ppermute x32, waiting for transfers between devices, shift(): lax.ppermute(value, 'line', [(at, (at + step) % count) for at in range(co...  179 us
    ppermute x16, waiting for transfers between devices, swap(): return lax.ppermute(value, 'plane', [(b, b ^ bits) for b in range(count)])  53.4 us
    ppermute x32, starting transfers between devices, shift(): lax.ppermute(value, 'line', [(at, (at + step) % count) for at in range(co...  52.1 us
    dot_general x7, matrix products, contract(): lax.dot_general(left, right, (((left_dim,), (right_dim,)), ((), ())), pre...  31.9 us
    pallas_call x2, Pallas kernels, weight_grad_call(): pl.pallas_call(weight_grad_kernel, grid_spec=pltpu.PrefetchScalarGridSpec...  27.2 us
    pallas_call x2, Pallas kernels, widen_call(): pl.pallas_call(functools.partial(widen_kernel, sharers // STEPS), grid_sp...  26.2 us
    all_gather x1, waiting for transfers between devices, shards(): lax.all_gather(down_weight, ('fsdp', 'plane'), axis=0, tiled=True)  20.4 us
    pallas_call x2, Pallas kernels, attend_back_call(): pl.pallas_call(attend_back_kernel, grid=(keys // block, group_size), in_s...  20 us
  transfers between devices with their start and end apart: 64, of which 35 were waited for; matrix products, arithmetic and copies ran while one was open for 17% of the time, Pallas kernels for 22%

profile of v7, /device:TPU:0, one launch (start us, length us, event | category | flops | bytes accessed | tf_op | source)
XLA Modules:
  0.0 621.4 jit_solution(9546531388606107069)
XLA Ops:
  23.2 8.8 %collective-permute-done.1 = bf16[128,2304]{1,0:T(8,128)(2,1)S(1)} collective-permute-done((bf16[128,2304]{1,0:T(8,128)(2,1)S(1)}, bf16[128,2304]{1,0:T(8,128)(2,1)S(1)}, u32[]{:S(2)}, u32[]{:S(2)}) %collective-permute-start.1) | collective-permute-done | bytes 589856 | tf_op jit(solution)/shard_map/ppermute | solution.py:508
  32.0 12.4 %collective-permute-done = bf16[128,2304]{1,0:T(8,128)(2,1)S(1)} collective-permute-done((bf16[128,2304]{1,0:T(8,128)(2,1)S(1)}, bf16[128,2304]{1,0:T(8,128)(2,1)S(1)}, u32[]{:S(2)}, u32[]{:S(2)}) %collective-permute-start) | collective-permute-done | bytes 589856 | tf_op jit(solution)/shard_map/ppermute | solution.py:508
  96.3 7.6 %collective-permute-done.6 = bf16[128,512]{1,0:T(8,128)(2,1)S(1)} collective-permute-done((bf16[128,512]{1,0:T(8,128)(2,1)S(1)}, bf16[128,512]{1,0:T(8,128)(2,1)S(1)}, u32[]{:S(2)}, u32[]{:S(2)}) %collective-permute-start.6) | collective-permute-done | bytes 131104 | tf_op jit(solution)/shard_map/ppermute | solution.py:552
  137.5 11.0 %collective-permute-done.14 = bf16[128,2304]{1,0:T(8,128)(2,1)S(1)} collective-permute-done((bf16[128,2304]{1,0:T(8,128)(2,1)S(1)}, bf16[128,2304]{1,0:T(8,128)(2,1)S(1)}, u32[]{:S(2)}, u32[]{:S(2)}) %collective-permute-start.14) | collective-permute-done | bytes 589856 | tf_op jit(solution)/shard_map/ppermute | solution.py:508
  148.5 8.9 %collective-permute-done.15 = bf16[128,2304]{1,0:T(8,128)(2,1)S(1)} collective-permute-done((bf16[128,2304]{1,0:T(8,128)(2,1)S(1)}, bf16[128,2304]{1,0:T(8,128)(2,1)S(1)}, u32[]{:S(2)}, u32[]{:S(2)}) %collective-permute-start.15) | collective-permute-done | bytes 589856 | tf_op jit(solution)/shard_map/ppermute | solution.py:508
  161.7 25.8 %collective-permute-done.17 = bf16[128,2304]{1,0:T(8,128)(2,1)S(1)} collective-permute-done((bf16[128,2304]{1,0:T(8,128)(2,1)S(1)}, bf16[128,2304]{1,0:T(8,128)(2,1)S(1)}, u32[]{:S(2)}, u32[]{:S(2)}) %collective-permute-start.17) | collective-permute-done | bytes 589856 | tf_op jit(solution)/shard_map/ppermute | solution.py:508
  196.7 12.5 %shard_map.199 = (bf16[2304,256]{1,0:T(8,128)(2,1)}, bf16[1152,256]{1,0:T(8,128)(2,1)}, bf16[2304,256]{1,0:T(8,128)(2,1)}, bf16[2304,256]{1,0:T(8,128)(2,1)}) custom-call(s32[1]{0:T(128)} %bitcast.19.core_ref, bf16[256,2304]{1,0:T(8,128)(2,1)} %copy-done.13, bf16[4608,2304]{1,0:T(8,128)(2,1)} %all-gather.5.cloned.1.call-done.weight_ref), custom_call_target="tpu_custom_call" | custom-call | bytes 67108864 | tf_op jit(solution)/shard_map/pallas_call | solution.py:339
  212.2 13.8 %shard_map.200 = (bf16[2304,256]{1,0:T(8,128)(2,1)}, bf16[1152,256]{1,0:T(8,128)(2,1)}, bf16[2304,256]{1,0:T(8,128)(2,1)}, bf16[2304,256]{1,0:T(8,128)(2,1)}) custom-call(s32[1]{0:T(128)} %bitcast.19.core_ref, bf16[256,2304]{1,0:T(8,128)(2,1)} %copy-done.21, bf16[4608,2304]{1,0:T(8,128)(2,1)} %all-gather.5.cloned.1.call-done.weight_ref), custom_call_target="tpu_custom_call" | custom-call | bytes 67108864 | tf_op jit(solution)/shard_map/pallas_call | solution.py:339
  230.1 20.4 %all-gather.7.cloned.1.call-done.weight_ref = bf16[2304,2304]{1,0:T(8,128)(2,1)} async-done(((bf16[288,2304]{1,0:T(8,128)(2,1)}), bf16[2304,2304]{1,0:T(8,128)(2,1)}) %all-gather.7.cloned.1.call-update) | async-done | bytes 10616848 | tf_op jit(solution)/shard_map/all_gather | solution.py:640
  278.6 14.2 %collective-permute-done.26 = bf16[128,2304]{1,0:T(8,128)(2,1)S(1)} collective-permute-done((bf16[128,2304]{1,0:T(8,128)(2,1)S(1)}, bf16[128,2304]{1,0:T(8,128)(2,1)S(1)}, u32[]{:S(2)}, u32[]{:S(2)}) %collective-permute-start.26) | collective-permute-done | bytes 589856 | tf_op jit(solution)/shard_map/ppermute | solution.py:508
  292.8 10.5 %collective-permute-done.27 = bf16[128,2304]{1,0:T(8,128)(2,1)S(1)} collective-permute-done((bf16[128,2304]{1,0:T(8,128)(2,1)S(1)}, bf16[128,2304]{1,0:T(8,128)(2,1)S(1)}, u32[]{:S(2)}, u32[]{:S(2)}) %collective-permute-start.27) | collective-permute-done | bytes 589856 | tf_op jit(solution)/shard_map/ppermute | solution.py:508
  307.3 25.1 %collective-permute-done.29 = bf16[128,2304]{1,0:T(8,128)(2,1)S(1)} collective-permute-done((bf16[128,2304]{1,0:T(8,128)(2,1)S(1)}, bf16[128,2304]{1,0:T(8,128)(2,1)S(1)}, u32[]{:S(2)}, u32[]{:S(2)}) %collective-permute-start.29) | collective-permute-done | bytes 589856 | tf_op jit(solution)/shard_map/ppermute | solution.py:508
  334.8 8.6 %shard_map.201 = (bf16[4608,256]{1,0:T(8,128)(2,1)}, bf16[2304,256]{1,0:T(8,128)(2,1)}) custom-call(s32[1]{0:T(128)} %bitcast.19.core_ref, bf16[256,2304]{1,0:T(8,128)(2,1)} %copy-done.14, bf16[2304,2304]{1,0:T(8,128)(2,1)} %all-gather.7.cloned.1.call-done.weight_ref, bf16[2304,256]{1,0:T(8,128)(2,1)} %get-tuple-element.170.bent_ref, ...), custom_call_target="tpu_custom_call" | custom-call | bytes 67108864 | tf_op jit(solution)/shard_map/pallas_call | solution.py:384
  349.1 8.8 %shard_map.202 = (bf16[4608,256]{1,0:T(8,128)(2,1)}, bf16[2304,256]{1,0:T(8,128)(2,1)}) custom-call(s32[1]{0:T(128)} %bitcast.19.core_ref, bf16[256,2304]{1,0:T(8,128)(2,1)} %copy-done.22, bf16[2304,2304]{1,0:T(8,128)(2,1)} %all-gather.7.cloned.1.call-done.weight_ref, bf16[2304,256]{1,0:T(8,128)(2,1)} %get-tuple-element.176.bent_ref, ...), custom_call_target="tpu_custom_call" | custom-call | bytes 67108864 | tf_op jit(solution)/shard_map/pallas_call | solution.py:384
  357.9 15.7 %fusion.58 = (bf16[512,2304]{1,0:T(8,128)(2,1)S(1)}, f32[512,2304]{1,0:T(8,128)S(1)}) fusion(bf16[4608,2304]{1,0:T(8,128)(2,1)} %all-gather.5.cloned.1.call-done.weight_ref, bf16[4608,256]{1,0:T(8,128)(2,1)} %get-tuple-element.187.refs_1_, bf16[4608,256]{1,0:T(8,128)(2,1)S(1)} %copy-done.29), kind=kOutput, calls=%fused_computation.208 | convolution fusion | flops 10882252800 | bytes 33030144 | tf_op jit(solution)/shard_map/dot_general | solution.py:25
  378.2 10.4 %shard_map.203 = bf16[1152,2304]{1,0:T(8,128)(2,1)} custom-call(s32[1]{0:T(128)} %bitcast.19.core_ref, bf16[2304,256]{1,0:T(8,128)(2,1)} %get-tuple-element.179.refs_0_, bf16[2304,256]{1,0:T(8,128)(2,1)} %get-tuple-element.180.refs_1_, bf16[1152,256]{1,0:T(8,128)(2,1)} %copy-done.43, bf16[1152,256]{1,0:T(8,128)(2,1)} %copy-done.44, ...), custom_call_target="tpu_custom_call" | custom-call | bytes 67108864 | tf_op jit(solution)/shard_map/pallas_call | solution.py:434
  401.4 16.8 %shard_map.204 = bf16[2304,2304]{1,0:T(8,128)(2,1)} custom-call(s32[1]{0:T(128)} %bitcast.19.core_ref, bf16[4608,256]{1,0:T(8,128)(2,1)} %get-tuple-element.186.refs_0_, bf16[4608,256]{1,0:T(8,128)(2,1)} %get-tuple-element.187.refs_1_, bf16[2304,256]{1,0:T(8,128)(2,1)} %copy-done.41, bf16[2304,256]{1,0:T(8,128)(2,1)} %copy-done.42, ...), custom_call_target="tpu_custom_call" | custom-call | bytes 67108864 | tf_op jit(solution)/shard_map/pallas_call | solution.py:434
  435.3 10.5 %collective-permute-done.41 = bf16[128,2304]{1,0:T(8,128)(2,1)S(1)} collective-permute-done((bf16[128,2304]{1,0:T(8,128)(2,1)S(1)}, bf16[128,2304]{1,0:T(8,128)(2,1)S(1)}, u32[]{:S(2)}, u32[]{:S(2)}) %collective-permute-start.41) | collective-permute-done | bytes 589856 | tf_op jit(solution)/shard_map/ppermute | solution.py:508
  445.8 11.9 %collective-permute-done.40 = bf16[128,2304]{1,0:T(8,128)(2,1)S(1)} collective-permute-done((bf16[128,2304]{1,0:T(8,128)(2,1)S(1)}, bf16[128,2304]{1,0:T(8,128)(2,1)S(1)}, u32[]{:S(2)}, u32[]{:S(2)}) %collective-permute-start.40) | collective-permute-done | bytes 589856 | tf_op jit(solution)/shard_map/ppermute | solution.py:508
  463.2 9.6 %shard_map.205 = (bf16[256,512]{1,0:T(8,128)(2,1)}, f32[2048,512]{1,0:T(8,128)}) custom-call(bf16[512,256]{1,0:T(8,128)(2,1)} %get-tuple-element.143.query_ref.refs_0_, bf16[256,512]{1,0:T(8,128)(2,1)} %convolution_convert_fusion.1.refs_1_, f32[256,512]{1,0:T(8,128)} %get-tuple-element.197.refs_2_, bf16[2048,512]{1,0:T(8,128)(2,1)} %copy-done.2, ...), custom_call_target="tpu_custom_call" | custom-call | bytes 67108864 | tf_op jit(solution)/shard_map/pallas_call | solution.py:230
  474.4 10.4 %shard_map.206 = (bf16[256,512]{1,0:T(8,128)(2,1)}, bf16[2048,512]{1,0:T(8,128)(2,1)}) custom-call(bf16[512,256]{1,0:T(8,128)(2,1)} %get-tuple-element.136.query_ref.refs_0_, bf16[256,512]{1,0:T(8,128)(2,1)} %convolution_convert_fusion.refs_1_, f32[256,512]{1,0:T(8,128)} %get-tuple-element.204.refs_2_, bf16[2048,512]{1,0:T(8,128)(2,1)} %copy-done.2, ...), custom_call_target="tpu_custom_call" | custom-call | bytes 67108864 | tf_op jit(solution)/shard_map/pallas_call | solution.py:230
  489.9 10.3 %collective-permute-done.46 = bf16[256,512]{1,0:T(8,128)(2,1)S(1)} collective-permute-done((bf16[256,512]{1,0:T(8,128)(2,1)S(1)}, bf16[256,512]{1,0:T(8,128)(2,1)S(1)}, u32[]{:S(2)}, u32[]{:S(2)}) %collective-permute-start.46) | collective-permute-done | bytes 262176 | tf_op jit(solution)/shard_map/ppermute | solution.py:552
  510.6 16.3 %collective-permute-done.47 = bf16[512,512]{1,0:T(8,128)(2,1)S(1)} collective-permute-done((bf16[512,512]{1,0:T(8,128)(2,1)S(1)}, bf16[512,512]{1,0:T(8,128)(2,1)S(1)}, u32[]{:S(2)}, u32[]{:S(2)}) %collective-permute-start.47) | collective-permute-done | bytes 524320 | tf_op jit(solution)/shard_map/ppermute | solution.py:552
  544.8 7.5 %shard_map.210 = (bf16[4,128,2304]{2,1,0:T(8,128)(2,1)}, bf16[4,128,2304]{2,1,0:T(8,128)(2,1)}) custom-call(s32[2]{0:T(128)} %pad_add_fusion.3.place_ref, bf16[256,1024]{1,0:T(8,128)(2,1)} %get-tuple-element.218.refs_0_, bf16[256,1024]{1,0:T(8,128)(2,1)} %get-tuple-element.220.refs_1_, bf16[256,2304]{1,0:T(8,128)(2,1)} %get-tuple-element.221.refs_2_, ...), custom_call_target="tpu_custom_call" | custom-call | bytes 67108864 | tf_op jit(solution)/shard_map/pallas_call | solution.py:482
  (427 shorter events, 298.0 us)
Async XLA Ops:
  7.2 55.0 %all-gather.9.cloned.1.call-start = ((), (), s32[]{:S(2)}) async-start(), calls=%async_computation.7 | async-start | bytes 7962624 | tf_op jit(solution)/shard_map/all_gather | solution.py:635
  9.4 187.1 %all-gather.5.cloned.1.call-start = ((), (), s32[]{:S(2)}) async-start(), calls=%async_computation.3 | async-start | bytes 23887872 | tf_op jit(solution)/shard_map/all_gather | solution.py:639
  12.2 238.4 %all-gather.7.cloned.1.call-start = ((), (), s32[]{:S(2)}) async-start(), calls=%async_computation.4 | async-start | bytes 11943936 | tf_op jit(solution)/shard_map/all_gather | solution.py:640
  13.0 580.1 %reduce-scatter.5.cloned.1.call-start = ((), (), s32[]{:S(2)}) async-start(), calls=%async_computation.6 | async-start | bytes 6635520 | tf_op jit(solution)/shard_map/reduce_scatter | solution.py:768
  18.3 26.1 %collective-permute-start = (bf16[128,2304]{1,0:T(8,128)(2,1)S(1)}, bf16[128,2304]{1,0:T(8,128)(2,1)S(1)}, u32[]{:S(2)}, u32[]{:S(2)}) collective-permute-start(bf16[128,2304]{1,0:T(8,128)(2,1)S(1)} %bitcast.121), channel_id=1, source_target_pairs={{0,8},{8,16},{16,24},{24,0},{1,9},{9,17},{17,25},{25,1},{2,10},{10... | collective-permute-start | bytes 1769480 | tf_op jit(solution)/shard_map/ppermute | solution.py:508
  131.9 25.5 %collective-permute-start.15 = (bf16[128,2304]{1,0:T(8,128)(2,1)S(1)}, bf16[128,2304]{1,0:T(8,128)(2,1)S(1)}, u32[]{:S(2)}, u32[]{:S(2)}) collective-permute-start(bf16[128,2304]{1,0:T(8,128)(2,1)S(1)} %add_convert_fusion.5), channel_id=1, source_target_pairs={{0,24},{8,0},{16,8},{24,16},{1,25},{9,1},{17,9},{25,17},{2,26},{10... | collective-permute-start | bytes 1769480 | tf_op jit(solution)/shard_map/ppermute | solution.py:508
  159.6 27.9 %collective-permute-start.17 = (bf16[128,2304]{1,0:T(8,128)(2,1)S(1)}, bf16[128,2304]{1,0:T(8,128)(2,1)S(1)}, u32[]{:S(2)}, u32[]{:S(2)}) collective-permute-start(bf16[128,2304]{1,0:T(8,128)(2,1)S(1)} %multiply_convert_fusion), channel_id=1, source_target_pairs={{0,24},{8,0},{16,8},{24,16},{1,25},{9,1},{17,9},{25,17},{2,26},{10... | collective-permute-start | bytes 1769480 | tf_op jit(solution)/shard_map/ppermute | solution.py:508
  161.3 26.2 %collective-permute-start.16 = (bf16[128,2304]{1,0:T(8,128)(2,1)S(1)}, bf16[128,2304]{1,0:T(8,128)(2,1)}, u32[]{:S(2)}, u32[]{:S(2)}) collective-permute-start(bf16[128,2304]{1,0:T(8,128)(2,1)S(1)} %multiply_convert_fusion), channel_id=1, source_target_pairs={{0,8},{8,16},{16,24},{24,0},{1,9},{9,17},{17,25},{25,1},{2,10},{10... | collective-permute-start | bytes 1769480 | tf_op jit(solution)/shard_map/ppermute | solution.py:508
  195.4 30.9 %collective-permute-start.22 = (bf16[256,2304]{1,0:T(8,128)(2,1)S(1)}, bf16[256,2304]{1,0:T(8,128)(2,1)}, u32[]{:S(2)}, u32[]{:S(2)}) collective-permute-start(bf16[256,2304]{1,0:T(8,128)(2,1)S(1)} %pad_maximum_fusion.4.rows_ref.refs_4_), channel_id=1, source_target_pairs={{0,1},{1,0},{2,3},{3,2},{4,5},{5,4},{6,7},{7,6},{8,9},{9,8},{10,11... | collective-permute-start | bytes 3538952 | tf_op jit(solution)/shard_map/ppermute | solution.py:596
  276.3 27.0 %collective-permute-start.27 = (bf16[128,2304]{1,0:T(8,128)(2,1)S(1)}, bf16[128,2304]{1,0:T(8,128)(2,1)S(1)}, u32[]{:S(2)}, u32[]{:S(2)}) collective-permute-start(bf16[128,2304]{1,0:T(8,128)(2,1)S(1)} %add_convert_fusion.4), channel_id=1, source_target_pairs={{0,24},{8,0},{16,8},{24,16},{1,25},{9,1},{17,9},{25,17},{2,26},{10... | collective-permute-start | bytes 1769480 | tf_op jit(solution)/shard_map/ppermute | solution.py:508
  305.2 27.2 %collective-permute-start.29 = (bf16[128,2304]{1,0:T(8,128)(2,1)S(1)}, bf16[128,2304]{1,0:T(8,128)(2,1)S(1)}, u32[]{:S(2)}, u32[]{:S(2)}) collective-permute-start(bf16[128,2304]{1,0:T(8,128)(2,1)S(1)} %get-tuple-element.293), channel_id=1, source_target_pairs={{0,24},{8,0},{16,8},{24,16},{1,25},{9,1},{17,9},{25,17},{2,26},{10... | collective-permute-start | bytes 1769480 | tf_op jit(solution)/shard_map/ppermute | solution.py:508
  307.3 25.2 %collective-permute-start.28 = (bf16[128,2304]{1,0:T(8,128)(2,1)S(1)}, bf16[128,2304]{1,0:T(8,128)(2,1)S(1)}, u32[]{:S(2)}, u32[]{:S(2)}) collective-permute-start(bf16[128,2304]{1,0:T(8,128)(2,1)S(1)} %get-tuple-element.293), channel_id=1, source_target_pairs={{0,8},{8,16},{16,24},{24,0},{1,9},{9,17},{17,25},{25,1},{2,10},{10... | collective-permute-start | bytes 1769480 | tf_op jit(solution)/shard_map/ppermute | solution.py:508
  334.8 43.4 %collective-permute-start.34 = (bf16[256,2304]{1,0:T(8,128)(2,1)S(1)}, bf16[256,2304]{1,0:T(8,128)(2,1)}, u32[]{:S(2)}, u32[]{:S(2)}) collective-permute-start(bf16[256,2304]{1,0:T(8,128)(2,1)S(1)} %pad_maximum_fusion.5.rows_ref.refs_4_), channel_id=1, source_target_pairs={{0,1},{1,0},{2,3},{3,2},{4,5},{5,4},{6,7},{7,6},{8,9},{9,8},{10,11... | collective-permute-start | bytes 3538952 | tf_op jit(solution)/shard_map/ppermute | solution.py:596
  348.1 30.1 %collective-permute-start.35 = (bf16[256,2304]{1,0:T(8,128)(2,1)S(1)}, bf16[256,2304]{1,0:T(8,128)(2,1)}, u32[]{:S(2)}, u32[]{:S(2)}) collective-permute-start(bf16[256,2304]{1,0:T(8,128)(2,1)S(1)} %constant_dynamic-update-slice_fusion.16.rows_ref.refs_5_), channel_id=1, source_target_pairs={{0,1},{1,0},{2,3},{3,2},{4,5},{5,4},{6,7},{7,6},{8,9},{9,8},{10,11... | collective-permute-start | bytes 3538952 | tf_op jit(solution)/shard_map/ppermute | solution.py:596
  390.5 205.6 %reduce-scatter.3.cloned.1.call-start = ((), (), s32[]{:S(2)}) async-start(), calls=%async_computation.5 | async-start | bytes 13271040 | tf_op jit(solution)/shard_map/reduce_scatter | solution.py:769
  395.5 22.7 %collective-permute-start.36 = (bf16[128,2304]{1,0:T(8,128)(2,1)}, bf16[128,2304]{1,0:T(8,128)(2,1)}, u32[]{:S(2)}, u32[]{:S(2)}) collective-permute-start(bf16[128,2304]{1,0:T(8,128)(2,1)} %fusion.33), channel_id=1, source_target_pairs={{0,8},{8,16},{16,24},{24,0},{1,9},{9,17},{17,25},{25,1},{2,10},{10... | collective-permute-start | bytes 1769480 | tf_op jit(solution)/shard_map/ppermute | solution.py:508
  397.0 28.0 %collective-permute-start.37 = (bf16[128,2304]{1,0:T(8,128)(2,1)}, bf16[128,2304]{1,0:T(8,128)(2,1)}, u32[]{:S(2)}, u32[]{:S(2)}) collective-permute-start(bf16[128,2304]{1,0:T(8,128)(2,1)} %add_convert_fusion.2), channel_id=1, source_target_pairs={{0,24},{8,0},{16,8},{24,16},{1,25},{9,1},{17,9},{25,17},{2,26},{10... | collective-permute-start | bytes 1769480 | tf_op jit(solution)/shard_map/ppermute | solution.py:508
  432.0 25.7 %collective-permute-start.40 = (bf16[128,2304]{1,0:T(8,128)(2,1)S(1)}, bf16[128,2304]{1,0:T(8,128)(2,1)S(1)}, u32[]{:S(2)}, u32[]{:S(2)}) collective-permute-start(bf16[128,2304]{1,0:T(8,128)(2,1)S(1)} %subtract_convert_fusion), channel_id=1, source_target_pairs={{0,8},{8,16},{16,24},{24,0},{1,9},{9,17},{17,25},{25,1},{2,10},{10... | collective-permute-start | bytes 1769480 | tf_op jit(solution)/shard_map/ppermute | solution.py:508
  501.8 25.2 %collective-permute-start.47 = (bf16[512,512]{1,0:T(8,128)(2,1)S(1)}, bf16[512,512]{1,0:T(8,128)(2,1)S(1)}, u32[]{:S(2)}, u32[]{:S(2)}) collective-permute-start(bf16[512,512]{1,0:T(8,128)(2,1)S(1)} %get-tuple-element.283), channel_id=1, source_target_pairs={{0,4},{2,6},{4,0},{6,2},{1,5},{3,7},{5,1},{7,3},{8,12},{10,14},{12... | collective-permute-start | bytes 1572872 | tf_op jit(solution)/shard_map/ppermute | solution.py:552
  502.4 25.0 %collective-permute-start.45 = (bf16[512,512]{1,0:T(8,128)(2,1)S(1)}, bf16[512,512]{1,0:T(8,128)(2,1)S(1)}, u32[]{:S(2)}, u32[]{:S(2)}) collective-permute-start(bf16[512,512]{1,0:T(8,128)(2,1)S(1)} %get-tuple-element.284), channel_id=1, source_target_pairs={{0,2},{2,0},{4,6},{6,4},{1,3},{3,1},{5,7},{7,5},{8,10},{10,8},{12,... | collective-permute-start | bytes 1572872 | tf_op jit(solution)/shard_map/ppermute | solution.py:552
  555.6 30.8 %collective-permute-start.50 = (bf16[128,2304]{1,0:T(8,128)(2,1)}, bf16[128,2304]{1,0:T(8,128)(2,1)}, u32[]{:S(2)}, u32[]{:S(2)}) collective-permute-start(bf16[128,2304]{1,0:T(8,128)(2,1)} %add_convert_fusion.1), channel_id=1, source_target_pairs={{0,8},{8,16},{16,24},{24,0},{1,9},{9,17},{17,25},{25,1},{2,10},{10... | collective-permute-start | bytes 1769480 | tf_op jit(solution)/shard_map/ppermute | solution.py:508
  556.1 30.2 %collective-permute-start.51 = (bf16[128,2304]{1,0:T(8,128)(2,1)}, bf16[128,2304]{1,0:T(8,128)(2,1)}, u32[]{:S(2)}, u32[]{:S(2)}) collective-permute-start(bf16[128,2304]{1,0:T(8,128)(2,1)} %add_convert_fusion), channel_id=1, source_target_pairs={{0,24},{8,0},{16,8},{24,16},{1,25},{9,1},{17,9},{25,17},{2,26},{10... | collective-permute-start | bytes 1769480 | tf_op jit(solution)/shard_map/ppermute | solution.py:508
  586.3 21.4 %collective-permute-start.56 = (bf16[192,2304]{1,0:T(8,128)(2,1)}, bf16[192,2304]{1,0:T(8,128)(2,1)S(1)}, u32[]{:S(2)}, u32[]{:S(2)}) collective-permute-start(bf16[192,2304]{1,0:T(8,128)(2,1)} %get-tuple-element.242), channel_id=1, source_target_pairs={{0,2},{2,0},{4,6},{6,4},{1,3},{3,1},{5,7},{7,5},{8,10},{10,8},{12,... | collective-permute-start | bytes 2654216 | tf_op jit(solution)/shard_map/ppermute | solution.py:552
  587.5 21.2 %collective-permute-start.57 = (bf16[192,2304]{1,0:T(8,128)(2,1)}, bf16[192,2304]{1,0:T(8,128)(2,1)S(1)}, u32[]{:S(2)}, u32[]{:S(2)}) collective-permute-start(bf16[192,2304]{1,0:T(8,128)(2,1)} %get-tuple-element.243), channel_id=1, source_target_pairs={{0,4},{2,6},{4,0},{6,2},{1,5},{3,7},{5,1},{7,3},{8,12},{10,14},{12... | collective-permute-start | bytes 2654216 | tf_op jit(solution)/shard_map/ppermute | solution.py:552
  (110 other events, 1164.2 us)
Sparse Core Ops, SparseCore 0:
  10.5 51.6 all-gather.8
  64.6 120.1 all-gather.4
  186.7 63.8 all-gather.6
  390.6 60.3 reduce-scatter.4
  454.0 121.8 reduce-scatter.2
